TPU v7x, 128 devices: a whole 4x4x4 slice. The times are simulated.
128 devices in a mesh: dp: 16 (over z, x_hi, core), mp: 8 (over y, x_lo).
Axes of the slice: x: 4 (x_hi: 2, x_lo: 2; x = x_hi * 2 + x_lo), y: 4, z: 4, core: 2. Of those that a mesh axis runs over, the one named last changes fastest.
Arguments:
- tokens: bfloat16 [12288, 2048], P('dp'), may hold values from -20 to 20
- cotangent: bfloat16 [12288, 2048], P('dp'), may hold values from -6 to 6
- w_gate: bfloat16 [2048, 8192], P(None, 'mp'), may hold values from -1 to 1
- w_up: bfloat16 [2048, 8192], P(None, 'mp'), may hold values from -1 to 1
- w_down: bfloat16 [8192, 2048], P('mp'), may hold values from -0.0625 to 0.0625
- row_gate: float32 [2048], P('dp'), may hold values from 0.0003 to 20
- col_gate: float32 [8192], P('mp'), may hold values from 0.0003 to 10
- row_up: float32 [2048], P('dp'), may hold values from 0.0003 to 20
- col_up: float32 [8192], P('mp'), may hold values from 0.0003 to 10
- row_down: float32 [8192], P(('mp', 'dp')), may hold values from 0.01 to 300
- col_down: float32 [2048], replicated, may hold values from 0.01 to 300
Outputs:
- token_grad: bfloat16 [12288, 2048], P('dp', 'mp')
- update_gate: float32 [2048, 8192], P('dp', 'mp')
- update_up: float32 [2048, 8192], P('dp', 'mp')
- update_down: float32 [8192, 2048], P(('mp', 'dp'))
- row_gate_new: float32 [2048], P('dp')
- col_gate_new: float32 [8192], P('mp')
- row_up_new: float32 [2048], P('dp')
- col_up_new: float32 [8192], P('mp')
- row_down_new: float32 [8192], P(('mp', 'dp'))
- col_down_new: float32 [2048], replicated
All inputs are finite; a program needn't handle non-finite values.
Results may differ from a plain program's by a relative error of at most 0.015.
Values may be sent and summed in bfloat16 or wider, within the bound.
No kernel may reach another device: no remote copies, remote signals or barrier semaphores. Data moves between devices by JAX's collectives and lax.ppermute only.
A program may use at most 128 MiB of HBM per device.

v0:
```python
import jax
import jax.numpy as jnp
from jax import lax
from jax.sharding import PartitionSpec as P

epsilon_one = 1e-30
decay_rate = 0.8


def silu_parts(gate_pre):
    sig = jax.nn.sigmoid(gate_pre)
    return (gate_pre * sig, sig * (1.0 + gate_pre * (1.0 - sig)))


def moment_step(old_value, column_total, count):
    return decay_rate * old_value + (1.0 - decay_rate) * (column_total / count + epsilon_one)


def body(
    tokens, cotangent, w_gate, w_up, w_down, row_gate, col_gate, row_up, col_up, row_down, col_down
):
    data_count = lax.axis_size("dp")
    model_count = lax.axis_size("mp")
    tok_rows, width_model = tokens.shape
    units = w_gate.shape[1]
    all_units = units * model_count
    grad_scale = float(tok_rows * data_count) ** (-0.5)
    gate_pre = jnp.dot(tokens, w_gate, preferred_element_type=jnp.float32)
    up_pre = jnp.dot(tokens, w_up, preferred_element_type=jnp.float32)
    activated, derivative = silu_parts(gate_pre)
    hidden = (activated * up_pre).astype(jnp.bfloat16)
    hidden_grad = jnp.einsum("td,fd->tf", cotangent, w_down, preferred_element_type=jnp.float32)
    grad_gate = (hidden_grad * up_pre * derivative).astype(jnp.bfloat16)
    grad_up = (hidden_grad * activated).astype(jnp.bfloat16)

    def weight_term(left_side, right_side):
        return (
            jnp.einsum("tr,tc->rc", left_side, right_side, preferred_element_type=jnp.float32)
            * grad_scale
        )

    g_gate, g_up, g_down = (
        lax.psum_scatter(
            weight_term(tokens, grad_gate).astype(jnp.bfloat16),
            "dp",
            scatter_dimension=0,
            tiled=True,
        ).astype(jnp.float32),
        lax.psum_scatter(
            weight_term(tokens, grad_up).astype(jnp.bfloat16), "dp", scatter_dimension=0, tiled=True
        ).astype(jnp.float32),
        lax.psum_scatter(
            weight_term(hidden, cotangent).astype(jnp.bfloat16),
            "dp",
            scatter_dimension=0,
            tiled=True,
        ).astype(jnp.float32),
    )
    input_terms = jnp.einsum("tf,df->td", grad_gate, w_gate, preferred_element_type=jnp.float32)
    input_terms = input_terms + jnp.einsum(
        "tf,df->td", grad_up, w_up, preferred_element_type=jnp.float32
    )
    token_grad = lax.psum_scatter(
        input_terms.astype(jnp.bfloat16), "mp", scatter_dimension=1, tiled=True
    )
    squares_gate = g_gate * g_gate
    squares_up = g_up * g_up
    squares_down = g_down * g_down
    row_totals = lax.psum((jnp.sum(squares_gate, 1), jnp.sum(squares_up, 1)), "mp")
    col_totals = lax.psum((jnp.sum(squares_gate, 0), jnp.sum(squares_up, 0)), "dp")
    row_gate_new = moment_step(row_gate, row_totals[0], all_units)
    row_up_new = moment_step(row_up, row_totals[1], all_units)
    col_gate_new = moment_step(col_gate, col_totals[0], width_model)
    col_up_new = moment_step(col_up, col_totals[1], width_model)
    row_down_new = moment_step(row_down, jnp.sum(squares_down, 1), width_model)
    row_counts = jnp.array([width_model, width_model, all_units], jnp.float32)
    down_total = lax.psum(jnp.sum(squares_down, 0), ("dp", "mp"))
    new_sums = jnp.stack(
        [
            jnp.sum(row_gate_new) / model_count,
            jnp.sum(row_up_new) / model_count,
            jnp.sum(row_down_new),
        ]
    )
    row_means = lax.psum(new_sums, ("dp", "mp")) / row_counts
    col_down_new = moment_step(col_down, down_total, all_units)
    raw_gate = g_gate / jnp.sqrt(row_gate_new[:, None] * col_gate_new[None, :] / row_means[0])
    raw_up = g_up / jnp.sqrt(row_up_new[:, None] * col_up_new[None, :] / row_means[1])
    raw_down = g_down / jnp.sqrt(row_down_new[:, None] * col_down_new[None, :] / row_means[2])
    raw_totals = lax.psum(
        jnp.stack(
            [jnp.sum(raw_gate * raw_gate), jnp.sum(raw_up * raw_up), jnp.sum(raw_down * raw_down)]
        ),
        ("dp", "mp"),
    )
    divisor = jnp.maximum(1.0, jnp.sqrt(raw_totals / float(width_model * all_units)))
    update_gate = raw_gate / divisor[0]
    update_up = raw_up / divisor[1]
    update_down = raw_down / divisor[2]
    return (
        token_grad,
        update_gate,
        update_up,
        update_down,
        row_gate_new,
        col_gate_new,
        row_up_new,
        col_up_new,
        row_down_new,
        col_down_new,
    )


def solution(mesh):
    in_specs = (
        P("dp", None),
        P("dp", None),
        P(None, "mp"),
        P(None, "mp"),
        P("mp", None),
        P("dp"),
        P("mp"),
        P("dp"),
        P("mp"),
        P(("mp", "dp")),
        P(),
    )
    out_specs = (
        P("dp", "mp"),
        P("dp", "mp"),
        P("dp", "mp"),
        P(("mp", "dp"), None),
        P("dp"),
        P("mp"),
        P("dp"),
        P("mp"),
        P(("mp", "dp")),
        P(),
    )
    return jax.shard_map(body, mesh=mesh, in_specs=in_specs, out_specs=out_specs, check_vma=False)
```

profile of v0, /device:TPU:0, one launch (start us, length us, event | category | flops | bytes accessed | tf_op | source)
XLA Modules:
  0.0 483.1 jit_solution(1240444555862126705)
XLA Ops:
  7.2 0.0 copy-start
  7.2 0.0 reduce-scatter.15.cloned.1.call-start
  7.2 1.8 copy-done
  9.1 5.3 %fusion.17 = f32[768,1024]{1,0:T(8,128)S(1)} fusion(bf16[768,2048]{1,0:T(8,128)(2,1)S(1)} %copy-done, bf16[2048,1024]{1,0:T(8,128)(2,1)} %param.14), kind=kOutput, calls=%fused_computation.45 | convolution fusion | flops 3221225472 | bytes 10485760 | tf_op jit(solution)/shard_map/dot_general | solution.py:28
  14.5 3.5 fusion.16
  17.9 0.8 copy-done.16
  18.7 5.6 %multiply_convert_fusion.4 = (bf16[768,1024]{1,0:T(8,128)(2,1)S(1)}, bf16[768,1024]{1,0:T(8,128)(2,1)}) fusion(f32[768,1024]{1,0:T(8,128)S(1)} %fusion.17, f32[768,1024]{1,0:T(8,128)S(1)} %fusion.16, bf16[768,2048]{1,0:T(8,128)(2,1)S(1)} %copy-done.16, bf16[1024,2048]{1,0:T(8,128)(2,1)S(1)} %copy-done.13), kind=kOutput, calls=%fused_computation.7 | convolution fusion | flops 3231449088 | bytes 16777216 | tf_op jit(solution)/shard_map/td,fd->tf/dot_general | solution.py:32
  24.3 1.2 copy-done.20
  25.5 5.1 %fusion.1 = bf16[2048,1024]{0,1:T(8,128)(2,1)} fusion(bf16[768,1024]{1,0:T(8,128)(2,1)S(1)} %get-tuple-element.48, bf16[768,2048]{1,0:T(8,128)(2,1)S(1)} %copy-done), kind=kOutput, calls=%fused_computation.5 | convolution fusion | flops 3225419776 | bytes 8912896 | tf_op jit(solution)/shard_map/tr,tc->rc/dot_general | solution.py:38
  30.6 6.4 %copy.28 = bf16[2048,1024]{1,0:T(8,128)(2,1)} copy(bf16[2048,1024]{0,1:T(8,128)(2,1)} %fusion.1) | data formatting | bytes 8388608
  37.0 0.0 reduce-scatter.15.cloned.1.call-update
  37.0 0.0 reduce-scatter.13.cloned.1.call-start
  37.0 6.5 %fusion = bf16[2048,1024]{0,1:T(8,128)(2,1)} fusion(bf16[768,1024]{1,0:T(8,128)(2,1)} %get-tuple-element.49, bf16[768,2048]{1,0:T(8,128)(2,1)S(1)} %copy-done), kind=kOutput, calls=%fused_computation.4 | convolution fusion | flops 3225419776 | bytes 8912896 | tf_op jit(solution)/shard_map/tr,tc->rc/dot_general | solution.py:38
  43.5 6.4 %copy.26 = bf16[2048,1024]{1,0:T(8,128)(2,1)} copy(bf16[2048,1024]{0,1:T(8,128)(2,1)} %fusion) | data formatting | bytes 8388608
  49.9 0.0 reduce-scatter.13.cloned.1.call-update
  49.9 0.2 reduce-scatter.11.cloned.1.call-start
  50.2 9.7 %multiply_convert_fusion = bf16[1024,2048]{1,0:T(8,128)(2,1)} fusion(bf16[768,2048]{1,0:T(8,128)(2,1)} %param.13, f32[768,1024]{1,0:T(8,128)} %copy-done.19, f32[768,1024]{1,0:T(8,128)} %copy-done.18), kind=kOutput, calls=%fused_computation | convolution fusion | flops 3230138368 | bytes 13631488 | tf_op jit(solution)/shard_map/tr,tc->rc/dot_general | solution.py:38
  59.9 0.0 reduce-scatter.11.cloned.1.call-update
  59.9 0.0 reduce-scatter.9.cloned.1.call-start
  60.0 6.1 %fusion.18 = f32[768,2048]{1,0:T(8,128)S(1)} fusion(bf16[768,1024]{1,0:T(8,128)(2,1)} %get-tuple-element.49, bf16[2048,1024]{1,0:T(8,128)(2,1)} %param.14), kind=kOutput, calls=%fused_computation.46 | convolution fusion | flops 3221225472 | bytes 12058624 | tf_op jit(solution)/shard_map/tf,df->td/dot_general | solution.py:59
  66.1 4.9 %add_convert_fusion = bf16[768,2048]{1,0:T(8,128)(2,1)} fusion(f32[768,2048]{1,0:T(8,128)S(1)} %fusion.18, bf16[768,1024]{1,0:T(8,128)(2,1)S(1)} %copy-done.21, bf16[2048,1024]{1,0:T(8,128)(2,1)S(1)} %copy-done.15), kind=kOutput, calls=%fused_computation.3 | convolution fusion | flops 3224371200 | bytes 15204352 | tf_op jit(solution)/shard_map/tf,df->td/dot_general | solution.py:60
  71.0 0.0 reduce-scatter.9.cloned.1.call-update
  71.0 49.3 %reduce-scatter.15.cloned.1.call-done = bf16[128,1024]{1,0:T(8,128)(2,1)} async-done(((bf16[2048,1024]{1,0:T(8,128)(2,1)}), bf16[128,1024]{1,0:T(8,128)(2,1)}) %reduce-scatter.15.cloned.1.call-update) | async-done | bytes 262160
  120.3 1.1 copy.29
  121.4 82.9 %reduce-scatter.13.cloned.1.call-done = bf16[128,1024]{1,0:T(8,128)(2,1)} async-done(((bf16[2048,1024]{1,0:T(8,128)(2,1)}), bf16[128,1024]{1,0:T(8,128)(2,1)}) %reduce-scatter.13.cloned.1.call-update) | async-done | bytes 262160
  204.3 1.8 copy.27
  206.1 0.2 fusion.5
  206.3 1.2 fusion.3
  207.5 18.8 %all-reduce.2 = (f32[128]{0:T(128)S(1)}, f32[128]{0:T(128)S(1)}) all-reduce(f32[128]{0:T(128)S(1)} %get-tuple-element.33, f32[128]{0:T(128)S(1)} %get-tuple-element.31), channel_id=1, replica_groups=mesh['dp'=16,'mp'=8] {'mp'}, use_global_device_ids=true, to_apply=%region_9.0 | all-reduce | flops 256 | bytes 2048 | tf_op jit(solution)/shard_map/psum | solution.py:69
  226.2 0.6 fusion.11
  228.2 59.6 %reduce-scatter.11.cloned.1.call-done = bf16[64,2048]{1,0:T(8,128)(2,1)} async-done(((bf16[1024,2048]{1,0:T(8,128)(2,1)}), bf16[64,2048]{1,0:T(8,128)(2,1)}) %reduce-scatter.11.cloned.1.call-update) | async-done | bytes 262160 | tf_op jit(solution)/shard_map/reduce_scatter | solution.py:52
  287.8 1.1 fusion.7
  289.0 0.6 fusion.13
  289.6 0.7 pad_maximum_fusion
  290.3 66.9 %all-reduce = (f32[3]{0:T(128)S(1)}, f32[2048]{0:T(1024)S(1)}) all-reduce(f32[3]{0:T(128)S(1)} %pad_maximum_fusion, f32[2048]{0:T(1024)S(1)} %get-tuple-element.34), channel_id=1, replica_groups=mesh['dp'=16,'mp'=8] {'dp','mp'}, use_global_device_ids=true, to_apply=%region_14.0 | all-reduce | flops 2051 | bytes 16408 | tf_op jit(solution)/shard_map/psum | solution.py:85
  357.2 34.8 %all-reduce.1 = (f32[1024]{0:T(1024)S(1)}, f32[1024]{0:T(1024)S(1)}) all-reduce(f32[1024]{0:T(1024)S(1)} %get-tuple-element.32, f32[1024]{0:T(1024)S(1)} %get-tuple-element.30), channel_id=1, replica_groups=mesh['dp'=16,'mp'=8] {'dp'}, use_global_device_ids=true, to_apply=%region_17.0 | all-reduce | flops 2048 | bytes 16384 | tf_op jit(solution)/shard_map/psum | solution.py:70
  392.0 0.7 fusion.15
  392.7 1.5 multiply_reduce_fusion.1
  394.2 2.4 multiply_reduce_fusion.2
  396.6 2.5 multiply_reduce_fusion
  399.1 2.0 pad_maximum_fusion.1
  401.1 62.1 %psum.55 = f32[3]{0:T(128)S(1)} all-reduce(f32[3]{0:T(128)S(1)} %pad_maximum_fusion.1), channel_id=1, replica_groups=mesh['dp'=16,'mp'=8] {'dp','mp'}, use_global_device_ids=true, to_apply=%region_22.0 | all-reduce | flops 3 | bytes 24 | tf_op jit(solution)/shard_map/psum | solution.py:90
  463.1 0.7 fusion.14
  463.8 2.3 broadcast_divide_fusion.1
  466.1 2.0 copy.25
  468.1 3.1 broadcast_divide_fusion.2
  471.2 2.0 copy.24
  473.3 3.2 broadcast_divide_fusion
  (45 shorter events, 0.1 us)
Async XLA Ops:
  7.2 1.9 copy-start
  7.2 113.1 %reduce-scatter.15.cloned.1.call-start = ((), (), s32[]{:S(2)}) async-start(), calls=%async_computation.7 | async-start | bytes 4456448
  9.1 5.4 %copy-start.14 = (bf16[2048,1024]{1,0:T(8,128)(2,1)S(1)}, bf16[2048,1024]{1,0:T(8,128)(2,1)}, u32[]{:S(2)}) copy-start(bf16[2048,1024]{1,0:T(8,128)(2,1)} %param.15) | copy-start | bytes 12582916
  14.4 3.5 copy-start.18
  14.4 3.5 copy-start.13
  14.5 4.3 copy-start.16
  18.7 5.6 %copy-start.19 = (f32[768,1024]{1,0:T(8,128)}, f32[768,1024]{1,0:T(8,128)S(1)}, u32[]{:S(2)}) copy-start(f32[768,1024]{1,0:T(8,128)S(1)} %fusion.16) | copy-start | bytes 9437188
  24.3 1.2 copy-start.20
  37.0 167.3 %reduce-scatter.13.cloned.1.call-start = ((), (), s32[]{:S(2)}) async-start(), calls=%async_computation.6 | async-start | bytes 4456448
  49.9 237.9 %reduce-scatter.11.cloned.1.call-start = ((), (), s32[]{:S(2)}) async-start(), calls=%async_computation.5 | async-start | bytes 4456448 | tf_op jit(solution)/shard_map/reduce_scatter | solution.py:52
  59.9 416.6 %reduce-scatter.9.cloned.1.call-start = ((), (), s32[]{:S(2)}) async-start(), calls=%async_computation.4 | async-start | bytes 3538944 | tf_op jit(solution)/shard_map/reduce_scatter | solution.py:63
  60.0 6.1 %copy-start.15 = (bf16[2048,1024]{1,0:T(8,128)(2,1)S(1)}, bf16[2048,1024]{1,0:T(8,128)(2,1)}, u32[]{:S(2)}) copy-start(bf16[2048,1024]{1,0:T(8,128)(2,1)} %param.15) | copy-start | bytes 12582916
  60.0 6.1 %copy-start.21 = (bf16[768,1024]{1,0:T(8,128)(2,1)S(1)}, bf16[768,1024]{1,0:T(8,128)(2,1)}, u32[]{:S(2)}) copy-start(bf16[768,1024]{1,0:T(8,128)(2,1)} %copy-done.20) | copy-start | bytes 4718596
  71.0 155.3 %copy-start.11 = (f32[128]{0:T(128)S(1)}, f32[128]{0:T(128)}, u32[]{:S(2)}) copy-start(f32[128]{0:T(128)} %param.17) | copy-start | bytes 1540
  71.0 155.3 %copy-start.12 = (f32[128]{0:T(128)S(1)}, f32[128]{0:T(128)}, u32[]{:S(2)}) copy-start(f32[128]{0:T(128)} %param.19) | copy-start | bytes 1540
  71.0 218.0 %copy-start.10 = (f32[64]{0:T(128)S(1)}, f32[64]{0:T(128)}, u32[]{:S(2)}) copy-start(f32[64]{0:T(128)} %param.21) | copy-start | bytes 772
  71.0 286.3 %copy-start.17 = (f32[3]{0:T(128)S(1)}, f32[3]{0:T(128)}, u32[]{:S(2)}) copy-start(f32[3]{0:T(128)} %constant.22) | copy-start | bytes 40
  71.0 321.7 %copy-start.8 = (f32[1024]{0:T(1024)S(1)}, f32[1024]{0:T(1024)}, u32[]{:S(2)}) copy-start(f32[1024]{0:T(1024)} %param.20) | copy-start | bytes 12292
  71.0 321.7 %copy-start.9 = (f32[1024]{0:T(1024)S(1)}, f32[1024]{0:T(1024)}, u32[]{:S(2)}) copy-start(f32[1024]{0:T(1024)} %param.18) | copy-start | bytes 12292
  71.0 325.6 %copy-start.4 = (f32[2048]{0:T(1024)S(1)}, f32[2048]{0:T(1024)}, u32[]{:S(2)}) copy-start(f32[2048]{0:T(1024)} %param.22) | copy-start | bytes 24580
  226.9 249.7 %copy-start.6 = (f32[128]{0:T(128)}, f32[128]{0:T(128)S(1)}, u32[]{:S(2)}) copy-start(f32[128]{0:T(128)S(1)} %get-tuple-element.43) | copy-start | bytes 1540
  226.9 249.7 %copy-start.7 = (f32[128]{0:T(128)}, f32[128]{0:T(128)S(1)}, u32[]{:S(2)}) copy-start(f32[128]{0:T(128)S(1)} %get-tuple-element.57) | copy-start | bytes 1540
  289.6 187.0 %copy-start.5 = (f32[64]{0:T(128)}, f32[64]{0:T(128)S(1)}, u32[]{:S(2)}) copy-start(f32[64]{0:T(128)S(1)} %get-tuple-element.47) | copy-start | bytes 772
  392.7 83.8 %copy-start.2 = (f32[1024]{0:T(1024)}, f32[1024]{0:T(1024)S(1)}, u32[]{:S(2)}) copy-start(f32[1024]{0:T(1024)S(1)} %get-tuple-element.58) | copy-start | bytes 12292
  392.7 83.8 %copy-start.3 = (f32[1024]{0:T(1024)}, f32[1024]{0:T(1024)S(1)}, u32[]{:S(2)}) copy-start(f32[1024]{0:T(1024)S(1)} %get-tuple-element.59) | copy-start | bytes 12292
  396.6 79.9 %copy-start.1 = (f32[2048]{0:T(1024)}, f32[2048]{0:T(1024)S(1)}, u32[]{:S(2)}) copy-start(f32[2048]{0:T(1024)S(1)} %multiply_add_fusion) | copy-start | bytes 24580
Sparse Core Ops, SparseCore 0:
  37.1 83.1 reduce-scatter.14
  124.8 79.4 reduce-scatter.12
  208.3 79.4 reduce-scatter.10
  290.8 71.7 reduce-scatter.8
where the time goes:
time: 485 us; the launch traced here: 483 us
  waiting for transfers between devices  192 us (40%)
  blocking collectives  183 us (38%)
  matrix products  46.6 us (10%)
  local copies, waits for them, and re-layouts  25 us (5%)
  other arithmetic  21.4 us (4%)
  between operations  15.3 us (3%)
    unnamed x6, waiting for transfers between devices  132 us
    psum x1, blocking collectives, body(): row_means = lax.psum(new_sums, ('dp', 'mp')) / row_counts  66.9 us
    psum x1, blocking collectives, body(): lax.psum(jnp.stack([jnp.sum(raw_gate * raw_gate), jnp.sum(raw_up * raw_up...  62.1 us
    reduce_scatter x1, waiting for transfers between devices, body(): lax.psum_scatter(weight_term(hidden, cotangent).astype(jnp.bfloat16), 'dp...  59.6 us
    psum x1, blocking collectives, body(): lax.psum((jnp.sum(squares_gate, 0), jnp.sum(squares_up, 0)), 'dp')  34.8 us
    unnamed x50, local copies, waits for them, and re-layouts  23.7 us
    dot_general x3, matrix products, weight_term(): jnp.einsum('tr,tc->rc', left_side, right_side, preferred_element_type=jnp...  21.3 us
    psum x1, blocking collectives, body(): lax.psum((jnp.sum(squares_gate, 1), jnp.sum(squares_up, 1)), 'mp')  18.8 us
  transfers between devices with their start and end apart: 4, of which 3 were waited for; matrix products, arithmetic and copies ran while one was open for 13% of the time, Pallas kernels for 0%

commit v1 on v0

v1 whole, which is shorter than its diff:
```python
import functools

import jax
import jax.numpy as jnp
from jax import lax
from jax.experimental import pallas as pl
from jax.experimental.pallas import tpu as pltpu
from jax.sharding import PartitionSpec as P

epsilon_one = 1e-30
decay_rate = 0.8
BF = jnp.bfloat16
F32 = jnp.float32
MIB = 1024 * 1024
EARLY = 16
FIRST = (((2, 0), (2, 1)), ((1, 1), (3, 0)))
SECOND = (((1, 0), (3, 1)), ((0, 0), (0, 1)))


def dp_shift(dz=0, dx=0, dc=0):
    pairs = []
    for z in range(4):
        for x in range(2):
            for c in range(2):
                to = ((z + dz) % 4) * 4 + (x ^ dx) * 2 + (c ^ dc)
                pairs.append((z * 4 + x * 2 + c, to))
    return pairs


def mp_shift(dy=0, dx=0):
    return [(y * 2 + x, ((y + dy) % 4) * 2 + (x ^ dx)) for y in range(4) for x in range(2)]


def contract(a, b, dim_a, dim_b):
    return lax.dot_general(a, b, (((dim_a,), (dim_b,)), ((), ())), preferred_element_type=F32)


def local_kernel(name, kernel, scalars, arrays, outs, flops, after=(), limit=6):
    vmem = pl.BlockSpec(memory_space=pltpu.VMEM)
    count, late = len(arrays), len(after)

    def run(*refs):
        first = 0 if scalars is None else 1
        kernel(*refs[: first + count], *refs[first + count + late :])

    specs = [] if scalars is None else [pl.BlockSpec(memory_space=pltpu.SMEM)]
    operands = [] if scalars is None else [scalars]
    return pl.pallas_call(
        run,
        in_specs=specs + [vmem] * count + [pl.BlockSpec(memory_space=pl.ANY)] * late,
        out_specs=[vmem] * len(outs),
        out_shape=outs,
        compiler_params=pltpu.CompilerParams(vmem_limit_bytes=limit * MIB),
        cost_estimate=pl.CostEstimate(flops=flops // EARLY, bytes_accessed=1024, transcendentals=0),
        name=name,
    )(
        *operands,
        *[pltpu.with_memory_space_constraint(a, pltpu.VMEM) for a in arrays],
        *after,
    )


def near(shape, dtype):
    return pltpu.VMEM(shape, dtype)


def gate_kernel(tok_in, wg_in, gate, tok, wg, tok_sem, wg_sem):
    rows = [pl.ds(m * 256, 256) for m in range(3)]
    cols = [pl.ds(n * 256, 256) for n in range(4)]
    tok_copy = [pltpu.make_async_copy(tok_in.at[r, :], tok.at[r, :], tok_sem.at[m])
                for m, r in enumerate(rows)]
    wg_copy = [pltpu.make_async_copy(wg_in.at[:, c], wg.at[:, c], wg_sem.at[n])
               for n, c in enumerate(cols)]
    for copy in (tok_copy[0], wg_copy[0], tok_copy[1], tok_copy[2], *wg_copy[1:]):
        copy.start()
    for n, c in enumerate(cols):
        wg_copy[n].wait()
        for m, r in enumerate(rows):
            if n == 0:
                tok_copy[m].wait()
            gate[r, c] = contract(tok[r, :], wg[:, c], 1, 0)


def gate_pre(tokens, w_gate):
    vmem, hbm = pl.BlockSpec(memory_space=pltpu.VMEM), pl.BlockSpec(memory_space=pltpu.HBM)
    rows, width = tokens.shape
    units = w_gate.shape[1]
    return pl.pallas_call(
        gate_kernel,
        in_specs=[hbm, hbm],
        out_specs=[vmem] * 3,
        out_shape=[near((rows, units), F32), near(tokens.shape, BF), near(w_gate.shape, BF)],
        scratch_shapes=[pltpu.SemaphoreType.DMA((3,)), pltpu.SemaphoreType.DMA((4,))],
        compiler_params=pltpu.CompilerParams(vmem_limit_bytes=4 * MIB),
        cost_estimate=pl.CostEstimate(flops=1000000, bytes_accessed=1024, transcendentals=0),
        name="gate_pre",
    )(*[pltpu.with_memory_space_constraint(a, pltpu.HBM) for a in (tokens, w_gate)])


def up_kernel(idx, tok, wu, gate, act_out, slope_out, h_own, h_send):
    z, xh, core = idx[0], idx[1], idx[2]
    for r in range(4):
        cols = pl.ds(pl.multiple_of(lax.rem(z + r, 4) * 256, 256), 256)
        pre = gate[:, cols]
        up = contract(tok[...], wu[:, cols], 1, 0)
        sig = 1.0 / (1.0 + jnp.exp(-pre))
        act = pre * sig
        act_out[:, cols] = act
        slope_out[:, cols] = up * (sig * (1.0 + pre * (1.0 - sig)))
        hid = (act * up).astype(BF).T
        piece = [hid[k * 64 : (k + 1) * 64, :] for k in range(4)]
        own = [jnp.where(core == 0, piece[2 * a], piece[2 * a + 1]) for a in range(2)]
        send = [jnp.where(core == 0, piece[2 * a + 1], piece[2 * a]) for a in range(2)]
        rows = pl.ds(r * 64, 64)
        for ref, pair in ((h_own, own), (h_send, send)):
            ref[0, rows, :] = jnp.where(xh == 0, pair[1], pair[0])
            ref[1, rows, :] = jnp.where(xh == 0, pair[0], pair[1])


def grad_kernel(cot, wd, act, slope, out):
    for j in range(4):
        cols = pl.ds(j * 256, 256)
        grad = contract(cot[...], wd[cols, :], 1, 1)
        out[0, :, cols] = (grad * slope[:, cols]).astype(BF)
        out[1, :, cols] = (grad * act[:, cols]).astype(BF)


def down_kernel(side, scale, h_own, h_peer, cot, cot_peer, out):
    for j in range(4):
        cols = pl.ds(j * 512, 512)
        term = contract(h_own[side], cot[:, cols], 1, 0)
        term = term + contract(h_peer[side], cot_peer[:, cols], 1, 0)
        out[:, cols] = (term * scale).astype(BF)


def weight_kernel(plan, scale, idx, tok, tok_peer, grad, grad_peer, one, two):
    z, xh, core = idx[0], idx[1], idx[2]

    def block(ref, r, side):
        x = xh if side == 1 else 1 - xh
        at = ((lax.rem(z + r, 4) * 2 + x) * 2 + core) * 128
        return ref[:, pl.ds(pl.multiple_of(at, 128), 128)]

    for k in range(2):
        mine, theirs = (
            jnp.concatenate([block(ref, *plan[k][0]), block(ref, *plan[k][1])], axis=1)
            for ref in (tok, tok_peer)
        )
        for j in range(4):
            cols, to = pl.ds((j % 2) * 512, 512), pl.ds(j * 512, 512)
            term = contract(mine, grad[j // 2, :, cols], 0, 0)
            term = (term + contract(theirs, grad_peer[j // 2, :, cols], 0, 0)) * scale
            one[k, :, to] = term[:128, :].astype(BF)
            two[k, :, to] = term[128:, :].astype(BF)


def token_kernel(plan, idx, grad, wg, wu, one, two):
    y, xl = idx[3], idx[4]
    for k in range(2):
        for out, (r, side) in zip((one, two), plan[k]):
            x = xl if side == 1 else 1 - xl
            at = (lax.rem(y + r, 4) * 2 + x) * 256
            rows = pl.ds(pl.multiple_of(at, 256), 256)
            term = contract(grad[0], wg[rows, :], 1, 1) + contract(grad[1], wu[rows, :], 1, 1)
            out[k] = term.astype(BF)


def mix_kernel(own, got, right, left, mid, keep):
    for r, rows in ((2, 0), (1, 64), (3, 128), (0, 192)):
        at = pl.ds(((r) % 4) * 64, 64)
        for side in range(2):
            cols = pl.ds(side * 1024, 1024)
            total = (own[at, cols].astype(F32) + got[at, cols].astype(F32)).astype(BF)
            for place, first, second in ((right, (2, 0), (1, 1)), (left, (2, 1), (3, 0)),
                                         (mid, (1, 0), (3, 1)), (keep, (0, 0), (0, 1))):
                if (r, side) == first:
                    place[0] = total
                if (r, side) == second:
                    place[1] = total


def add(*terms):
    total = terms[0].astype(F32)
    for term in terms[1:]:
        total = total + term.astype(F32)
    return total


def moment_step(old_value, column_total, count):
    return decay_rate * old_value + (1.0 - decay_rate) * (column_total / count + epsilon_one)


def row_totals(values):
    folded = values[:, :128]
    for k in range(1, values.shape[1] // 128):
        folded = folded + values[:, k * 128 : (k + 1) * 128]
    return jnp.sum(folded.T, axis=0, keepdims=True)


def down_rows(row):
    return jnp.broadcast_to(row, (128, row.shape[1])).T


def rows_kernel(keep, near_one, end, got, g_gate, g_up, pay):
    units = g_gate.shape[1]
    sums = []
    for k, out in enumerate((g_gate, g_up)):
        cols = pl.ds(k * units, units)
        g = add(keep[1, :, cols], near_one[1, :, cols], end[:, cols], got[:, cols])
        out[...] = g
        sums.append(row_totals(g * g))
    block = jnp.concatenate(sums + [jnp.zeros((6, 128), F32)], axis=0)
    for k in range(pay.shape[0]):
        pay[k] = block


def columns_kernel(
    counts, g_gate, g_up, keep, left, right, end_a, end_b, rows, row_gate, row_up, row_down,
    g_down, gate_new, up_new, down_new, pay, gate_out, up_out, down_out, work,
):
    all_units, width = counts
    half = end_a.shape[1]
    g_down[:, :half] = add(keep[0], left[1], end_a[...])
    g_down[:, half:] = add(keep[1], right[1], end_b[...])
    total = rows[0]
    for k in range(1, rows.shape[0]):
        total = total + rows[k]
    gate_new[...] = moment_step(row_gate[...], total[0:1, :], all_units)
    up_new[...] = moment_step(row_up[...], total[1:2, :], all_units)
    down = g_down[...]
    down_new[...] = moment_step(row_down[...], row_totals(down * down), width)
    gate_out[...] = gate_new[...]
    up_out[...] = up_new[...]
    down_out[...] = down_new[...]
    at = 0
    for g, new in ((g_gate, gate_new), (g_up, up_new), (g_down, down_new)):
        blocks = g.shape[1] // 128
        scale = 1.0 / down_rows(new[...])
        for k in range(blocks):
            value = g[:, k * 128 : (k + 1) * 128]
            square = value * value
            work[pl.ds(at + k, 1), :] = jnp.sum(square, axis=0, keepdims=True)
            work[pl.ds(at + blocks + k, 1), :] = jnp.sum(square * scale, axis=0, keepdims=True)
        at += 2 * blocks
    for k, new in enumerate((gate_new, up_new, down_new)):
        work[pl.ds(at + k, 1), :] = jnp.broadcast_to(
            jnp.sum(new[...], axis=1, keepdims=True), (1, 128)
        )
    work[pl.ds(at + 3, 5), :] = jnp.zeros((5, 128), F32)
    for k in range(pay.shape[0]):
        pay[k] = work[...]


def spread(value):
    return jnp.broadcast_to(
        jnp.sum(jnp.sum(value, axis=0, keepdims=True), axis=1, keepdims=True), (1, 128)
    )


def partial_kernel(width, got, col_gate, col_up, gate_new, up_new, sums, pay, gate_out, up_out):
    total = got[0]
    for k in range(1, got.shape[0]):
        total = total + got[k]
    gate = moment_step(col_gate[...], total[0:8], width)
    up = moment_step(col_up[...], total[16:24], width)
    gate_new[...] = gate
    up_new[...] = up
    gate_out[...] = gate
    up_out[...] = up
    sums[...] = total[64:72]
    for k in range(pay.shape[0]):
        pay[k, 0:32, :] = total[32:64]
        pay[k, 32:40, :] = jnp.concatenate(
            [
                spread(total[8:16] / gate),
                spread(total[24:32] / up),
                total[66:67],
                jnp.zeros((5, 128), F32),
            ],
            axis=0,
        )


def update_kernel(
    counts, got, sums, col_down, g_gate, g_up, g_down, row_gate, row_up, row_down, col_gate, col_up,
    gate_out, up_out, down_out, down_new,
):
    all_units, width = counts
    total = got[0]
    for k in range(1, got.shape[0]):
        total = total + got[k]
    down = moment_step(col_down[...], total[0:16], all_units)
    down_new[...] = down
    entries = float(width * all_units)
    work = (
        (gate_out, g_gate, row_gate, col_gate[...], sums[0:1, :] / width, total[32:33]),
        (up_out, g_up, row_up, col_up[...], sums[1:2, :] / width, total[33:34]),
        (down_out, g_down, row_down, down, total[34:35] / all_units, spread(total[16:32] / down)),
    )
    for out, g, row, col, mean, squares in work:
        factor = jnp.sqrt(mean) / jnp.maximum(1.0, jnp.sqrt(mean * squares / entries))
        by_row = lax.rsqrt(down_rows(row[...]))
        by_col = lax.rsqrt(col) * factor
        for k in range(col.shape[0]):
            cols = pl.ds(k * 128, 128)
            out[:, cols] = g[:, cols] * by_row * by_col[k : k + 1, :]


def body(
    tokens, cotangent, w_gate, w_up, w_down, row_gate, col_gate, row_up, col_up, row_down, col_down
):
    rows, width = tokens.shape
    units = w_gate.shape[1]
    all_units = units * 8
    scale = float(rows * 16) ** (-0.5)
    dp, mp = lax.axis_index("dp"), lax.axis_index("mp")
    idx = jnp.stack([dp // 4, (dp // 2) % 2, dp % 2, mp // 2, mp % 2]).astype(jnp.int32)
    swap = dp_shift(dc=1)
    forth, back, across = dp_shift(dz=1), dp_shift(dz=3), dp_shift(dx=1)
    y_forth, y_back, x_across = mp_shift(dy=1), mp_shift(dy=3), mp_shift(dx=1)
    one = 2 * rows * width * units

    tok_peer = lax.ppermute(tokens, "dp", swap)
    cot_peer = lax.ppermute(cotangent, "dp", swap)
    square = near((rows, units), F32)
    gate, tokens, w_gate = gate_pre(tokens, w_gate)
    hid = near((2, units // 4, rows), BF)
    act, slope, h_own, h_send = local_kernel(
        "up_pre", up_kernel, idx, [tokens, w_up, gate], [square, square, hid, hid], one
    )
    h_peer = lax.ppermute(h_send, "dp", swap)
    (grad,) = local_kernel(
        "hidden_grad", grad_kernel, None, [cotangent, w_down, act, slope],
        [near((2, rows, units), BF)], one,
        after=(tok_peer, cot_peer),
    )
    grad_peer = lax.ppermute(grad, "dp", swap)

    def down_part(side, after):
        return local_kernel(
            "down", functools.partial(down_kernel, side, scale), None,
            [h_own, h_peer, cotangent, cot_peer], [near((units // 4, width), BF)], one // 2,
            after=after,
        )[0]

    def weight_part(plan, after):
        out = near((2, width // 16, 2 * units), BF)
        return local_kernel(
            "weight", functools.partial(weight_kernel, plan, scale), idx,
            [tokens, tok_peer, grad, grad_peer], [out, out], one, after=after,
        )

    def token_part(plan, after):
        out = near((2, rows, width // 8), BF)
        return local_kernel(
            "token_grad", functools.partial(token_kernel, plan), idx, [grad, w_gate, w_up],
            [out, out], one, after=after,
        )

    tok_r, tok_l = token_part(FIRST, ())
    pair_r, pair_l = weight_part(FIRST, (tok_r,))
    away = down_part(0, (pair_r,))
    pair_a, pair_b = weight_part(SECOND, (away,))
    tok_a, tok_b = token_part(SECOND, (pair_a,))
    own = down_part(1, (tok_a,))

    def ring_first(axis, pairs, right, left, mid_a, mid_b):
        from_left = lax.ppermute(right, axis, pairs[0])
        from_right = lax.ppermute(left, axis, pairs[1])
        onward = add(mid_a, from_left[0]).astype(BF)
        backward = add(mid_b, from_right[0]).astype(BF)
        return onward, backward, from_left, from_right

    def ring_second(axis, pairs, onward, backward):
        return lax.ppermute(onward, axis, pairs[0]), lax.ppermute(backward, axis, pairs[1])

    ring, y_ring = (forth, back), (y_forth, y_back)
    pair_mid = ring_first("dp", ring, pair_r, pair_l, pair_a[0], pair_b[0])
    pair_end = ring_second("dp", ring, *pair_mid[:2])
    part = near((2, units // 16, width // 2), BF)
    down_r, down_l, down_m, down_k = local_kernel(
        "down_mix", mix_kernel, None, [own, lax.ppermute(away, "dp", across)], [part] * 4, 1000
    )
    down_mid = ring_first("dp", ring, down_r, down_l, down_m[0], down_m[1])
    down_end = ring_second("dp", ring, *down_mid[:2])
    tok_mid = ring_first("mp", y_ring, tok_r, tok_l, tok_a[0], tok_b[0])
    tok_end = ring_second("mp", y_ring, *tok_mid[:2])

    def cross(keep, mid, end, axis, pairs):
        return lax.ppermute(add(keep[1], mid[3][1], end[0]).astype(BF), axis, pairs)

    pair_got = cross(pair_a, pair_mid, pair_end, "dp", across)
    tok_got = cross(tok_a, tok_mid, tok_end, "mp", x_across)
    token_grad = add(tok_b[1], tok_mid[2][1], tok_end[1], tok_got).astype(BF)

    shard = near((width // 16, units), F32)
    g_gate, g_up, pay = local_kernel(
        "row_sums", rows_kernel, None,
        [pair_b, pair_mid[2], pair_end[1], pair_got],
        [shard, shard, near((8, 8, 128), F32)], 1000, after=(token_grad,), limit=4,
    )
    row_got = lax.all_to_all(pay, "mp", 0, 0, tiled=True)

    counts = (all_units, width)
    line = near((1, width // 16), F32)
    short = near((1, units // 16), F32)
    line_out = jax.ShapeDtypeStruct((1, width // 16), F32)
    short_out = jax.ShapeDtypeStruct((1, units // 16), F32)
    g_down, row_gate_new, row_up_new, row_down_new, pay, *rows_out, _ = local_kernel(
        "column_sums", functools.partial(columns_kernel, counts), None,
        [
            g_gate, g_up, down_k, down_mid[3], down_mid[2], *down_end, row_got,
            row_gate.reshape(1, -1), row_up.reshape(1, -1), row_down.reshape(1, -1),
        ],
        [near((units // 16, width), F32), line, line, short, near((16, 72, 128), F32),
         line_out, line_out, short_out, near((72, 128), F32)],
        1000, limit=4,
    )
    col_got = lax.all_to_all(pay, "dp", 0, 0, tiled=True)

    lines = near((units // 128, 128), F32)
    lines_out = jax.ShapeDtypeStruct((units // 128, 128), F32)
    col_gate_new, col_up_new, sums, pay, *cols_out = local_kernel(
        "partial_sums", functools.partial(partial_kernel, width), None,
        [col_got, col_gate.reshape(-1, 128), col_up.reshape(-1, 128)],
        [lines, lines, near((8, 128), F32), near((8, 40, 128), F32), lines_out, lines_out], 1000, limit=4,
    )
    last = lax.all_to_all(pay, "mp", 0, 0, tiled=True)
    update_gate, update_up, update_down, col_down_new = local_kernel(
        "updates", functools.partial(update_kernel, counts), None,
        [
            last, sums, col_down.reshape(-1, 128), g_gate, g_up, g_down,
            row_gate_new, row_up_new, row_down_new, col_gate_new, col_up_new,
        ],
        [
            jax.ShapeDtypeStruct((width // 16, units), F32),
            jax.ShapeDtypeStruct((width // 16, units), F32),
            jax.ShapeDtypeStruct((units // 16, width), F32),
            jax.ShapeDtypeStruct((width // 128, 128), F32),
        ],
        1000, limit=8,
    )
    return (
        token_grad,
        update_gate,
        update_up,
        update_down,
        rows_out[0].reshape(-1),
        cols_out[0].reshape(-1),
        rows_out[1].reshape(-1),
        cols_out[1].reshape(-1),
        rows_out[2].reshape(-1),
        col_down_new.reshape(-1),
    )


def solution(mesh):
    in_specs = (
        P("dp", None),
        P("dp", None),
        P(None, "mp"),
        P(None, "mp"),
        P("mp", None),
        P("dp"),
        P("mp"),
        P("dp"),
        P("mp"),
        P(("mp", "dp")),
        P(),
    )
    out_specs = (
        P("dp", "mp"),
        P("dp", "mp"),
        P("dp", "mp"),
        P(("mp", "dp"), None),
        P("dp"),
        P("mp"),
        P("dp"),
        P("mp"),
        P(("mp", "dp")),
        P(),
    )
    return jax.shard_map(body, mesh=mesh, in_specs=in_specs, out_specs=out_specs, check_vma=False)
```

time: 485 us -> 129 us (0.27)
  waiting for transfers between devices: 192 us -> 28.4 us
  blocking collectives: 183 us -> 27.4 us
  matrix products: 46.6 us -> 0 us
  Pallas kernels: 0 us -> 42.8 us
  starting transfers between devices: 0.34 us -> 27.5 us
  local copies, waits for them, and re-layouts: 25 us -> 0.14 us
  other arithmetic: 21.4 us -> 1.11 us
  between operations: 15.3 us -> 0.93 us
    psum x4 -> x0, blocking collectives: 183 us -> none  [the longest x1 66.9 us: body(): row_means = lax.psum(new_sums, ('dp', 'mp')) / row_counts]
    unnamed x6 -> x0, waiting for transfers between devices: 132 us -> none
    reduce_scatter x2 -> x0, waiting for transfers between devices: 59.7 us -> none  [the longest x1 59.6 us: body(): lax.psum_scatter(weight_term(hidden, cotangent).astype(jnp.bfloat16), 'dp...]
    dot_general x8 -> x0, matrix products: 46.6 us -> none  [the longest x3 21.3 us: weight_term(): jnp.einsum('tr,tc->rc', left_side, right_side, preferred_element_type=jnp...]
    pallas_call x0 -> x14, Pallas kernels: none -> 42.8 us  [the longest x13 35.2 us: local_kernel(): pl.pallas_call(run, in_specs=specs + [vmem] * count + [pl.BlockSpec(memor...]
    all_to_all x0 -> x2, blocking collectives: none -> 27.4 us  [the longest x1 18.2 us: body(): col_got = lax.all_to_all(pay, 'dp', 0, 0, tiled=True)]
    ppermute x0 -> x19, starting transfers between devices: none -> 23.8 us  [the longest x3 5.52 us: ring_first(): from_right = lax.ppermute(left, axis, pairs[1])]
    unnamed x50 -> x20, local copies, waits for them, and re-layouts: 23.7 us -> 0.05 us
  transfers between devices with their start and end apart: 4 -> 20, of which waited for: 3 -> 6; matrix products, arithmetic and copies ran while one was open for 13% -> 1% of each run, Pallas kernels for 0% -> 28%
where the time goes in v1:
time: 129 us; the launch traced here: 128 us
  Pallas kernels  42.8 us (33%)
  waiting for transfers between devices  28.4 us (22%)
  starting transfers between devices  27.5 us (21%)
  blocking collectives  27.4 us (21%)
    pallas_call x13, Pallas kernels, local_kernel(): pl.pallas_call(run, in_specs=specs + [vmem] * count + [pl.BlockSpec(memor...  35.2 us
    all_to_all x1, blocking collectives, body(): col_got = lax.all_to_all(pay, 'dp', 0, 0, tiled=True)  18.2 us
    ppermute x3, waiting for transfers between devices, ring_second(): lax.ppermute(onward, axis, pairs[0])  12.8 us
    all_to_all x1, blocking collectives, body(): last = lax.all_to_all(pay, 'mp', 0, 0, tiled=True)  9.21 us
    pallas_call x1, Pallas kernels, gate_pre(): pl.pallas_call(gate_kernel, in_specs=[hbm, hbm], out_specs=[vmem] * 3, ou...  7.59 us
    all_to_all x1, waiting for transfers between devices, body(): row_got = lax.all_to_all(pay, 'mp', 0, 0, tiled=True)  6.24 us
    ppermute x3, waiting for transfers between devices, ring_second(): lax.ppermute(backward, axis, pairs[1])  5.52 us
    ppermute x3, starting transfers between devices, ring_first(): from_right = lax.ppermute(left, axis, pairs[1])  5.52 us
  transfers between devices with their start and end apart: 20, of which 6 were waited for; matrix products, arithmetic and copies ran while one was open for 1% of the time, Pallas kernels for 28%

profile of v1, /device:TPU:0, one launch (start us, length us, event | category | flops | bytes accessed | tf_op | source)
XLA Modules:
  0.0 128.2 jit_solution(9591979090705070647)
XLA Ops:
  0.6 0.1 collective-permute-start
  0.7 0.5 collective-permute-start.1
  1.3 7.6 %gate_pre.1 = (f32[768,1024]{1,0:T(8,128)S(1)}, bf16[768,2048]{1,0:T(8,128)(2,1)S(1)}, bf16[2048,1024]{1,0:T(8,128)(2,1)S(1)}) custom-call(bf16[768,2048]{1,0:T(8,128)(2,1)} %tok_in.1, bf16[2048,1024]{1,0:T(8,128)(2,1)} %wg_in.1), custom_call_target="tpu_custom_call" | custom-call | flops 1000000 | bytes 1024 | tf_op jit(solution)/shard_map/gate_pre/pallas_call | solution.py:88
  9.0 5.1 %up_pre.1 = (f32[768,1024]{1,0:T(8,128)S(1)}, f32[768,1024]{1,0:T(8,128)S(1)}, bf16[2,256,768]{2,1,0:T(8,128)(2,1)S(1)}, bf16[2,256,768]{2,1,0:T(8,128)(2,1)S(1)}) custom-call(s32[5]{0:T(128)S(1)} %stack.23.refs_0_, bf16[768,2048]{1,0:T(8,128)(2,1)S(1)} %get-tuple-element.50.refs_1_, bf16[2048,1024]{1,0:T(8,128)(2,1)S(1)} %copy-done, ...), custom_call_target="tpu_custom_call" | custom-call | flops 201326592 | bytes 1024 | tf_op jit(solution)/shard_map/up_pre/pallas_call | solution.py:48
  14.1 3.5 %hidden_grad.1.refs_1_.refs_3_ = bf16[2,768,1024]{2,1,0:T(8,128)(2,1)S(1)} custom-call(bf16[768,2048]{1,0:T(8,128)(2,1)S(1)} %copy-done.1, bf16[1024,2048]{1,0:T(8,128)(2,1)S(1)} %copy-done.2, f32[768,1024]{1,0:T(8,128)S(1)} %get-tuple-element.52.refs_2_, f32[768,1024]{1,0:T(8,128)S(1)} %get-tuple-element.53.refs_3_, ...), custom_call_target="tpu_custom_call" | custom-call | flops 201326592 | bytes 1024 | tf_op jit(solution)/shard_map/hidden_grad/pallas_call | solution.py:48
  17.5 0.2 collective-permute-start.2
  17.7 0.4 collective-permute-start.3
  18.1 4.0 %token_grad.2 = (bf16[2,768,256]{2,1,0:T(8,128)(2,1)S(1)}, bf16[2,768,256]{2,1,0:T(8,128)(2,1)S(1)}) custom-call(s32[5]{0:T(128)S(1)} %stack.23.refs_0_, bf16[2,768,1024]{2,1,0:T(8,128)(2,1)S(1)} %hidden_grad.1.refs_1_.refs_3_, bf16[2048,1024]{1,0:T(8,128)(2,1)S(1)} %get-tuple-element.54.refs_2_, bf16[2048,1024]{1,0:T(8,128)(2,1)S(1)} %copy-done), custom_call_target="tpu_custom_call" | custom-call | flops 201326592 | bytes 1024 | tf_op jit(solution)/shard_map/token_grad/pallas_call | solution.py:48
  22.1 1.7 %collective-permute-start.4 = (bf16[2,768,256]{2,1,0:T(8,128)(2,1)S(1)}, bf16[2,768,256]{2,1,0:T(8,128)(2,1)S(1)}, u32[]{:S(2)}, u32[]{:S(2)}) collective-permute-start(bf16[2,768,256]{2,1,0:T(8,128)(2,1)S(1)} %get-tuple-element.57.refs_5_), channel_id=1, source_target_pairs={{0,2},{1,3},{2,4},{3,5},{4,6},{5,7},{6,0},{7,1},{8,10},{9,11},{10,... | collective-permute-start | bytes 2359304 | tf_op jit(solution)/shard_map/ppermute | solution.py:368
  23.9 1.6 %collective-permute-start.5 = (bf16[2,768,256]{2,1,0:T(8,128)(2,1)S(1)}, bf16[2,768,256]{2,1,0:T(8,128)(2,1)S(1)}, u32[]{:S(2)}, u32[]{:S(2)}) collective-permute-start(bf16[2,768,256]{2,1,0:T(8,128)(2,1)S(1)} %get-tuple-element.61), channel_id=1, source_target_pairs={{0,6},{1,7},{2,0},{3,1},{4,2},{5,3},{6,4},{7,5},{8,14},{9,15},{10,... | collective-permute-start | bytes 2359304 | tf_op jit(solution)/shard_map/ppermute | solution.py:369
  25.4 5.4 %weight.2 = (bf16[2,128,2048]{2,1,0:T(8,128)(2,1)S(1)}, bf16[2,128,2048]{2,1,0:T(8,128)(2,1)S(1)}) custom-call(s32[5]{0:T(128)S(1)} %stack.23.refs_0_, bf16[768,2048]{1,0:T(8,128)(2,1)S(1)} %get-tuple-element.50.refs_1_, bf16[768,2048]{1,0:T(8,128)(2,1)} %collective-permute-done.refs_4_.refs_2_, bf16[2,768,1024]{2,1,0:T(8,128)(2,1)S(1)} %hidden_grad.1.refs_1_.refs_3_, ...), custom_call_target="tpu_custom_call" | custom-call | flops 201326592 | bytes 1024 | tf_op jit(solution)/shard_map/weight/pallas_call | solution.py:48
  30.9 2.0 %collective-permute-start.9 = (bf16[2,128,2048]{2,1,0:T(8,128)(2,1)S(1)}, bf16[2,128,2048]{2,1,0:T(8,128)(2,1)S(1)}, u32[]{:S(2)}, u32[]{:S(2)}) collective-permute-start(bf16[2,128,2048]{2,1,0:T(8,128)(2,1)S(1)} %get-tuple-element.58.refs_4_), channel_id=1, source_target_pairs={{0,32},{8,40},{16,48},{24,56},{32,64},{40,72},{48,80},{56,88},{64,... | collective-permute-start | bytes 3145736 | tf_op jit(solution)/shard_map/ppermute | solution.py:368
  32.9 1.8 %down.2.refs_5_ = bf16[256,2048]{1,0:T(8,128)(2,1)S(1)} custom-call(bf16[2,256,768]{2,1,0:T(8,128)(2,1)S(1)} %get-tuple-element.55.refs_0_, bf16[2,256,768]{2,1,0:T(8,128)(2,1)S(1)} %collective-permute-done.3.refs_1_, bf16[768,2048]{1,0:T(8,128)(2,1)S(1)} %copy-done.1, bf16[768,2048]{1,0:T(8,128)(2,1)S(1)} %collective-permute-done.1.refs_5_.refs_3_, ...), custom_call_target="tpu_custom_call" | custom-call | flops 100663296 | bytes 1024 | tf_op jit(solution)/shard_map/down/pallas_call | solution.py:48
  34.7 3.1 %collective-permute-start.14 = (bf16[256,2048]{1,0:T(8,128)(2,1)S(1)}, bf16[256,2048]{1,0:T(8,128)(2,1)S(1)}, u32[]{:S(2)}, u32[]{:S(2)}) collective-permute-start(bf16[256,2048]{1,0:T(8,128)(2,1)S(1)} %down.2.refs_5_), channel_id=1, source_target_pairs={{0,16},{8,24},{16,0},{24,8},{32,48},{40,56},{48,32},{56,40},{64,80... | collective-permute-start | bytes 3145736 | tf_op jit(solution)/shard_map/ppermute | solution.py:382
  37.9 2.1 %collective-permute-start.10 = (bf16[2,128,2048]{2,1,0:T(8,128)(2,1)S(1)}, bf16[2,128,2048]{2,1,0:T(8,128)(2,1)S(1)}, u32[]{:S(2)}, u32[]{:S(2)}) collective-permute-start(bf16[2,128,2048]{2,1,0:T(8,128)(2,1)S(1)} %get-tuple-element.64), channel_id=1, source_target_pairs={{0,96},{8,104},{16,112},{24,120},{32,0},{40,8},{48,16},{56,24},{64... | collective-permute-start | bytes 3145736 | tf_op jit(solution)/shard_map/ppermute | solution.py:369
  40.0 5.4 %weight.3 = (bf16[2,128,2048]{2,1,0:T(8,128)(2,1)S(1)}, bf16[2,128,2048]{2,1,0:T(8,128)(2,1)S(1)}) custom-call(s32[5]{0:T(128)S(1)} %stack.23.refs_0_, bf16[768,2048]{1,0:T(8,128)(2,1)S(1)} %get-tuple-element.50.refs_1_, bf16[768,2048]{1,0:T(8,128)(2,1)} %collective-permute-done.refs_4_.refs_2_, bf16[2,768,1024]{2,1,0:T(8,128)(2,1)S(1)} %hidden_grad.1.refs_1_.refs_3_, ...), custom_call_target="tpu_custom_call" | custom-call | flops 201326592 | bytes 1024 | tf_op jit(solution)/shard_map/weight/pallas_call | solution.py:48
  45.4 4.0 %token_grad.3 = (bf16[2,768,256]{2,1,0:T(8,128)(2,1)S(1)}, bf16[2,768,256]{2,1,0:T(8,128)(2,1)S(1)}) custom-call(s32[5]{0:T(128)S(1)} %stack.23.refs_0_, bf16[2,768,1024]{2,1,0:T(8,128)(2,1)S(1)} %hidden_grad.1.refs_1_.refs_3_, bf16[2048,1024]{1,0:T(8,128)(2,1)S(1)} %get-tuple-element.54.refs_2_, bf16[2048,1024]{1,0:T(8,128)(2,1)S(1)} %copy-done, ...), custom_call_target="tpu_custom_call" | custom-call | flops 201326592 | bytes 1024 | tf_op jit(solution)/shard_map/token_grad/pallas_call | solution.py:48
  49.4 0.1 fusion.7
  49.5 0.4 collective-permute-start.7
  49.9 0.1 fusion.6
  50.0 2.9 %collective-permute-start.6 = (bf16[768,256]{1,0:T(8,128)(2,1)S(1)}, bf16[768,256]{1,0:T(8,128)(2,1)S(1)}, u32[]{:S(2)}, u32[]{:S(2)}) collective-permute-start(bf16[768,256]{1,0:T(8,128)(2,1)S(1)} %fusion.6), channel_id=1, source_target_pairs={{0,6},{1,7},{2,0},{3,1},{4,2},{5,3},{6,4},{7,5},{8,14},{9,15},{10,... | collective-permute-start | bytes 1179656 | tf_op jit(solution)/shard_map/ppermute | solution.py:375
  53.0 1.8 %down.3.refs_0_ = bf16[256,2048]{1,0:T(8,128)(2,1)S(1)} custom-call(bf16[2,256,768]{2,1,0:T(8,128)(2,1)S(1)} %get-tuple-element.55.refs_0_, bf16[2,256,768]{2,1,0:T(8,128)(2,1)S(1)} %collective-permute-done.3.refs_1_, bf16[768,2048]{1,0:T(8,128)(2,1)S(1)} %copy-done.1, bf16[768,2048]{1,0:T(8,128)(2,1)S(1)} %collective-permute-done.1.refs_5_.refs_3_, ...), custom_call_target="tpu_custom_call" | custom-call | flops 100663296 | bytes 1024 | tf_op jit(solution)/shard_map/down/pallas_call | solution.py:48
  54.8 3.4 %collective-permute-done.9.refs_1_ = bf16[2,128,2048]{2,1,0:T(8,128)(2,1)S(1)} collective-permute-done((bf16[2,128,2048]{2,1,0:T(8,128)(2,1)S(1)}, bf16[2,128,2048]{2,1,0:T(8,128)(2,1)S(1)}, u32[]{:S(2)}, u32[]{:S(2)}) %collective-permute-start.9) | collective-permute-done | bytes 1048608 | tf_op jit(solution)/shard_map/ppermute | solution.py:368
  58.2 0.1 fusion.5
  58.4 2.7 %collective-permute-done.7 = bf16[768,256]{1,0:T(8,128)(2,1)S(1)} collective-permute-done((bf16[768,256]{1,0:T(8,128)(2,1)S(1)}, bf16[768,256]{1,0:T(8,128)(2,1)S(1)}, u32[]{:S(2)}, u32[]{:S(2)}) %collective-permute-start.7) | collective-permute-done | bytes 393248 | tf_op jit(solution)/shard_map/ppermute | solution.py:375
  61.1 0.1 fusion.1
  61.2 0.7 collective-permute-start.8
  61.9 0.2 down_mix.1
  62.2 1.8 %collective-permute-start.15 = (bf16[2,64,1024]{2,1,0:T(8,128)(2,1)S(1)}, bf16[2,64,1024]{2,1,0:T(8,128)(2,1)S(1)}, u32[]{:S(2)}, u32[]{:S(2)}) collective-permute-start(bf16[2,64,1024]{2,1,0:T(8,128)(2,1)S(1)} %get-tuple-element.68), channel_id=1, source_target_pairs={{0,96},{8,104},{16,112},{24,120},{32,0},{40,8},{48,16},{56,24},{64... | collective-permute-start | bytes 786440 | tf_op jit(solution)/shard_map/ppermute | solution.py:369
  64.0 0.3 collective-permute-start.16
  64.3 0.1 fusion.4
  64.4 10.1 %collective-permute-done.12 = bf16[128,2048]{1,0:T(8,128)(2,1)S(1)} collective-permute-done((bf16[128,2048]{1,0:T(8,128)(2,1)S(1)}, bf16[128,2048]{1,0:T(8,128)(2,1)S(1)}, u32[]{:S(2)}, u32[]{:S(2)}) %collective-permute-start.12) | collective-permute-done | bytes 524320 | tf_op jit(solution)/shard_map/ppermute | solution.py:375
  74.5 0.5 collective-permute-start.11
  75.0 0.2 fusion
  75.2 3.1 %collective-permute-start.13 = (bf16[128,2048]{1,0:T(8,128)(2,1)S(1)}, bf16[128,2048]{1,0:T(8,128)(2,1)S(1)}, u32[]{:S(2)}, u32[]{:S(2)}) collective-permute-start(bf16[128,2048]{1,0:T(8,128)(2,1)S(1)} %fusion), channel_id=1, source_target_pairs={{0,16},{8,24},{16,0},{24,8},{32,48},{40,56},{48,32},{56,40},{64,80... | collective-permute-start | bytes 1572872 | tf_op jit(solution)/shard_map/ppermute | solution.py:390
  78.5 0.5 collective-permute-start.18
  78.9 1.6 %collective-permute-start.17 = (bf16[64,1024]{1,0:T(8,128)(2,1)S(1)}, bf16[64,1024]{1,0:T(8,128)(2,1)S(1)}, u32[]{:S(2)}, u32[]{:S(2)}) collective-permute-start(bf16[64,1024]{1,0:T(8,128)(2,1)S(1)} %get-tuple-element.91), channel_id=1, source_target_pairs={{0,32},{8,40},{16,48},{24,56},{32,64},{40,72},{48,80},{56,88},{64,... | collective-permute-start | bytes 393224 | tf_op jit(solution)/shard_map/ppermute | solution.py:375
  80.6 0.2 fusion.3.refs_4_
  80.8 5.5 %collective-permute-done.11.refs_2_ = bf16[128,2048]{1,0:T(8,128)(2,1)S(1)} collective-permute-done((bf16[128,2048]{1,0:T(8,128)(2,1)S(1)}, bf16[128,2048]{1,0:T(8,128)(2,1)S(1)}, u32[]{:S(2)}, u32[]{:S(2)}) %collective-permute-start.11) | collective-permute-done | bytes 524320 | tf_op jit(solution)/shard_map/ppermute | solution.py:375
  86.3 0.4 collective-permute-done.13.refs_3_
  86.8 1.0 row_sums.1
  87.8 3.7 %all-to-all-start = ((f32[8,8,128]{2,1,0:T(8,128)}), f32[8,8,128]{2,1,0:T(8,128)S(1)}, u32[]{:S(2)}, u32[]{:S(2)}) async-start(f32[8,8,128]{2,1,0:T(8,128)} %get-tuple-element.71), calls=%async_computation | async-start | bytes 65536 | tf_op jit(solution)/shard_map/all_to_all | solution.py:402
  91.5 6.2 %all-to-all-done.refs_7_ = f32[8,8,128]{2,1,0:T(8,128)S(1)} async-done(((f32[8,8,128]{2,1,0:T(8,128)}), f32[8,8,128]{2,1,0:T(8,128)S(1)}, u32[]{:S(2)}, u32[]{:S(2)}) %all-to-all-start) | async-done | bytes 32800 | tf_op jit(solution)/shard_map/all_to_all | solution.py:402
  97.8 1.1 column_sums.1
  98.9 18.2 %all_to_all.15.refs_0_ = f32[16,72,128]{2,1,0:T(8,128)S(1)} all-to-all(f32[16,72,128]{2,1,0:T(8,128)S(1)} %get-tuple-element.72), channel_id=1, replica_groups=mesh['dp'=16,'mp'=8] {'dp'}, dimensions={0} | all-to-all | bytes 1179648 | tf_op jit(solution)/shard_map/all_to_all | solution.py:419
  117.1 0.6 partial_sums.1
  117.7 9.2 %all_to_all.16.refs_0_ = f32[8,40,128]{2,1,0:T(8,128)S(1)} all-to-all(f32[8,40,128]{2,1,0:T(8,128)S(1)} %get-tuple-element.73), channel_id=1, replica_groups=mesh['dp'=16,'mp'=8] {'mp'}, dimensions={0} | all-to-all | bytes 327680 | tf_op jit(solution)/shard_map/all_to_all | solution.py:428
  126.9 1.3 updates.1
  (37 shorter events, 0.3 us)
Async XLA Ops:
  0.6 13.4 %collective-permute-start = (bf16[768,2048]{1,0:T(8,128)(2,1)}, bf16[768,2048]{1,0:T(8,128)(2,1)}, u32[]{:S(2)}, u32[]{:S(2)}) collective-permute-start(bf16[768,2048]{1,0:T(8,128)(2,1)} %tok_in.1), channel_id=1, source_target_pairs={{0,8},{8,0},{16,24},{24,16},{32,40},{40,32},{48,56},{56,48},{64,72... | collective-permute-start | bytes 9437192 | tf_op jit(solution)/shard_map/ppermute | solution.py:323
  0.7 13.3 %collective-permute-start.1 = (bf16[768,2048]{1,0:T(8,128)(2,1)}, bf16[768,2048]{1,0:T(8,128)(2,1)S(1)}, u32[]{:S(2)}, u32[]{:S(2)}) collective-permute-start(bf16[768,2048]{1,0:T(8,128)(2,1)} %refs_2_.5), channel_id=1, source_target_pairs={{0,8},{8,0},{16,24},{24,16},{32,40},{40,32},{48,56},{56,48},{64,72... | collective-permute-start | bytes 9437192 | tf_op jit(solution)/shard_map/ppermute | solution.py:324
  1.3 7.6 %copy-start = (bf16[2048,1024]{1,0:T(8,128)(2,1)S(1)}, bf16[2048,1024]{1,0:T(8,128)(2,1)}, u32[]{:S(2)}) copy-start(bf16[2048,1024]{1,0:T(8,128)(2,1)} %refs_3_.3) | copy-start | bytes 12582916
  8.9 5.1 %copy-start.1 = (bf16[768,2048]{1,0:T(8,128)(2,1)S(1)}, bf16[768,2048]{1,0:T(8,128)(2,1)}, u32[]{:S(2)}) copy-start(bf16[768,2048]{1,0:T(8,128)(2,1)} %refs_2_.5) | copy-start | bytes 9437188
  8.9 5.1 %copy-start.2 = (bf16[1024,2048]{1,0:T(8,128)(2,1)S(1)}, bf16[1024,2048]{1,0:T(8,128)(2,1)}, u32[]{:S(2)}) copy-start(bf16[1024,2048]{1,0:T(8,128)(2,1)} %refs_1_.1) | copy-start | bytes 12582916
  17.5 7.9 %collective-permute-start.2 = (bf16[2,768,1024]{2,1,0:T(8,128)(2,1)S(1)}, bf16[2,768,1024]{2,1,0:T(8,128)(2,1)S(1)}, u32[]{:S(2)}, u32[]{:S(2)}) collective-permute-start(bf16[2,768,1024]{2,1,0:T(8,128)(2,1)S(1)} %hidden_grad.1.refs_1_.refs_3_), channel_id=1, source_target_pairs={{0,8},{8,0},{16,24},{24,16},{32,40},{40,32},{48,56},{56,48},{64,72... | collective-permute-start | bytes 9437192 | tf_op jit(solution)/shard_map/ppermute | solution.py:337
  17.7 15.2 %collective-permute-start.3 = (bf16[2,256,768]{2,1,0:T(8,128)(2,1)S(1)}, bf16[2,256,768]{2,1,0:T(8,128)(2,1)S(1)}, u32[]{:S(2)}, u32[]{:S(2)}) collective-permute-start(bf16[2,256,768]{2,1,0:T(8,128)(2,1)S(1)} %get-tuple-element.56), channel_id=1, source_target_pairs={{0,8},{8,0},{16,24},{24,16},{32,40},{40,32},{48,56},{56,48},{64,72... | collective-permute-start | bytes 2359304 | tf_op jit(solution)/shard_map/ppermute | solution.py:331
  22.1 27.2 %collective-permute-start.4 = (bf16[2,768,256]{2,1,0:T(8,128)(2,1)S(1)}, bf16[2,768,256]{2,1,0:T(8,128)(2,1)S(1)}, u32[]{:S(2)}, u32[]{:S(2)}) collective-permute-start(bf16[2,768,256]{2,1,0:T(8,128)(2,1)S(1)} %get-tuple-element.57.refs_5_), channel_id=1, source_target_pairs={{0,2},{1,3},{2,4},{3,5},{4,6},{5,7},{6,0},{7,1},{8,10},{9,11},{10,... | collective-permute-start | bytes 2359304 | tf_op jit(solution)/shard_map/ppermute | solution.py:368
  23.9 26.1 %collective-permute-start.5 = (bf16[2,768,256]{2,1,0:T(8,128)(2,1)S(1)}, bf16[2,768,256]{2,1,0:T(8,128)(2,1)S(1)}, u32[]{:S(2)}, u32[]{:S(2)}) collective-permute-start(bf16[2,768,256]{2,1,0:T(8,128)(2,1)S(1)} %get-tuple-element.61), channel_id=1, source_target_pairs={{0,6},{1,7},{2,0},{3,1},{4,2},{5,3},{6,4},{7,5},{8,14},{9,15},{10,... | collective-permute-start | bytes 2359304 | tf_op jit(solution)/shard_map/ppermute | solution.py:369
  30.9 27.3 %collective-permute-start.9 = (bf16[2,128,2048]{2,1,0:T(8,128)(2,1)S(1)}, bf16[2,128,2048]{2,1,0:T(8,128)(2,1)S(1)}, u32[]{:S(2)}, u32[]{:S(2)}) collective-permute-start(bf16[2,128,2048]{2,1,0:T(8,128)(2,1)S(1)} %get-tuple-element.58.refs_4_), channel_id=1, source_target_pairs={{0,32},{8,40},{16,48},{24,56},{32,64},{40,72},{48,80},{56,88},{64,... | collective-permute-start | bytes 3145736 | tf_op jit(solution)/shard_map/ppermute | solution.py:368
  34.7 27.2 %collective-permute-start.14 = (bf16[256,2048]{1,0:T(8,128)(2,1)S(1)}, bf16[256,2048]{1,0:T(8,128)(2,1)S(1)}, u32[]{:S(2)}, u32[]{:S(2)}) collective-permute-start(bf16[256,2048]{1,0:T(8,128)(2,1)S(1)} %down.2.refs_5_), channel_id=1, source_target_pairs={{0,16},{8,24},{16,0},{24,8},{32,48},{40,56},{48,32},{56,40},{64,80... | collective-permute-start | bytes 3145736 | tf_op jit(solution)/shard_map/ppermute | solution.py:382
  37.9 26.1 %collective-permute-start.10 = (bf16[2,128,2048]{2,1,0:T(8,128)(2,1)S(1)}, bf16[2,128,2048]{2,1,0:T(8,128)(2,1)S(1)}, u32[]{:S(2)}, u32[]{:S(2)}) collective-permute-start(bf16[2,128,2048]{2,1,0:T(8,128)(2,1)S(1)} %get-tuple-element.64), channel_id=1, source_target_pairs={{0,96},{8,104},{16,112},{24,120},{32,0},{40,8},{48,16},{56,24},{64... | collective-permute-start | bytes 3145736 | tf_op jit(solution)/shard_map/ppermute | solution.py:369
  49.5 11.6 %collective-permute-start.7 = (bf16[768,256]{1,0:T(8,128)(2,1)S(1)}, bf16[768,256]{1,0:T(8,128)(2,1)S(1)}, u32[]{:S(2)}, u32[]{:S(2)}) collective-permute-start(bf16[768,256]{1,0:T(8,128)(2,1)S(1)} %fusion.7), channel_id=1, source_target_pairs={{0,2},{1,3},{2,4},{3,5},{4,6},{5,7},{6,0},{7,1},{8,10},{9,11},{10,... | collective-permute-start | bytes 1179656 | tf_op jit(solution)/shard_map/ppermute | solution.py:375
  50.0 28.9 %collective-permute-start.6 = (bf16[768,256]{1,0:T(8,128)(2,1)S(1)}, bf16[768,256]{1,0:T(8,128)(2,1)S(1)}, u32[]{:S(2)}, u32[]{:S(2)}) collective-permute-start(bf16[768,256]{1,0:T(8,128)(2,1)S(1)} %fusion.6), channel_id=1, source_target_pairs={{0,6},{1,7},{2,0},{3,1},{4,2},{5,3},{6,4},{7,5},{8,14},{9,15},{10,... | collective-permute-start | bytes 1179656 | tf_op jit(solution)/shard_map/ppermute | solution.py:375
  58.3 16.1 %collective-permute-start.12 = (bf16[128,2048]{1,0:T(8,128)(2,1)S(1)}, bf16[128,2048]{1,0:T(8,128)(2,1)S(1)}, u32[]{:S(2)}, u32[]{:S(2)}) collective-permute-start(bf16[128,2048]{1,0:T(8,128)(2,1)S(1)} %fusion.5), channel_id=1, source_target_pairs={{0,32},{8,40},{16,48},{24,56},{32,64},{40,72},{48,80},{56,88},{64,... | collective-permute-start | bytes 1572872 | tf_op jit(solution)/shard_map/ppermute | solution.py:375
  61.2 19.3 %collective-permute-start.8 = (bf16[768,256]{1,0:T(8,128)(2,1)S(1)}, bf16[768,256]{1,0:T(8,128)(2,1)S(1)}, u32[]{:S(2)}, u32[]{:S(2)}) collective-permute-start(bf16[768,256]{1,0:T(8,128)(2,1)S(1)} %fusion.1), channel_id=1, source_target_pairs={{0,1},{1,0},{2,3},{3,2},{4,5},{5,4},{6,7},{7,6},{8,9},{9,8},{10,11... | collective-permute-start | bytes 1179656 | tf_op jit(solution)/shard_map/ppermute | solution.py:390
  62.2 13.1 %collective-permute-start.15 = (bf16[2,64,1024]{2,1,0:T(8,128)(2,1)S(1)}, bf16[2,64,1024]{2,1,0:T(8,128)(2,1)S(1)}, u32[]{:S(2)}, u32[]{:S(2)}) collective-permute-start(bf16[2,64,1024]{2,1,0:T(8,128)(2,1)S(1)} %get-tuple-element.68), channel_id=1, source_target_pairs={{0,96},{8,104},{16,112},{24,120},{32,0},{40,8},{48,16},{56,24},{64... | collective-permute-start | bytes 786440 | tf_op jit(solution)/shard_map/ppermute | solution.py:369
  64.0 14.4 %collective-permute-start.16 = (bf16[2,64,1024]{2,1,0:T(8,128)(2,1)S(1)}, bf16[2,64,1024]{2,1,0:T(8,128)(2,1)S(1)}, u32[]{:S(2)}, u32[]{:S(2)}) collective-permute-start(bf16[2,64,1024]{2,1,0:T(8,128)(2,1)S(1)} %get-tuple-element.69), channel_id=1, source_target_pairs={{0,32},{8,40},{16,48},{24,56},{32,64},{40,72},{48,80},{56,88},{64,... | collective-permute-start | bytes 786440 | tf_op jit(solution)/shard_map/ppermute | solution.py:368
  74.5 11.9 %collective-permute-start.11 = (bf16[128,2048]{1,0:T(8,128)(2,1)S(1)}, bf16[128,2048]{1,0:T(8,128)(2,1)S(1)}, u32[]{:S(2)}, u32[]{:S(2)}) collective-permute-start(bf16[128,2048]{1,0:T(8,128)(2,1)S(1)} %fusion.4), channel_id=1, source_target_pairs={{0,96},{8,104},{16,112},{24,120},{32,0},{40,8},{48,16},{56,24},{64... | collective-permute-start | bytes 1572872 | tf_op jit(solution)/shard_map/ppermute | solution.py:375
  75.2 11.5 %collective-permute-start.13 = (bf16[128,2048]{1,0:T(8,128)(2,1)S(1)}, bf16[128,2048]{1,0:T(8,128)(2,1)S(1)}, u32[]{:S(2)}, u32[]{:S(2)}) collective-permute-start(bf16[128,2048]{1,0:T(8,128)(2,1)S(1)} %fusion), channel_id=1, source_target_pairs={{0,16},{8,24},{16,0},{24,8},{32,48},{40,56},{48,32},{56,40},{64,80... | collective-permute-start | bytes 1572872 | tf_op jit(solution)/shard_map/ppermute | solution.py:390
  78.4 19.4 %copy-start.7 = (f32[128]{0:T(128)S(1)}, f32[128]{0:T(128)}, u32[]{:S(2)}) copy-start(f32[128]{0:T(128)} %param.16) | copy-start | bytes 1540
  78.4 19.4 %copy-start.8 = (f32[128]{0:T(128)S(1)}, f32[128]{0:T(128)}, u32[]{:S(2)}) copy-start(f32[128]{0:T(128)} %param.18) | copy-start | bytes 1540
  78.4 19.4 %copy-start.9 = (f32[64]{0:T(128)S(1)}, f32[64]{0:T(128)}, u32[]{:S(2)}) copy-start(f32[64]{0:T(128)} %param.20) | copy-start | bytes 772
  78.5 13.1 %collective-permute-start.18 = (bf16[64,1024]{1,0:T(8,128)(2,1)S(1)}, bf16[64,1024]{1,0:T(8,128)(2,1)S(1)}, u32[]{:S(2)}, u32[]{:S(2)}) collective-permute-start(bf16[64,1024]{1,0:T(8,128)(2,1)S(1)} %get-tuple-element.90), channel_id=1, source_target_pairs={{0,96},{8,104},{16,112},{24,120},{32,0},{40,8},{48,16},{56,24},{64... | collective-permute-start | bytes 393224 | tf_op jit(solution)/shard_map/ppermute | solution.py:375
  78.9 12.6 %collective-permute-start.17 = (bf16[64,1024]{1,0:T(8,128)(2,1)S(1)}, bf16[64,1024]{1,0:T(8,128)(2,1)S(1)}, u32[]{:S(2)}, u32[]{:S(2)}) collective-permute-start(bf16[64,1024]{1,0:T(8,128)(2,1)S(1)} %get-tuple-element.91), channel_id=1, source_target_pairs={{0,32},{8,40},{16,48},{24,56},{32,64},{40,72},{48,80},{56,88},{64,... | collective-permute-start | bytes 393224 | tf_op jit(solution)/shard_map/ppermute | solution.py:375
  80.8 36.3 %copy-start.3 = (bf16[768,256]{1,0:T(8,128)(2,1)}, bf16[768,256]{1,0:T(8,128)(2,1)S(1)}, u32[]{:S(2)}) copy-start(bf16[768,256]{1,0:T(8,128)(2,1)S(1)} %fusion.3.refs_4_) | copy-start | bytes 1179652
  80.8 36.3 %copy-start.5 = (f32[1024]{0:T(1024)S(1)}, f32[1024]{0:T(1024)}, u32[]{:S(2)}) copy-start(f32[1024]{0:T(1024)} %param.17) | copy-start | bytes 12292
  80.8 36.3 %copy-start.6 = (f32[1024]{0:T(1024)S(1)}, f32[1024]{0:T(1024)}, u32[]{:S(2)}) copy-start(f32[1024]{0:T(1024)} %param.19) | copy-start | bytes 12292
  80.8 46.1 %copy-start.4 = (f32[2048]{0:T(1024)S(1)}, f32[2048]{0:T(1024)}, u32[]{:S(2)}) copy-start(f32[2048]{0:T(1024)} %param.21) | copy-start | bytes 24580
  87.8 10.0 %all-to-all-start = ((f32[8,8,128]{2,1,0:T(8,128)}), f32[8,8,128]{2,1,0:T(8,128)S(1)}, u32[]{:S(2)}, u32[]{:S(2)}) async-start(f32[8,8,128]{2,1,0:T(8,128)} %get-tuple-element.71), calls=%async_computation | async-start | bytes 65536 | tf_op jit(solution)/shard_map/all_to_all | solution.py:402

commit v2 on v1

--- a/solution.py
+++ b/solution.py
@@ -25,6 +25,10 @@
                 to = ((z + dz) % 4) * 4 + (x ^ dx) * 2 + (c ^ dc)
                 pairs.append((z * 4 + x * 2 + c, to))
     return pairs
+
+
+def dp_pairs(flip):
+    return [(k, (((k // 4) ^ flip) * 4) + k % 4) for k in range(16)]
 
 
 def mp_shift(dy=0, dx=0):
@@ -64,43 +68,44 @@
     return pltpu.VMEM(shape, dtype)
 
 
-def gate_kernel(tok_in, wg_in, gate, tok, wg, tok_sem, wg_sem):
+def gate_kernel(idx, tok_in, wg_in, gate, tok, wg, tok_sem, wg_sem):
     rows = [pl.ds(m * 256, 256) for m in range(3)]
-    cols = [pl.ds(n * 256, 256) for n in range(4)]
+    deep = [pl.ds(n * 256, 256) for n in range(8)]
+    wg_copy = [pltpu.make_async_copy(wg_in.at[d, :], wg.at[d, :], wg_sem.at[n])
+               for n, d in enumerate(deep)]
     tok_copy = [pltpu.make_async_copy(tok_in.at[r, :], tok.at[r, :], tok_sem.at[m])
                 for m, r in enumerate(rows)]
-    wg_copy = [pltpu.make_async_copy(wg_in.at[:, c], wg.at[:, c], wg_sem.at[n])
-               for n, c in enumerate(cols)]
-    for copy in (tok_copy[0], wg_copy[0], tok_copy[1], tok_copy[2], *wg_copy[1:]):
+    for copy in (tok_copy[0], *wg_copy, *tok_copy[1:]):
         copy.start()
-    for n, c in enumerate(cols):
-        wg_copy[n].wait()
-        for m, r in enumerate(rows):
-            if n == 0:
-                tok_copy[m].wait()
+    for copy in wg_copy:
+        copy.wait()
+    for m, r in enumerate(rows):
+        tok_copy[m].wait()
+        for n in range(2):
+            c = pl.ds(n * 512, 512)
             gate[r, c] = contract(tok[r, :], wg[:, c], 1, 0)
 
 
-def gate_pre(tokens, w_gate):
+def gate_pre(idx, tokens, w_gate):
     vmem, hbm = pl.BlockSpec(memory_space=pltpu.VMEM), pl.BlockSpec(memory_space=pltpu.HBM)
     rows, width = tokens.shape
     units = w_gate.shape[1]
     return pl.pallas_call(
         gate_kernel,
-        in_specs=[hbm, hbm],
+        in_specs=[pl.BlockSpec(memory_space=pltpu.SMEM), hbm, hbm],
         out_specs=[vmem] * 3,
         out_shape=[near((rows, units), F32), near(tokens.shape, BF), near(w_gate.shape, BF)],
-        scratch_shapes=[pltpu.SemaphoreType.DMA((3,)), pltpu.SemaphoreType.DMA((4,))],
+        scratch_shapes=[pltpu.SemaphoreType.DMA((3,)), pltpu.SemaphoreType.DMA((8,))],
         compiler_params=pltpu.CompilerParams(vmem_limit_bytes=4 * MIB),
         cost_estimate=pl.CostEstimate(flops=1000000, bytes_accessed=1024, transcendentals=0),
         name="gate_pre",
-    )(*[pltpu.with_memory_space_constraint(a, pltpu.HBM) for a in (tokens, w_gate)])
+    )(idx, *[pltpu.with_memory_space_constraint(a, pltpu.HBM) for a in (tokens, w_gate)])
 
 
 def up_kernel(idx, tok, wu, gate, act_out, slope_out, h_own, h_send):
     z, xh, core = idx[0], idx[1], idx[2]
-    for r in range(4):
-        cols = pl.ds(pl.multiple_of(lax.rem(z + r, 4) * 256, 256), 256)
+    for r, far in enumerate((2, 1, 3, 0)):
+        cols = pl.ds(pl.multiple_of(lax.bitwise_xor(z, far) * 256, 256), 256)
         pre = gate[:, cols]
         up = contract(tok[...], wu[:, cols], 1, 0)
         sig = 1.0 / (1.0 + jnp.exp(-pre))
@@ -165,18 +170,10 @@
             out[k] = term.astype(BF)
 
 
-def mix_kernel(own, got, right, left, mid, keep):
-    for r, rows in ((2, 0), (1, 64), (3, 128), (0, 192)):
-        at = pl.ds(((r) % 4) * 64, 64)
-        for side in range(2):
-            cols = pl.ds(side * 1024, 1024)
-            total = (own[at, cols].astype(F32) + got[at, cols].astype(F32)).astype(BF)
-            for place, first, second in ((right, (2, 0), (1, 1)), (left, (2, 1), (3, 0)),
-                                         (mid, (1, 0), (3, 1)), (keep, (0, 0), (0, 1))):
-                if (r, side) == first:
-                    place[0] = total
-                if (r, side) == second:
-                    place[1] = total
+def mix_kernel(own, got, send, keep):
+    half = send.shape[0]
+    send[...] = add(own[:half, :], got[:half, :]).astype(BF)
+    keep[...] = add(own[half:, :], got[half:, :]).astype(BF)
 
 
 def add(*terms):
@@ -184,6 +181,25 @@
     for term in terms[1:]:
         total = total + term.astype(F32)
     return total
+
+
+def middle_kernel(one, two, from_left, from_right, onward, backward):
+    onward[...] = add(one[0], from_left[0]).astype(BF)
+    backward[...] = add(two[0], from_right[0]).astype(BF)
+
+
+def crossing_kernel(keep, got, end, out):
+    out[...] = add(keep[1], got[1], end[...]).astype(BF)
+
+
+def down_middle_kernel(keep, got, out):
+    size = out.shape[0]
+    out[...] = add(keep[:size, :], got[:size, :]).astype(BF)
+
+
+def token_end_kernel(keep, got, end, last, out, ended):
+    ended[...] = jnp.zeros_like(ended)
+    out[...] = add(keep[1], got[1], end[...], last[...]).astype(BF)
 
 
 def moment_step(old_value, column_total, count):
@@ -215,13 +231,12 @@
 
 
 def columns_kernel(
-    counts, g_gate, g_up, keep, left, right, end_a, end_b, rows, row_gate, row_up, row_down,
+    counts, g_gate, g_up, keep, near_one, end, rows, row_gate, row_up, row_down,
     g_down, gate_new, up_new, down_new, pay, gate_out, up_out, down_out, work,
 ):
     all_units, width = counts
-    half = end_a.shape[1]
-    g_down[:, :half] = add(keep[0], left[1], end_a[...])
-    g_down[:, half:] = add(keep[1], right[1], end_b[...])
+    size = g_down.shape[0]
+    g_down[...] = add(keep[size:, :], near_one[size:, :], end[...])
     total = rows[0]
     for k in range(1, rows.shape[0]):
         total = total + rows[k]
@@ -242,13 +257,20 @@
             work[pl.ds(at + k, 1), :] = jnp.sum(square, axis=0, keepdims=True)
             work[pl.ds(at + blocks + k, 1), :] = jnp.sum(square * scale, axis=0, keepdims=True)
         at += 2 * blocks
-    for k, new in enumerate((gate_new, up_new, down_new)):
-        work[pl.ds(at + k, 1), :] = jnp.broadcast_to(
-            jnp.sum(new[...], axis=1, keepdims=True), (1, 128)
-        )
-    work[pl.ds(at + 3, 5), :] = jnp.zeros((5, 128), F32)
+    sums = jnp.concatenate(
+        [
+            jnp.broadcast_to(jnp.sum(new[...], axis=1, keepdims=True), (1, 128))
+            for new in (gate_new, up_new, down_new)
+        ]
+        + [jnp.zeros((5, 128), F32)],
+        axis=0,
+    )
+    high = sums.astype(BF).astype(F32)
+    work[64:72, :] = high
+    work[72:80, :] = sums - high
+    block = work[...].astype(BF)
     for k in range(pay.shape[0]):
-        pay[k] = work[...]
+        pay[k] = block
 
 
 def spread(value):
@@ -258,23 +280,22 @@
 
 
 def partial_kernel(width, got, col_gate, col_up, gate_new, up_new, sums, pay, gate_out, up_out):
-    total = got[0]
-    for k in range(1, got.shape[0]):
-        total = total + got[k]
+    total = add(*[got[k] for k in range(got.shape[0])])
+    row_sums = total[64:72] + total[72:80]
     gate = moment_step(col_gate[...], total[0:8], width)
     up = moment_step(col_up[...], total[16:24], width)
     gate_new[...] = gate
     up_new[...] = up
     gate_out[...] = gate
     up_out[...] = up
-    sums[...] = total[64:72]
+    sums[...] = row_sums
     for k in range(pay.shape[0]):
         pay[k, 0:32, :] = total[32:64]
         pay[k, 32:40, :] = jnp.concatenate(
             [
                 spread(total[8:16] / gate),
                 spread(total[24:32] / up),
-                total[66:67],
+                row_sums[2:3],
                 jnp.zeros((5, 128), F32),
             ],
             axis=0,
@@ -320,10 +341,10 @@
     y_forth, y_back, x_across = mp_shift(dy=1), mp_shift(dy=3), mp_shift(dx=1)
     one = 2 * rows * width * units
 
-    tok_peer = lax.ppermute(tokens, "dp", swap)
     cot_peer = lax.ppermute(cotangent, "dp", swap)
     square = near((rows, units), F32)
-    gate, tokens, w_gate = gate_pre(tokens, w_gate)
+    gate, tokens, w_gate = gate_pre(idx, tokens, w_gate)
+    tok_peer = lax.ppermute(tokens, "dp", swap)
     hid = near((2, units // 4, rows), BF)
     act, slope, h_own, h_send = local_kernel(
         "up_pre", up_kernel, idx, [tokens, w_up, gate], [square, square, hid, hid], one
@@ -364,40 +385,48 @@
     tok_a, tok_b = token_part(SECOND, (pair_a,))
     own = down_part(1, (tok_a,))
 
-    def ring_first(axis, pairs, right, left, mid_a, mid_b):
-        from_left = lax.ppermute(right, axis, pairs[0])
-        from_right = lax.ppermute(left, axis, pairs[1])
-        onward = add(mid_a, from_left[0]).astype(BF)
-        backward = add(mid_b, from_right[0]).astype(BF)
-        return onward, backward, from_left, from_right
-
-    def ring_second(axis, pairs, onward, backward):
-        return lax.ppermute(onward, axis, pairs[0]), lax.ppermute(backward, axis, pairs[1])
-
-    ring, y_ring = (forth, back), (y_forth, y_back)
-    pair_mid = ring_first("dp", ring, pair_r, pair_l, pair_a[0], pair_b[0])
-    pair_end = ring_second("dp", ring, *pair_mid[:2])
-    part = near((2, units // 16, width // 2), BF)
-    down_r, down_l, down_m, down_k = local_kernel(
-        "down_mix", mix_kernel, None, [own, lax.ppermute(away, "dp", across)], [part] * 4, 1000
-    )
-    down_mid = ring_first("dp", ring, down_r, down_l, down_m[0], down_m[1])
-    down_end = ring_second("dp", ring, *down_mid[:2])
-    tok_mid = ring_first("mp", y_ring, tok_r, tok_l, tok_a[0], tok_b[0])
-    tok_end = ring_second("mp", y_ring, *tok_mid[:2])
-
-    def cross(keep, mid, end, axis, pairs):
-        return lax.ppermute(add(keep[1], mid[3][1], end[0]).astype(BF), axis, pairs)
-
-    pair_got = cross(pair_a, pair_mid, pair_end, "dp", across)
-    tok_got = cross(tok_a, tok_mid, tok_end, "mp", x_across)
-    token_grad = add(tok_b[1], tok_mid[2][1], tok_end[1], tok_got).astype(BF)
+    def middle(parts, got, after):
+        out = near(parts[0].shape[1:], BF)
+        return local_kernel("middle", middle_kernel, None, [*parts, *got], [out, out], 1000,
+                            after=after)
+
+    def crossing(keep, got, end, after):
+        out = near(end.shape, BF)
+        return local_kernel("crossing", crossing_kernel, None, [keep, got, end], [out], 1000,
+                            after=after)[0]
+
+    tok_got = lax.ppermute(tok_r, "mp", y_forth), lax.ppermute(tok_l, "mp", y_back)
+    tok_mid = middle((tok_a, tok_b), tok_got, (own,))
+    tok_end = lax.ppermute(tok_mid[0], "mp", y_forth), lax.ppermute(tok_mid[1], "mp", y_back)
+    pair_got = lax.ppermute(pair_r, "dp", forth), lax.ppermute(pair_l, "dp", back)
+    pair_mid = middle((pair_a, pair_b), pair_got, (tok_mid[0],))
+    pair_end = lax.ppermute(pair_mid[0], "dp", forth), lax.ppermute(pair_mid[1], "dp", back)
+    tok_away = crossing(tok_a, tok_got[1], tok_end[0], (pair_mid[0], tok_end[1]))
+    tok_last = lax.ppermute(tok_away, "mp", x_across)
+    part = near((units // 8, width), BF)
+    down_away, down_keep = local_kernel(
+        "down_mix", mix_kernel, None, [own, lax.ppermute(away, "dp", across)], [part] * 2, 1000,
+        after=(tok_away,),
+    )
+    down_got = lax.ppermute(down_away, "dp", dp_pairs(1))
+    pair_away = crossing(pair_a, pair_got[1], pair_end[0], (down_away, pair_end[1], tok_last))
+    pair_last = lax.ppermute(pair_away, "dp", across)
+    (down_mid,) = local_kernel(
+        "down_middle", down_middle_kernel, None, [down_keep, down_got],
+        [near((units // 16, width), BF)], 1000, after=(pair_away,),
+    )
+    down_end = lax.ppermute(down_mid, "dp", dp_pairs(3))
+    token_grad, tok_ended = local_kernel(
+        "token_end", token_end_kernel, None, [tok_b, tok_got[0], tok_end[1], tok_last],
+        [jax.ShapeDtypeStruct((rows, width // 8), BF), near((8, 128), F32)], 1000,
+        after=(down_mid,),
+    )
 
     shard = near((width // 16, units), F32)
     g_gate, g_up, pay = local_kernel(
         "row_sums", rows_kernel, None,
-        [pair_b, pair_mid[2], pair_end[1], pair_got],
-        [shard, shard, near((8, 8, 128), F32)], 1000, after=(token_grad,), limit=4,
+        [pair_b, pair_got[0], pair_end[1], pair_last],
+        [shard, shard, near((8, 8, 128), F32)], 1000, after=(tok_ended,), limit=4,
     )
     row_got = lax.all_to_all(pay, "mp", 0, 0, tiled=True)
 
@@ -409,11 +438,11 @@
     g_down, row_gate_new, row_up_new, row_down_new, pay, *rows_out, _ = local_kernel(
         "column_sums", functools.partial(columns_kernel, counts), None,
         [
-            g_gate, g_up, down_k, down_mid[3], down_mid[2], *down_end, row_got,
+            g_gate, g_up, down_keep, down_got, down_end, row_got,
             row_gate.reshape(1, -1), row_up.reshape(1, -1), row_down.reshape(1, -1),
         ],
-        [near((units // 16, width), F32), line, line, short, near((16, 72, 128), F32),
-         line_out, line_out, short_out, near((72, 128), F32)],
+        [near((units // 16, width), F32), line, line, short, near((16, 80, 128), BF),
+         line_out, line_out, short_out, near((80, 128), F32)],
         1000, limit=4,
     )
     col_got = lax.all_to_all(pay, "dp", 0, 0, tiled=True)

time: 129 us -> 127 us (0.984)
  waiting for transfers between devices: 28.4 us -> 33 us
  blocking collectives: 27.4 us -> 24.3 us
    ppermute x14 -> x12, waiting for transfers between devices: 22.1 us -> 26.7 us  [the longest x1 8 us: body(): tok_last = lax.ppermute(tok_away, 'mp', x_across)]
    all_to_all x1, blocking collectives: 18.2 us -> 15.1 us  [body(): col_got = lax.all_to_all(pay, 'dp', 0, 0, tiled=True)]
    ppermute x14 -> x12, starting transfers between devices: 19.5 us -> 17.3 us  [the longest x1 4.1 us: body(): lax.ppermute(pair_l, 'dp', back)]
    pallas_call x13 -> x19, Pallas kernels: 35.2 us -> 34.4 us  [local_kernel(): pl.pallas_call(run, in_specs=specs + [vmem] * count + [pl.BlockSpec(memor...]
  transfers between devices with their start and end apart: 20 -> 18, of which waited for: 6 -> 8; matrix products, arithmetic and copies ran while one was open for 1% -> 0% of each run, Pallas kernels for 28% -> 28%
where the time goes in v2:
time: 127 us
  Pallas kernels  41.8 us (33%)
  waiting for transfers between devices  33 us (26%)
  starting transfers between devices  26.5 us (21%)
  blocking collectives  24.3 us (19%)
    pallas_call x19, Pallas kernels, local_kernel(): pl.pallas_call(run, in_specs=specs + [vmem] * count + [pl.BlockSpec(memor...  34.4 us
    all_to_all x1, blocking collectives, body(): col_got = lax.all_to_all(pay, 'dp', 0, 0, tiled=True)  15.1 us
    all_to_all x1, blocking collectives, body(): last = lax.all_to_all(pay, 'mp', 0, 0, tiled=True)  9.21 us
    ppermute x1, waiting for transfers between devices, body(): tok_last = lax.ppermute(tok_away, 'mp', x_across)  8 us
    pallas_call x1, Pallas kernels, gate_pre(): pl.pallas_call(gate_kernel, in_specs=[pl.BlockSpec(memory_space=pltpu.SME...  7.42 us
    all_to_all x1, waiting for transfers between devices, body(): row_got = lax.all_to_all(pay, 'mp', 0, 0, tiled=True)  6.25 us
    ppermute x1, waiting for transfers between devices, body(): down_got = lax.ppermute(down_away, 'dp', dp_pairs(1))  5.66 us
    all_to_all x1, starting transfers between devices, body(): row_got = lax.all_to_all(pay, 'mp', 0, 0, tiled=True)  4.53 us
  transfers between devices with their start and end apart: 18, of which 8 were waited for; matrix products, arithmetic and copies ran while one was open for 0% of the time, Pallas kernels for 28%

profile of v2, /device:TPU:0, one launch (start us, length us, event | category | flops | bytes accessed | tf_op | source)
XLA Modules:
  0.0 126.6 jit_solution(619381953166651035)
XLA Ops:
  0.6 0.1 collective-permute-start.1
  0.8 0.1 stack.23.idx.refs_0_
  0.9 7.4 %gate_pre.1 = (f32[768,1024]{1,0:T(8,128)S(1)}, bf16[768,2048]{1,0:T(8,128)(2,1)S(1)}, bf16[2048,1024]{1,0:T(8,128)(2,1)S(1)}) custom-call(s32[5]{0:T(128)S(1)} %stack.23.idx.refs_0_, bf16[768,2048]{1,0:T(8,128)(2,1)} %tok_in.1, bf16[2048,1024]{1,0:T(8,128)(2,1)} %wg_in.1), custom_call_target="tpu_custom_call" | custom-call | flops 1000000 | bytes 1024 | tf_op jit(solution)/shard_map/gate_pre/pallas_call | solution.py:93
  8.3 0.5 collective-permute-start
  8.8 5.3 %up_pre.1 = (f32[768,1024]{1,0:T(8,128)S(1)}, f32[768,1024]{1,0:T(8,128)S(1)}, bf16[2,256,768]{2,1,0:T(8,128)(2,1)S(1)}, bf16[2,256,768]{2,1,0:T(8,128)(2,1)S(1)}) custom-call(s32[5]{0:T(128)S(1)} %stack.23.idx.refs_0_, bf16[768,2048]{1,0:T(8,128)(2,1)S(1)} %get-tuple-element.54.refs_1_, bf16[2048,1024]{1,0:T(8,128)(2,1)S(1)} %copy-done, ...), custom_call_target="tpu_custom_call" | custom-call | flops 201326592 | bytes 1024 | tf_op jit(solution)/shard_map/up_pre/pallas_call | solution.py:52
  14.2 3.5 %hidden_grad.1.refs_1_.refs_3_ = bf16[2,768,1024]{2,1,0:T(8,128)(2,1)S(1)} custom-call(bf16[768,2048]{1,0:T(8,128)(2,1)S(1)} %copy-done.1, bf16[1024,2048]{1,0:T(8,128)(2,1)S(1)} %copy-done.2, f32[768,1024]{1,0:T(8,128)S(1)} %get-tuple-element.56.refs_2_, f32[768,1024]{1,0:T(8,128)S(1)} %get-tuple-element.57.refs_3_, ...), custom_call_target="tpu_custom_call" | custom-call | flops 201326592 | bytes 1024 | tf_op jit(solution)/shard_map/hidden_grad/pallas_call | solution.py:52
  17.6 0.4 collective-permute-start.2
  18.0 0.3 collective-permute-start.3
  18.3 4.0 %token_grad.2 = (bf16[2,768,256]{2,1,0:T(8,128)(2,1)S(1)}, bf16[2,768,256]{2,1,0:T(8,128)(2,1)S(1)}) custom-call(s32[5]{0:T(128)S(1)} %stack.23.idx.refs_0_, bf16[2,768,1024]{2,1,0:T(8,128)(2,1)S(1)} %hidden_grad.1.refs_1_.refs_3_, bf16[2048,1024]{1,0:T(8,128)(2,1)S(1)} %get-tuple-element.58.refs_2_, bf16[2048,1024]{1,0:T(8,128)(2,1)S(1)} %copy-done), custom_call_target="tpu_custom_call" | custom-call | flops 201326592 | bytes 1024 | tf_op jit(solution)/shard_map/token_grad/pallas_call | solution.py:52
  22.3 3.2 %collective-permute-start.5 = (bf16[2,768,256]{2,1,0:T(8,128)(2,1)S(1)}, bf16[2,768,256]{2,1,0:T(8,128)(2,1)S(1)}, u32[]{:S(2)}, u32[]{:S(2)}) collective-permute-start(bf16[2,768,256]{2,1,0:T(8,128)(2,1)S(1)} %get-tuple-element.66), channel_id=1, source_target_pairs={{0,6},{1,7},{2,0},{3,1},{4,2},{5,3},{6,4},{7,5},{8,14},{9,15},{10,... | collective-permute-start | bytes 2359304 | tf_op jit(solution)/shard_map/ppermute | solution.py:398
  25.5 4.0 %weight.2 = (bf16[2,128,2048]{2,1,0:T(8,128)(2,1)S(1)}, bf16[2,128,2048]{2,1,0:T(8,128)(2,1)S(1)}) custom-call(s32[5]{0:T(128)S(1)} %stack.23.idx.refs_0_, bf16[768,2048]{1,0:T(8,128)(2,1)S(1)} %get-tuple-element.54.refs_1_, bf16[768,2048]{1,0:T(8,128)(2,1)S(1)} %collective-permute-done.refs_4_.refs_2_, ...), custom_call_target="tpu_custom_call" | custom-call | flops 201326592 | bytes 1024 | tf_op jit(solution)/shard_map/weight/pallas_call | solution.py:52
  29.5 4.1 %collective-permute-start.9 = (bf16[2,128,2048]{2,1,0:T(8,128)(2,1)S(1)}, bf16[2,128,2048]{2,1,0:T(8,128)(2,1)S(1)}, u32[]{:S(2)}, u32[]{:S(2)}) collective-permute-start(bf16[2,128,2048]{2,1,0:T(8,128)(2,1)S(1)} %get-tuple-element.70), channel_id=1, source_target_pairs={{0,96},{8,104},{16,112},{24,120},{32,0},{40,8},{48,16},{56,24},{64... | collective-permute-start | bytes 3145736 | tf_op jit(solution)/shard_map/ppermute | solution.py:401
  33.6 1.8 %down.2.refs_5_ = bf16[256,2048]{1,0:T(8,128)(2,1)S(1)} custom-call(bf16[2,256,768]{2,1,0:T(8,128)(2,1)S(1)} %get-tuple-element.59.refs_0_, bf16[2,256,768]{2,1,0:T(8,128)(2,1)S(1)} %collective-permute-done.3.refs_1_, bf16[768,2048]{1,0:T(8,128)(2,1)S(1)} %copy-done.1, bf16[768,2048]{1,0:T(8,128)(2,1)S(1)} %collective-permute-done.1.refs_5_.refs_3_, ...), custom_call_target="tpu_custom_call" | custom-call | flops 100663296 | bytes 1024 | tf_op jit(solution)/shard_map/down/pallas_call | solution.py:52
  35.5 3.3 %collective-permute-start.11 = (bf16[256,2048]{1,0:T(8,128)(2,1)S(1)}, bf16[256,2048]{1,0:T(8,128)(2,1)S(1)}, u32[]{:S(2)}, u32[]{:S(2)}) collective-permute-start(bf16[256,2048]{1,0:T(8,128)(2,1)S(1)} %down.2.refs_5_), channel_id=1, source_target_pairs={{0,16},{8,24},{16,0},{24,8},{32,48},{40,56},{48,32},{56,40},{64,80... | collective-permute-start | bytes 3145736 | tf_op jit(solution)/shard_map/ppermute | solution.py:408
  38.8 4.0 %weight.3 = (bf16[2,128,2048]{2,1,0:T(8,128)(2,1)S(1)}, bf16[2,128,2048]{2,1,0:T(8,128)(2,1)S(1)}) custom-call(s32[5]{0:T(128)S(1)} %stack.23.idx.refs_0_, bf16[768,2048]{1,0:T(8,128)(2,1)S(1)} %get-tuple-element.54.refs_1_, bf16[768,2048]{1,0:T(8,128)(2,1)S(1)} %collective-permute-done.refs_4_.refs_2_, ...), custom_call_target="tpu_custom_call" | custom-call | flops 201326592 | bytes 1024 | tf_op jit(solution)/shard_map/weight/pallas_call | solution.py:52
  42.8 4.0 %token_grad.3 = (bf16[2,768,256]{2,1,0:T(8,128)(2,1)S(1)}, bf16[2,768,256]{2,1,0:T(8,128)(2,1)S(1)}) custom-call(s32[5]{0:T(128)S(1)} %stack.23.idx.refs_0_, bf16[2,768,1024]{2,1,0:T(8,128)(2,1)S(1)} %hidden_grad.1.refs_1_.refs_3_, bf16[2048,1024]{1,0:T(8,128)(2,1)S(1)} %get-tuple-element.58.refs_2_, bf16[2048,1024]{1,0:T(8,128)(2,1)S(1)} %copy-done, ...), custom_call_target="tpu_custom_call" | custom-call | flops 201326592 | bytes 1024 | tf_op jit(solution)/shard_map/token_grad/pallas_call | solution.py:52
  46.8 1.8 %down.3.refs_4_.refs_0_ = bf16[256,2048]{1,0:T(8,128)(2,1)S(1)} custom-call(bf16[2,256,768]{2,1,0:T(8,128)(2,1)S(1)} %get-tuple-element.59.refs_0_, bf16[2,256,768]{2,1,0:T(8,128)(2,1)S(1)} %collective-permute-done.3.refs_1_, bf16[768,2048]{1,0:T(8,128)(2,1)S(1)} %copy-done.1, bf16[768,2048]{1,0:T(8,128)(2,1)S(1)} %collective-permute-done.1.refs_5_.refs_3_, ...), custom_call_target="tpu_custom_call" | custom-call | flops 100663296 | bytes 1024 | tf_op jit(solution)/shard_map/down/pallas_call | solution.py:52
  48.7 0.2 middle.2
  48.9 3.3 %collective-permute-start.6 = (bf16[768,256]{1,0:T(8,128)(2,1)S(1)}, bf16[768,256]{1,0:T(8,128)(2,1)S(1)}, u32[]{:S(2)}, u32[]{:S(2)}) collective-permute-start(bf16[768,256]{1,0:T(8,128)(2,1)S(1)} %get-tuple-element.67), channel_id=1, source_target_pairs={{0,6},{1,7},{2,0},{3,1},{4,2},{5,3},{6,4},{7,5},{8,14},{9,15},{10,... | collective-permute-start | bytes 1179656 | tf_op jit(solution)/shard_map/ppermute | solution.py:400
  52.2 4.0 %collective-permute-done.9.refs_3_.refs_1_ = bf16[2,128,2048]{2,1,0:T(8,128)(2,1)S(1)} collective-permute-done((bf16[2,128,2048]{2,1,0:T(8,128)(2,1)S(1)}, bf16[2,128,2048]{2,1,0:T(8,128)(2,1)S(1)}, u32[]{:S(2)}, u32[]{:S(2)}) %collective-permute-start.9) | collective-permute-done | bytes 1048608 | tf_op jit(solution)/shard_map/ppermute | solution.py:401
  56.2 3.4 %collective-permute-done.8.refs_2_.refs_1_ = bf16[2,128,2048]{2,1,0:T(8,128)(2,1)S(1)} collective-permute-done((bf16[2,128,2048]{2,1,0:T(8,128)(2,1)S(1)}, bf16[2,128,2048]{2,1,0:T(8,128)(2,1)S(1)}, u32[]{:S(2)}, u32[]{:S(2)}) %collective-permute-start.8) | collective-permute-done | bytes 1048608 | tf_op jit(solution)/shard_map/ppermute | solution.py:401
  59.6 0.2 middle.3
  59.8 0.4 collective-permute-start.14
  60.2 1.7 %collective-permute-start.13 = (bf16[128,2048]{1,0:T(8,128)(2,1)S(1)}, bf16[128,2048]{1,0:T(8,128)(2,1)S(1)}, u32[]{:S(2)}, u32[]{:S(2)}) collective-permute-start(bf16[128,2048]{1,0:T(8,128)(2,1)S(1)} %get-tuple-element.71.refs_3_), channel_id=1, source_target_pairs={{0,32},{8,40},{16,48},{24,56},{32,64},{40,72},{48,80},{56,88},{64,... | collective-permute-start | bytes 1572872 | tf_op jit(solution)/shard_map/ppermute | solution.py:403
  61.9 1.3 %collective-permute-done.7.refs_2_ = bf16[768,256]{1,0:T(8,128)(2,1)S(1)} collective-permute-done((bf16[768,256]{1,0:T(8,128)(2,1)S(1)}, bf16[768,256]{1,0:T(8,128)(2,1)S(1)}, u32[]{:S(2)}, u32[]{:S(2)}) %collective-permute-start.7) | collective-permute-done | bytes 393248 | tf_op jit(solution)/shard_map/ppermute | solution.py:400
  63.3 0.1 crossing.2.refs_2_
  63.4 0.7 collective-permute-start.10
  64.1 0.2 down_mix.1
  64.3 0.1 collective-permute-start.12
  64.4 8.0 %collective-permute-done.10.refs_5_.refs_3_ = bf16[768,256]{1,0:T(8,128)(2,1)S(1)} collective-permute-done((bf16[768,256]{1,0:T(8,128)(2,1)S(1)}, bf16[768,256]{1,0:T(8,128)(2,1)S(1)}, u32[]{:S(2)}, u32[]{:S(2)}) %collective-permute-start.10) | collective-permute-done | bytes 393248 | tf_op jit(solution)/shard_map/ppermute | solution.py:405
  72.4 2.3 %collective-permute-done.14.refs_4_.refs_2_ = bf16[128,2048]{1,0:T(8,128)(2,1)S(1)} collective-permute-done((bf16[128,2048]{1,0:T(8,128)(2,1)S(1)}, bf16[128,2048]{1,0:T(8,128)(2,1)S(1)}, u32[]{:S(2)}, u32[]{:S(2)}) %collective-permute-start.14) | collective-permute-done | bytes 524320 | tf_op jit(solution)/shard_map/ppermute | solution.py:403
  74.7 0.2 crossing.3.refs_2_
  74.9 3.1 %collective-permute-start.15 = (bf16[128,2048]{1,0:T(8,128)(2,1)S(1)}, bf16[128,2048]{1,0:T(8,128)(2,1)S(1)}, u32[]{:S(2)}, u32[]{:S(2)}) collective-permute-start(bf16[128,2048]{1,0:T(8,128)(2,1)S(1)} %crossing.3.refs_2_), channel_id=1, source_target_pairs={{0,16},{8,24},{16,0},{24,8},{32,48},{40,56},{48,32},{56,40},{64,80... | collective-permute-start | bytes 1572872 | tf_op jit(solution)/shard_map/ppermute | solution.py:413
  78.1 5.7 %collective-permute-done.12.refs_1_.refs_3_ = bf16[128,2048]{1,0:T(8,128)(2,1)S(1)} collective-permute-done((bf16[128,2048]{1,0:T(8,128)(2,1)S(1)}, bf16[128,2048]{1,0:T(8,128)(2,1)S(1)}, u32[]{:S(2)}, u32[]{:S(2)}) %collective-permute-start.12) | collective-permute-done | bytes 524320 | tf_op jit(solution)/shard_map/ppermute | solution.py:411
  83.7 0.1 down_middle.1.refs_4_
  83.8 0.0 copy-start.6
  83.8 0.0 copy-start.7
  83.8 0.8 collective-permute-start.16
  84.6 0.9 token_end.1
  85.5 2.0 %collective-permute-done.15.refs_3_ = bf16[128,2048]{1,0:T(8,128)(2,1)S(1)} collective-permute-done((bf16[128,2048]{1,0:T(8,128)(2,1)S(1)}, bf16[128,2048]{1,0:T(8,128)(2,1)S(1)}, u32[]{:S(2)}, u32[]{:S(2)}) %collective-permute-start.15) | collective-permute-done | bytes 524320 | tf_op jit(solution)/shard_map/ppermute | solution.py:413
  87.5 1.0 row_sums.1
  88.5 4.5 %all-to-all-start = ((f32[8,8,128]{2,1,0:T(8,128)}), f32[8,8,128]{2,1,0:T(8,128)S(1)}, u32[]{:S(2)}, u32[]{:S(2)}) async-start(f32[8,8,128]{2,1,0:T(8,128)} %get-tuple-element.79), calls=%async_computation | async-start | bytes 65536 | tf_op jit(solution)/shard_map/all_to_all | solution.py:431
  93.1 6.3 %all-to-all-done.refs_5_ = f32[8,8,128]{2,1,0:T(8,128)S(1)} async-done(((f32[8,8,128]{2,1,0:T(8,128)}), f32[8,8,128]{2,1,0:T(8,128)S(1)}, u32[]{:S(2)}, u32[]{:S(2)}) %all-to-all-start) | async-done | bytes 32800 | tf_op jit(solution)/shard_map/all_to_all | solution.py:431
  99.3 1.1 column_sums.1
  100.4 15.1 %all_to_all.15.refs_0_ = bf16[16,80,128]{2,1,0:T(8,128)(2,1)S(1)} all-to-all(bf16[16,80,128]{2,1,0:T(8,128)(2,1)S(1)} %get-tuple-element.80), channel_id=1, replica_groups=mesh['dp'=16,'mp'=8] {'dp'}, dimensions={0} | all-to-all | bytes 655360 | tf_op jit(solution)/shard_map/all_to_all | solution.py:448
  115.5 0.6 partial_sums.1
  116.1 9.2 %all_to_all.16.refs_0_ = f32[8,40,128]{2,1,0:T(8,128)S(1)} all-to-all(f32[8,40,128]{2,1,0:T(8,128)S(1)} %get-tuple-element.81), channel_id=1, replica_groups=mesh['dp'=16,'mp'=8] {'mp'}, dimensions={0} | all-to-all | bytes 327680 | tf_op jit(solution)/shard_map/all_to_all | solution.py:457
  125.3 1.3 %updates.1 = (f32[128,1024]{1,0:T(8,128)}, f32[128,1024]{1,0:T(8,128)}, f32[64,2048]{1,0:T(8,128)}, f32[16,128]{1,0:T(8,128)}) custom-call(f32[8,40,128]{2,1,0:T(8,128)S(1)} %all_to_all.16.refs_0_, f32[8,128]{1,0:T(8,128)S(1)} %get-tuple-element.82.refs_1_, f32[16,128]{1,0:T(8,128)S(1)} %bitcast.17, f32[128,1024]{1,0:T(8,128)S(1)} %get-tuple-element.77.refs_0_.refs_3_, ...), custom_call_target="tpu_custom_call" | custom-call | flops 62 | bytes 1024 | tf_op jit(solution)/shard_map/updates/pallas_call | solution.py:52
  (29 shorter events, 0.1 us)
Async XLA Ops:
  0.6 13.5 %collective-permute-start.1 = (bf16[768,2048]{1,0:T(8,128)(2,1)}, bf16[768,2048]{1,0:T(8,128)(2,1)S(1)}, u32[]{:S(2)}, u32[]{:S(2)}) collective-permute-start(bf16[768,2048]{1,0:T(8,128)(2,1)} %refs_2_.5), channel_id=1, source_target_pairs={{0,8},{8,0},{16,24},{24,16},{32,40},{40,32},{48,56},{56,48},{64,72... | collective-permute-start | bytes 9437192 | tf_op jit(solution)/shard_map/ppermute | solution.py:344
  0.9 7.9 %copy-start = (bf16[2048,1024]{1,0:T(8,128)(2,1)S(1)}, bf16[2048,1024]{1,0:T(8,128)(2,1)}, u32[]{:S(2)}) copy-start(bf16[2048,1024]{1,0:T(8,128)(2,1)} %refs_3_.3) | copy-start | bytes 12582916
  8.3 5.8 %collective-permute-start = (bf16[768,2048]{1,0:T(8,128)(2,1)S(1)}, bf16[768,2048]{1,0:T(8,128)(2,1)S(1)}, u32[]{:S(2)}, u32[]{:S(2)}) collective-permute-start(bf16[768,2048]{1,0:T(8,128)(2,1)S(1)} %get-tuple-element.54.refs_1_), channel_id=1, source_target_pairs={{0,8},{8,0},{16,24},{24,16},{32,40},{40,32},{48,56},{56,48},{64,72... | collective-permute-start | bytes 9437192 | tf_op jit(solution)/shard_map/ppermute | solution.py:347
  8.8 5.3 %copy-start.1 = (bf16[768,2048]{1,0:T(8,128)(2,1)S(1)}, bf16[768,2048]{1,0:T(8,128)(2,1)}, u32[]{:S(2)}) copy-start(bf16[768,2048]{1,0:T(8,128)(2,1)} %refs_2_.5) | copy-start | bytes 9437188
  8.8 5.3 %copy-start.2 = (bf16[1024,2048]{1,0:T(8,128)(2,1)S(1)}, bf16[1024,2048]{1,0:T(8,128)(2,1)}, u32[]{:S(2)}) copy-start(bf16[1024,2048]{1,0:T(8,128)(2,1)} %refs_1_.1) | copy-start | bytes 12582916
  17.6 7.9 %collective-permute-start.2 = (bf16[2,768,1024]{2,1,0:T(8,128)(2,1)S(1)}, bf16[2,768,1024]{2,1,0:T(8,128)(2,1)S(1)}, u32[]{:S(2)}, u32[]{:S(2)}) collective-permute-start(bf16[2,768,1024]{2,1,0:T(8,128)(2,1)S(1)} %hidden_grad.1.refs_1_.refs_3_), channel_id=1, source_target_pairs={{0,8},{8,0},{16,24},{24,16},{32,40},{40,32},{48,56},{56,48},{64,72... | collective-permute-start | bytes 9437192 | tf_op jit(solution)/shard_map/ppermute | solution.py:358
  18.0 15.6 %collective-permute-start.3 = (bf16[2,256,768]{2,1,0:T(8,128)(2,1)S(1)}, bf16[2,256,768]{2,1,0:T(8,128)(2,1)S(1)}, u32[]{:S(2)}, u32[]{:S(2)}) collective-permute-start(bf16[2,256,768]{2,1,0:T(8,128)(2,1)S(1)} %get-tuple-element.60), channel_id=1, source_target_pairs={{0,8},{8,0},{16,24},{24,16},{32,40},{40,32},{48,56},{56,48},{64,72... | collective-permute-start | bytes 2359304 | tf_op jit(solution)/shard_map/ppermute | solution.py:352
  22.3 26.4 %collective-permute-start.5 = (bf16[2,768,256]{2,1,0:T(8,128)(2,1)S(1)}, bf16[2,768,256]{2,1,0:T(8,128)(2,1)S(1)}, u32[]{:S(2)}, u32[]{:S(2)}) collective-permute-start(bf16[2,768,256]{2,1,0:T(8,128)(2,1)S(1)} %get-tuple-element.66), channel_id=1, source_target_pairs={{0,6},{1,7},{2,0},{3,1},{4,2},{5,3},{6,4},{7,5},{8,14},{9,15},{10,... | collective-permute-start | bytes 2359304 | tf_op jit(solution)/shard_map/ppermute | solution.py:398
  25.5 23.2 %collective-permute-start.4 = (bf16[2,768,256]{2,1,0:T(8,128)(2,1)S(1)}, bf16[2,768,256]{2,1,0:T(8,128)(2,1)S(1)}, u32[]{:S(2)}, u32[]{:S(2)}) collective-permute-start(bf16[2,768,256]{2,1,0:T(8,128)(2,1)S(1)} %get-tuple-element.61.refs_5_), channel_id=1, source_target_pairs={{0,2},{1,3},{2,4},{3,5},{4,6},{5,7},{6,0},{7,1},{8,10},{9,11},{10,... | collective-permute-start | bytes 2359304 | tf_op jit(solution)/shard_map/ppermute | solution.py:398
  29.5 26.6 %collective-permute-start.9 = (bf16[2,128,2048]{2,1,0:T(8,128)(2,1)S(1)}, bf16[2,128,2048]{2,1,0:T(8,128)(2,1)S(1)}, u32[]{:S(2)}, u32[]{:S(2)}) collective-permute-start(bf16[2,128,2048]{2,1,0:T(8,128)(2,1)S(1)} %get-tuple-element.70), channel_id=1, source_target_pairs={{0,96},{8,104},{16,112},{24,120},{32,0},{40,8},{48,16},{56,24},{64... | collective-permute-start | bytes 3145736 | tf_op jit(solution)/shard_map/ppermute | solution.py:401
  33.6 25.9 %collective-permute-start.8 = (bf16[2,128,2048]{2,1,0:T(8,128)(2,1)S(1)}, bf16[2,128,2048]{2,1,0:T(8,128)(2,1)S(1)}, u32[]{:S(2)}, u32[]{:S(2)}) collective-permute-start(bf16[2,128,2048]{2,1,0:T(8,128)(2,1)S(1)} %get-tuple-element.62.refs_4_), channel_id=1, source_target_pairs={{0,32},{8,40},{16,48},{24,56},{32,64},{40,72},{48,80},{56,88},{64,... | collective-permute-start | bytes 3145736 | tf_op jit(solution)/shard_map/ppermute | solution.py:401
  35.5 28.6 %collective-permute-start.11 = (bf16[256,2048]{1,0:T(8,128)(2,1)S(1)}, bf16[256,2048]{1,0:T(8,128)(2,1)S(1)}, u32[]{:S(2)}, u32[]{:S(2)}) collective-permute-start(bf16[256,2048]{1,0:T(8,128)(2,1)S(1)} %down.2.refs_5_), channel_id=1, source_target_pairs={{0,16},{8,24},{16,0},{24,8},{32,48},{40,56},{48,32},{56,40},{64,80... | collective-permute-start | bytes 3145736 | tf_op jit(solution)/shard_map/ppermute | solution.py:408
  48.9 13.0 %collective-permute-start.6 = (bf16[768,256]{1,0:T(8,128)(2,1)S(1)}, bf16[768,256]{1,0:T(8,128)(2,1)S(1)}, u32[]{:S(2)}, u32[]{:S(2)}) collective-permute-start(bf16[768,256]{1,0:T(8,128)(2,1)S(1)} %get-tuple-element.67), channel_id=1, source_target_pairs={{0,6},{1,7},{2,0},{3,1},{4,2},{5,3},{6,4},{7,5},{8,14},{9,15},{10,... | collective-permute-start | bytes 1179656 | tf_op jit(solution)/shard_map/ppermute | solution.py:400
  52.2 11.1 %collective-permute-start.7 = (bf16[768,256]{1,0:T(8,128)(2,1)S(1)}, bf16[768,256]{1,0:T(8,128)(2,1)S(1)}, u32[]{:S(2)}, u32[]{:S(2)}) collective-permute-start(bf16[768,256]{1,0:T(8,128)(2,1)S(1)} %get-tuple-element.68.refs_4_), channel_id=1, source_target_pairs={{0,2},{1,3},{2,4},{3,5},{4,6},{5,7},{6,0},{7,1},{8,10},{9,11},{10,... | collective-permute-start | bytes 1179656 | tf_op jit(solution)/shard_map/ppermute | solution.py:400
  59.8 14.9 %collective-permute-start.14 = (bf16[128,2048]{1,0:T(8,128)(2,1)S(1)}, bf16[128,2048]{1,0:T(8,128)(2,1)S(1)}, u32[]{:S(2)}, u32[]{:S(2)}) collective-permute-start(bf16[128,2048]{1,0:T(8,128)(2,1)S(1)} %get-tuple-element.74), channel_id=1, source_target_pairs={{0,96},{8,104},{16,112},{24,120},{32,0},{40,8},{48,16},{56,24},{64... | collective-permute-start | bytes 1572872 | tf_op jit(solution)/shard_map/ppermute | solution.py:403
  60.2 14.6 %collective-permute-start.13 = (bf16[128,2048]{1,0:T(8,128)(2,1)S(1)}, bf16[128,2048]{1,0:T(8,128)(2,1)S(1)}, u32[]{:S(2)}, u32[]{:S(2)}) collective-permute-start(bf16[128,2048]{1,0:T(8,128)(2,1)S(1)} %get-tuple-element.71.refs_3_), channel_id=1, source_target_pairs={{0,32},{8,40},{16,48},{24,56},{32,64},{40,72},{48,80},{56,88},{64,... | collective-permute-start | bytes 1572872 | tf_op jit(solution)/shard_map/ppermute | solution.py:403
  63.4 9.0 %collective-permute-start.10 = (bf16[768,256]{1,0:T(8,128)(2,1)S(1)}, bf16[768,256]{1,0:T(8,128)(2,1)S(1)}, u32[]{:S(2)}, u32[]{:S(2)}) collective-permute-start(bf16[768,256]{1,0:T(8,128)(2,1)S(1)} %crossing.2.refs_2_), channel_id=1, source_target_pairs={{0,1},{1,0},{2,3},{3,2},{4,5},{5,4},{6,7},{7,6},{8,9},{9,8},{10,11... | collective-permute-start | bytes 1179656 | tf_op jit(solution)/shard_map/ppermute | solution.py:405
  64.3 19.4 %collective-permute-start.12 = (bf16[128,2048]{1,0:T(8,128)(2,1)S(1)}, bf16[128,2048]{1,0:T(8,128)(2,1)S(1)}, u32[]{:S(2)}, u32[]{:S(2)}) collective-permute-start(bf16[128,2048]{1,0:T(8,128)(2,1)S(1)} %get-tuple-element.73.refs_3_), channel_id=1, source_target_pairs={{0,32},{8,40},{16,48},{24,56},{32,0},{40,8},{48,16},{56,24},{64,96... | collective-permute-start | bytes 1572872 | tf_op jit(solution)/shard_map/ppermute | solution.py:411
  74.9 12.6 %collective-permute-start.15 = (bf16[128,2048]{1,0:T(8,128)(2,1)S(1)}, bf16[128,2048]{1,0:T(8,128)(2,1)S(1)}, u32[]{:S(2)}, u32[]{:S(2)}) collective-permute-start(bf16[128,2048]{1,0:T(8,128)(2,1)S(1)} %crossing.3.refs_2_), channel_id=1, source_target_pairs={{0,16},{8,24},{16,0},{24,8},{32,48},{40,56},{48,32},{56,40},{64,80... | collective-permute-start | bytes 1572872 | tf_op jit(solution)/shard_map/ppermute | solution.py:413
  83.8 15.5 %copy-start.6 = (f32[128]{0:T(128)S(1)}, f32[128]{0:T(128)}, u32[]{:S(2)}) copy-start(f32[128]{0:T(128)} %param.16) | copy-start | bytes 1540
  83.8 15.5 %copy-start.7 = (f32[128]{0:T(128)S(1)}, f32[128]{0:T(128)}, u32[]{:S(2)}) copy-start(f32[128]{0:T(128)} %param.18) | copy-start | bytes 1540
  83.8 15.5 %copy-start.8 = (f32[64]{0:T(128)S(1)}, f32[64]{0:T(128)}, u32[]{:S(2)}) copy-start(f32[64]{0:T(128)} %param.20) | copy-start | bytes 772
  83.8 9.2 %collective-permute-start.16 = (bf16[64,2048]{1,0:T(8,128)(2,1)S(1)}, bf16[64,2048]{1,0:T(8,128)(2,1)S(1)}, u32[]{:S(2)}, u32[]{:S(2)}) collective-permute-start(bf16[64,2048]{1,0:T(8,128)(2,1)S(1)} %down_middle.1.refs_4_), channel_id=1, source_target_pairs={{0,96},{8,104},{16,112},{24,120},{32,64},{40,72},{48,80},{56,88},{... | collective-permute-start | bytes 786440 | tf_op jit(solution)/shard_map/ppermute | solution.py:418
  85.5 30.0 %copy-start.4 = (f32[1024]{0:T(1024)S(1)}, f32[1024]{0:T(1024)}, u32[]{:S(2)}) copy-start(f32[1024]{0:T(1024)} %param.17) | copy-start | bytes 12292
  85.5 30.0 %copy-start.5 = (f32[1024]{0:T(1024)S(1)}, f32[1024]{0:T(1024)}, u32[]{:S(2)}) copy-start(f32[1024]{0:T(1024)} %param.19) | copy-start | bytes 12292
  87.5 37.8 %copy-start.3 = (f32[2048]{0:T(1024)S(1)}, f32[2048]{0:T(1024)}, u32[]{:S(2)}) copy-start(f32[2048]{0:T(1024)} %param.21) | copy-start | bytes 24580
  88.5 10.8 %all-to-all-start = ((f32[8,8,128]{2,1,0:T(8,128)}), f32[8,8,128]{2,1,0:T(8,128)S(1)}, u32[]{:S(2)}, u32[]{:S(2)}) async-start(f32[8,8,128]{2,1,0:T(8,128)} %get-tuple-element.79), calls=%async_computation | async-start | bytes 65536 | tf_op jit(solution)/shard_map/all_to_all | solution.py:431

commit v3 on v2

--- a/solution.py
+++ b/solution.py
@@ -68,14 +68,15 @@
     return pltpu.VMEM(shape, dtype)
 
 
-def gate_kernel(idx, tok_in, wg_in, gate, tok, wg, tok_sem, wg_sem):
+def gate_kernel(idx, tok_in, wg_in, wu_in, gate, tok, wg, wu, tok_sem, wg_sem, wu_sem):
     rows = [pl.ds(m * 256, 256) for m in range(3)]
     deep = [pl.ds(n * 256, 256) for n in range(8)]
     wg_copy = [pltpu.make_async_copy(wg_in.at[d, :], wg.at[d, :], wg_sem.at[n])
                for n, d in enumerate(deep)]
     tok_copy = [pltpu.make_async_copy(tok_in.at[r, :], tok.at[r, :], tok_sem.at[m])
                 for m, r in enumerate(rows)]
-    for copy in (tok_copy[0], *wg_copy, *tok_copy[1:]):
+    wu_copy = pltpu.make_async_copy(wu_in, wu, wu_sem)
+    for copy in (tok_copy[0], *wg_copy, *tok_copy[1:], wu_copy):
         copy.start()
     for copy in wg_copy:
         copy.wait()
@@ -84,22 +85,25 @@
         for n in range(2):
             c = pl.ds(n * 512, 512)
             gate[r, c] = contract(tok[r, :], wg[:, c], 1, 0)
-
-
-def gate_pre(idx, tokens, w_gate):
+    wu_copy.wait()
+
+
+def gate_pre(idx, tokens, w_gate, w_up):
     vmem, hbm = pl.BlockSpec(memory_space=pltpu.VMEM), pl.BlockSpec(memory_space=pltpu.HBM)
     rows, width = tokens.shape
     units = w_gate.shape[1]
     return pl.pallas_call(
         gate_kernel,
-        in_specs=[pl.BlockSpec(memory_space=pltpu.SMEM), hbm, hbm],
-        out_specs=[vmem] * 3,
-        out_shape=[near((rows, units), F32), near(tokens.shape, BF), near(w_gate.shape, BF)],
-        scratch_shapes=[pltpu.SemaphoreType.DMA((3,)), pltpu.SemaphoreType.DMA((8,))],
+        in_specs=[pl.BlockSpec(memory_space=pltpu.SMEM), hbm, hbm, hbm],
+        out_specs=[vmem] * 4,
+        out_shape=[near((rows, units), F32), near(tokens.shape, BF), near(w_gate.shape, BF),
+                   near(w_up.shape, BF)],
+        scratch_shapes=[pltpu.SemaphoreType.DMA((3,)), pltpu.SemaphoreType.DMA((8,)),
+                        pltpu.SemaphoreType.DMA],
         compiler_params=pltpu.CompilerParams(vmem_limit_bytes=4 * MIB),
         cost_estimate=pl.CostEstimate(flops=1000000, bytes_accessed=1024, transcendentals=0),
         name="gate_pre",
-    )(idx, *[pltpu.with_memory_space_constraint(a, pltpu.HBM) for a in (tokens, w_gate)])
+    )(idx, *[pltpu.with_memory_space_constraint(a, pltpu.HBM) for a in (tokens, w_gate, w_up)])
 
 
 def up_kernel(idx, tok, wu, gate, act_out, slope_out, h_own, h_send):
@@ -343,7 +347,7 @@
 
     cot_peer = lax.ppermute(cotangent, "dp", swap)
     square = near((rows, units), F32)
-    gate, tokens, w_gate = gate_pre(idx, tokens, w_gate)
+    gate, tokens, w_gate, w_up = gate_pre(idx, tokens, w_gate, w_up)
     tok_peer = lax.ppermute(tokens, "dp", swap)
     hid = near((2, units // 4, rows), BF)
     act, slope, h_own, h_send = local_kernel(

time: 127 us -> 127 us (level)
  no operation moved by 1% of the time
where the time goes in v3:
time: 127 us; the launch traced here: 126 us
  Pallas kernels  41.6 us (33%)
  waiting for transfers between devices  33 us (26%)
  starting transfers between devices  26.5 us (21%)
  blocking collectives  24.3 us (19%)
    pallas_call x19, Pallas kernels, local_kernel(): pl.pallas_call(run, in_specs=specs + [vmem] * count + [pl.BlockSpec(memor...  34.4 us
    all_to_all x1, blocking collectives, body(): col_got = lax.all_to_all(pay, 'dp', 0, 0, tiled=True)  15.1 us
    all_to_all x1, blocking collectives, body(): last = lax.all_to_all(pay, 'mp', 0, 0, tiled=True)  9.21 us
    ppermute x1, waiting for transfers between devices, body(): tok_last = lax.ppermute(tok_away, 'mp', x_across)  8 us
    pallas_call x1, Pallas kernels, gate_pre(): pl.pallas_call(gate_kernel, in_specs=[pl.BlockSpec(memory_space=pltpu.SME...  7.17 us
    all_to_all x1, waiting for transfers between devices, body(): row_got = lax.all_to_all(pay, 'mp', 0, 0, tiled=True)  6.25 us
    ppermute x1, waiting for transfers between devices, body(): down_got = lax.ppermute(down_away, 'dp', dp_pairs(1))  5.66 us
    all_to_all x1, starting transfers between devices, body(): row_got = lax.all_to_all(pay, 'mp', 0, 0, tiled=True)  4.53 us
  transfers between devices with their start and end apart: 18, of which 8 were waited for; matrix products, arithmetic and copies ran while one was open for 0% of the time, Pallas kernels for 28%

profile of v3, /device:TPU:0, one launch (start us, length us, event | category | flops | bytes accessed | tf_op | source)
XLA Modules:
  0.0 126.4 jit_solution(9507124152502675132)
XLA Ops:
  0.6 0.1 collective-permute-start.1
  0.8 0.1 stack.23.idx.refs_0_
  0.9 7.2 %gate_pre.1 = (f32[768,1024]{1,0:T(8,128)S(1)}, bf16[768,2048]{1,0:T(8,128)(2,1)S(1)}, bf16[2048,1024]{1,0:T(8,128)(2,1)S(1)}, bf16[2048,1024]{1,0:T(8,128)(2,1)S(1)}) custom-call(s32[5]{0:T(128)S(1)} %stack.23.idx.refs_0_, bf16[768,2048]{1,0:T(8,128)(2,1)} %tok_in.1, bf16[2048,1024]{1,0:T(8,128)(2,1)} %wg_in.1, bf16[2048,1024]{1,0:T(8,128)(2,1)} %wu_in.1), custom_call_target="tpu_custom_call" | custom-call | flops 1000000 | bytes 1024 | tf_op jit(solution)/shard_map/gate_pre/pallas_call | solution.py:95
  8.1 0.5 collective-permute-start
  8.6 5.3 %up_pre.1 = (f32[768,1024]{1,0:T(8,128)S(1)}, f32[768,1024]{1,0:T(8,128)S(1)}, bf16[2,256,768]{2,1,0:T(8,128)(2,1)S(1)}, bf16[2,256,768]{2,1,0:T(8,128)(2,1)S(1)}) custom-call(s32[5]{0:T(128)S(1)} %stack.23.idx.refs_0_, bf16[768,2048]{1,0:T(8,128)(2,1)S(1)} %get-tuple-element.55.refs_1_, bf16[2048,1024]{1,0:T(8,128)(2,1)S(1)} %get-tuple-element.56.refs_2_.refs_3_, ...), custom_call_target="tpu_custom_call" | custom-call | flops 201326592 | bytes 1024 | tf_op jit(solution)/shard_map/up_pre/pallas_call | solution.py:52
  13.9 3.5 %hidden_grad.1.refs_1_.refs_3_ = bf16[2,768,1024]{2,1,0:T(8,128)(2,1)S(1)} custom-call(bf16[768,2048]{1,0:T(8,128)(2,1)S(1)} %copy-done, bf16[1024,2048]{1,0:T(8,128)(2,1)S(1)} %copy-done.1, f32[768,1024]{1,0:T(8,128)S(1)} %get-tuple-element.58.refs_2_, f32[768,1024]{1,0:T(8,128)S(1)} %get-tuple-element.59.refs_3_, ...), custom_call_target="tpu_custom_call" | custom-call | flops 201326592 | bytes 1024 | tf_op jit(solution)/shard_map/hidden_grad/pallas_call | solution.py:52
  17.4 0.4 collective-permute-start.2
  17.8 0.3 collective-permute-start.3
  18.1 4.0 %token_grad.2 = (bf16[2,768,256]{2,1,0:T(8,128)(2,1)S(1)}, bf16[2,768,256]{2,1,0:T(8,128)(2,1)S(1)}) custom-call(s32[5]{0:T(128)S(1)} %stack.23.idx.refs_0_, bf16[2,768,1024]{2,1,0:T(8,128)(2,1)S(1)} %hidden_grad.1.refs_1_.refs_3_, bf16[2048,1024]{1,0:T(8,128)(2,1)S(1)} %get-tuple-element.60.refs_2_, bf16[2048,1024]{1,0:T(8,128)(2,1)S(1)} %get-tuple-element.56.refs_2_.refs_3_), custom_call_target="tpu_custom_call" | custom-call | flops 201326592 | bytes 1024 | tf_op jit(solution)/shard_map/token_grad/pallas_call | solution.py:52
  22.1 3.2 %collective-permute-start.5 = (bf16[2,768,256]{2,1,0:T(8,128)(2,1)S(1)}, bf16[2,768,256]{2,1,0:T(8,128)(2,1)S(1)}, u32[]{:S(2)}, u32[]{:S(2)}) collective-permute-start(bf16[2,768,256]{2,1,0:T(8,128)(2,1)S(1)} %get-tuple-element.68), channel_id=1, source_target_pairs={{0,6},{1,7},{2,0},{3,1},{4,2},{5,3},{6,4},{7,5},{8,14},{9,15},{10,... | collective-permute-start | bytes 2359304 | tf_op jit(solution)/shard_map/ppermute | solution.py:402
  25.2 4.1 %weight.2 = (bf16[2,128,2048]{2,1,0:T(8,128)(2,1)S(1)}, bf16[2,128,2048]{2,1,0:T(8,128)(2,1)S(1)}) custom-call(s32[5]{0:T(128)S(1)} %stack.23.idx.refs_0_, bf16[768,2048]{1,0:T(8,128)(2,1)S(1)} %get-tuple-element.55.refs_1_, bf16[768,2048]{1,0:T(8,128)(2,1)S(1)} %collective-permute-done.refs_4_.refs_2_, ...), custom_call_target="tpu_custom_call" | custom-call | flops 201326592 | bytes 1024 | tf_op jit(solution)/shard_map/weight/pallas_call | solution.py:52
  29.3 4.1 %collective-permute-start.9 = (bf16[2,128,2048]{2,1,0:T(8,128)(2,1)S(1)}, bf16[2,128,2048]{2,1,0:T(8,128)(2,1)S(1)}, u32[]{:S(2)}, u32[]{:S(2)}) collective-permute-start(bf16[2,128,2048]{2,1,0:T(8,128)(2,1)S(1)} %get-tuple-element.72), channel_id=1, source_target_pairs={{0,96},{8,104},{16,112},{24,120},{32,0},{40,8},{48,16},{56,24},{64... | collective-permute-start | bytes 3145736 | tf_op jit(solution)/shard_map/ppermute | solution.py:405
  33.4 1.8 %down.2.refs_5_ = bf16[256,2048]{1,0:T(8,128)(2,1)S(1)} custom-call(bf16[2,256,768]{2,1,0:T(8,128)(2,1)S(1)} %get-tuple-element.61.refs_0_, bf16[2,256,768]{2,1,0:T(8,128)(2,1)S(1)} %collective-permute-done.3.refs_1_, bf16[768,2048]{1,0:T(8,128)(2,1)S(1)} %copy-done, bf16[768,2048]{1,0:T(8,128)(2,1)S(1)} %collective-permute-done.1.refs_5_.refs_3_, ...), custom_call_target="tpu_custom_call" | custom-call | flops 100663296 | bytes 1024 | tf_op jit(solution)/shard_map/down/pallas_call | solution.py:52
  35.2 3.3 %collective-permute-start.11 = (bf16[256,2048]{1,0:T(8,128)(2,1)S(1)}, bf16[256,2048]{1,0:T(8,128)(2,1)S(1)}, u32[]{:S(2)}, u32[]{:S(2)}) collective-permute-start(bf16[256,2048]{1,0:T(8,128)(2,1)S(1)} %down.2.refs_5_), channel_id=1, source_target_pairs={{0,16},{8,24},{16,0},{24,8},{32,48},{40,56},{48,32},{56,40},{64,80... | collective-permute-start | bytes 3145736 | tf_op jit(solution)/shard_map/ppermute | solution.py:412
  38.6 4.0 %weight.3 = (bf16[2,128,2048]{2,1,0:T(8,128)(2,1)S(1)}, bf16[2,128,2048]{2,1,0:T(8,128)(2,1)S(1)}) custom-call(s32[5]{0:T(128)S(1)} %stack.23.idx.refs_0_, bf16[768,2048]{1,0:T(8,128)(2,1)S(1)} %get-tuple-element.55.refs_1_, bf16[768,2048]{1,0:T(8,128)(2,1)S(1)} %collective-permute-done.refs_4_.refs_2_, ...), custom_call_target="tpu_custom_call" | custom-call | flops 201326592 | bytes 1024 | tf_op jit(solution)/shard_map/weight/pallas_call | solution.py:52
  42.6 4.0 %token_grad.3 = (bf16[2,768,256]{2,1,0:T(8,128)(2,1)S(1)}, bf16[2,768,256]{2,1,0:T(8,128)(2,1)S(1)}) custom-call(s32[5]{0:T(128)S(1)} %stack.23.idx.refs_0_, bf16[2,768,1024]{2,1,0:T(8,128)(2,1)S(1)} %hidden_grad.1.refs_1_.refs_3_, bf16[2048,1024]{1,0:T(8,128)(2,1)S(1)} %get-tuple-element.60.refs_2_, ...), custom_call_target="tpu_custom_call" | custom-call | flops 201326592 | bytes 1024 | tf_op jit(solution)/shard_map/token_grad/pallas_call | solution.py:52
  46.6 1.8 %down.3.refs_4_.refs_0_ = bf16[256,2048]{1,0:T(8,128)(2,1)S(1)} custom-call(bf16[2,256,768]{2,1,0:T(8,128)(2,1)S(1)} %get-tuple-element.61.refs_0_, bf16[2,256,768]{2,1,0:T(8,128)(2,1)S(1)} %collective-permute-done.3.refs_1_, bf16[768,2048]{1,0:T(8,128)(2,1)S(1)} %copy-done, bf16[768,2048]{1,0:T(8,128)(2,1)S(1)} %collective-permute-done.1.refs_5_.refs_3_, ...), custom_call_target="tpu_custom_call" | custom-call | flops 100663296 | bytes 1024 | tf_op jit(solution)/shard_map/down/pallas_call | solution.py:52
  48.4 0.2 middle.2
  48.6 3.3 %collective-permute-start.6 = (bf16[768,256]{1,0:T(8,128)(2,1)S(1)}, bf16[768,256]{1,0:T(8,128)(2,1)S(1)}, u32[]{:S(2)}, u32[]{:S(2)}) collective-permute-start(bf16[768,256]{1,0:T(8,128)(2,1)S(1)} %get-tuple-element.69), channel_id=1, source_target_pairs={{0,6},{1,7},{2,0},{3,1},{4,2},{5,3},{6,4},{7,5},{8,14},{9,15},{10,... | collective-permute-start | bytes 1179656 | tf_op jit(solution)/shard_map/ppermute | solution.py:404
  51.9 4.0 %collective-permute-done.9.refs_3_.refs_1_ = bf16[2,128,2048]{2,1,0:T(8,128)(2,1)S(1)} collective-permute-done((bf16[2,128,2048]{2,1,0:T(8,128)(2,1)S(1)}, bf16[2,128,2048]{2,1,0:T(8,128)(2,1)S(1)}, u32[]{:S(2)}, u32[]{:S(2)}) %collective-permute-start.9) | collective-permute-done | bytes 1048608 | tf_op jit(solution)/shard_map/ppermute | solution.py:405
  55.9 3.4 %collective-permute-done.8.refs_2_.refs_1_ = bf16[2,128,2048]{2,1,0:T(8,128)(2,1)S(1)} collective-permute-done((bf16[2,128,2048]{2,1,0:T(8,128)(2,1)S(1)}, bf16[2,128,2048]{2,1,0:T(8,128)(2,1)S(1)}, u32[]{:S(2)}, u32[]{:S(2)}) %collective-permute-start.8) | collective-permute-done | bytes 1048608 | tf_op jit(solution)/shard_map/ppermute | solution.py:405
  59.3 0.2 middle.3
  59.6 0.4 collective-permute-start.14
  59.9 1.7 %collective-permute-start.13 = (bf16[128,2048]{1,0:T(8,128)(2,1)S(1)}, bf16[128,2048]{1,0:T(8,128)(2,1)S(1)}, u32[]{:S(2)}, u32[]{:S(2)}) collective-permute-start(bf16[128,2048]{1,0:T(8,128)(2,1)S(1)} %get-tuple-element.73.refs_3_), channel_id=1, source_target_pairs={{0,32},{8,40},{16,48},{24,56},{32,64},{40,72},{48,80},{56,88},{64,... | collective-permute-start | bytes 1572872 | tf_op jit(solution)/shard_map/ppermute | solution.py:407
  61.7 1.3 %collective-permute-done.7.refs_2_ = bf16[768,256]{1,0:T(8,128)(2,1)S(1)} collective-permute-done((bf16[768,256]{1,0:T(8,128)(2,1)S(1)}, bf16[768,256]{1,0:T(8,128)(2,1)S(1)}, u32[]{:S(2)}, u32[]{:S(2)}) %collective-permute-start.7) | collective-permute-done | bytes 393248 | tf_op jit(solution)/shard_map/ppermute | solution.py:404
  63.0 0.1 crossing.2.refs_2_
  63.2 0.7 collective-permute-start.10
  63.8 0.2 down_mix.1
  64.1 0.1 collective-permute-start.12
  64.2 8.0 %collective-permute-done.10.refs_5_.refs_3_ = bf16[768,256]{1,0:T(8,128)(2,1)S(1)} collective-permute-done((bf16[768,256]{1,0:T(8,128)(2,1)S(1)}, bf16[768,256]{1,0:T(8,128)(2,1)S(1)}, u32[]{:S(2)}, u32[]{:S(2)}) %collective-permute-start.10) | collective-permute-done | bytes 393248 | tf_op jit(solution)/shard_map/ppermute | solution.py:409
  72.2 2.3 %collective-permute-done.14.refs_4_.refs_2_ = bf16[128,2048]{1,0:T(8,128)(2,1)S(1)} collective-permute-done((bf16[128,2048]{1,0:T(8,128)(2,1)S(1)}, bf16[128,2048]{1,0:T(8,128)(2,1)S(1)}, u32[]{:S(2)}, u32[]{:S(2)}) %collective-permute-start.14) | collective-permute-done | bytes 524320 | tf_op jit(solution)/shard_map/ppermute | solution.py:407
  74.5 0.2 crossing.3.refs_2_
  74.7 3.1 %collective-permute-start.15 = (bf16[128,2048]{1,0:T(8,128)(2,1)S(1)}, bf16[128,2048]{1,0:T(8,128)(2,1)S(1)}, u32[]{:S(2)}, u32[]{:S(2)}) collective-permute-start(bf16[128,2048]{1,0:T(8,128)(2,1)S(1)} %crossing.3.refs_2_), channel_id=1, source_target_pairs={{0,16},{8,24},{16,0},{24,8},{32,48},{40,56},{48,32},{56,40},{64,80... | collective-permute-start | bytes 1572872 | tf_op jit(solution)/shard_map/ppermute | solution.py:417
  77.8 5.7 %collective-permute-done.12.refs_1_.refs_3_ = bf16[128,2048]{1,0:T(8,128)(2,1)S(1)} collective-permute-done((bf16[128,2048]{1,0:T(8,128)(2,1)S(1)}, bf16[128,2048]{1,0:T(8,128)(2,1)S(1)}, u32[]{:S(2)}, u32[]{:S(2)}) %collective-permute-start.12) | collective-permute-done | bytes 524320 | tf_op jit(solution)/shard_map/ppermute | solution.py:415
  83.5 0.1 down_middle.1.refs_4_
  83.5 0.0 copy-start.5
  83.6 0.0 copy-start.7
  83.6 0.8 collective-permute-start.16
  84.3 0.9 token_end.1
  85.3 2.0 %collective-permute-done.15.refs_3_ = bf16[128,2048]{1,0:T(8,128)(2,1)S(1)} collective-permute-done((bf16[128,2048]{1,0:T(8,128)(2,1)S(1)}, bf16[128,2048]{1,0:T(8,128)(2,1)S(1)}, u32[]{:S(2)}, u32[]{:S(2)}) %collective-permute-start.15) | collective-permute-done | bytes 524320 | tf_op jit(solution)/shard_map/ppermute | solution.py:417
  87.3 1.0 row_sums.1
  88.3 4.5 %all-to-all-start = ((f32[8,8,128]{2,1,0:T(8,128)}), f32[8,8,128]{2,1,0:T(8,128)S(1)}, u32[]{:S(2)}, u32[]{:S(2)}) async-start(f32[8,8,128]{2,1,0:T(8,128)} %get-tuple-element.81), calls=%async_computation | async-start | bytes 65536 | tf_op jit(solution)/shard_map/all_to_all | solution.py:435
  92.8 6.3 %all-to-all-done.refs_5_ = f32[8,8,128]{2,1,0:T(8,128)S(1)} async-done(((f32[8,8,128]{2,1,0:T(8,128)}), f32[8,8,128]{2,1,0:T(8,128)S(1)}, u32[]{:S(2)}, u32[]{:S(2)}) %all-to-all-start) | async-done | bytes 32800 | tf_op jit(solution)/shard_map/all_to_all | solution.py:435
  99.1 1.1 column_sums.1
  100.2 15.1 %all_to_all.15.refs_0_ = bf16[16,80,128]{2,1,0:T(8,128)(2,1)S(1)} all-to-all(bf16[16,80,128]{2,1,0:T(8,128)(2,1)S(1)} %get-tuple-element.82), channel_id=1, replica_groups=mesh['dp'=16,'mp'=8] {'dp'}, dimensions={0} | all-to-all | bytes 655360 | tf_op jit(solution)/shard_map/all_to_all | solution.py:452
  115.3 0.6 partial_sums.1
  115.9 9.2 %all_to_all.16.refs_0_ = f32[8,40,128]{2,1,0:T(8,128)S(1)} all-to-all(f32[8,40,128]{2,1,0:T(8,128)S(1)} %get-tuple-element.83), channel_id=1, replica_groups=mesh['dp'=16,'mp'=8] {'mp'}, dimensions={0} | all-to-all | bytes 327680 | tf_op jit(solution)/shard_map/all_to_all | solution.py:461
  125.1 1.3 %updates.1 = (f32[128,1024]{1,0:T(8,128)}, f32[128,1024]{1,0:T(8,128)}, f32[64,2048]{1,0:T(8,128)}, f32[16,128]{1,0:T(8,128)}) custom-call(f32[8,40,128]{2,1,0:T(8,128)S(1)} %all_to_all.16.refs_0_, f32[8,128]{1,0:T(8,128)S(1)} %get-tuple-element.84.refs_1_, f32[16,128]{1,0:T(8,128)S(1)} %bitcast.17, f32[128,1024]{1,0:T(8,128)S(1)} %get-tuple-element.79.refs_0_.refs_3_, ...), custom_call_target="tpu_custom_call" | custom-call | flops 62 | bytes 1024 | tf_op jit(solution)/shard_map/updates/pallas_call | solution.py:52
  (27 shorter events, 0.1 us)
Async XLA Ops:
  0.6 13.2 %collective-permute-start.1 = (bf16[768,2048]{1,0:T(8,128)(2,1)}, bf16[768,2048]{1,0:T(8,128)(2,1)S(1)}, u32[]{:S(2)}, u32[]{:S(2)}) collective-permute-start(bf16[768,2048]{1,0:T(8,128)(2,1)} %refs_2_.3), channel_id=1, source_target_pairs={{0,8},{8,0},{16,24},{24,16},{32,40},{40,32},{48,56},{56,48},{64,72... | collective-permute-start | bytes 9437192 | tf_op jit(solution)/shard_map/ppermute | solution.py:348
  8.1 5.8 %collective-permute-start = (bf16[768,2048]{1,0:T(8,128)(2,1)S(1)}, bf16[768,2048]{1,0:T(8,128)(2,1)S(1)}, u32[]{:S(2)}, u32[]{:S(2)}) collective-permute-start(bf16[768,2048]{1,0:T(8,128)(2,1)S(1)} %get-tuple-element.55.refs_1_), channel_id=1, source_target_pairs={{0,8},{8,0},{16,24},{24,16},{32,40},{40,32},{48,56},{56,48},{64,72... | collective-permute-start | bytes 9437192 | tf_op jit(solution)/shard_map/ppermute | solution.py:351
  8.6 5.3 %copy-start = (bf16[768,2048]{1,0:T(8,128)(2,1)S(1)}, bf16[768,2048]{1,0:T(8,128)(2,1)}, u32[]{:S(2)}) copy-start(bf16[768,2048]{1,0:T(8,128)(2,1)} %refs_2_.3) | copy-start | bytes 9437188
  8.6 5.3 %copy-start.1 = (bf16[1024,2048]{1,0:T(8,128)(2,1)S(1)}, bf16[1024,2048]{1,0:T(8,128)(2,1)}, u32[]{:S(2)}) copy-start(bf16[1024,2048]{1,0:T(8,128)(2,1)} %refs_1_.1) | copy-start | bytes 12582916
  17.4 7.9 %collective-permute-start.2 = (bf16[2,768,1024]{2,1,0:T(8,128)(2,1)S(1)}, bf16[2,768,1024]{2,1,0:T(8,128)(2,1)S(1)}, u32[]{:S(2)}, u32[]{:S(2)}) collective-permute-start(bf16[2,768,1024]{2,1,0:T(8,128)(2,1)S(1)} %hidden_grad.1.refs_1_.refs_3_), channel_id=1, source_target_pairs={{0,8},{8,0},{16,24},{24,16},{32,40},{40,32},{48,56},{56,48},{64,72... | collective-permute-start | bytes 9437192 | tf_op jit(solution)/shard_map/ppermute | solution.py:362
  17.8 15.6 %collective-permute-start.3 = (bf16[2,256,768]{2,1,0:T(8,128)(2,1)S(1)}, bf16[2,256,768]{2,1,0:T(8,128)(2,1)S(1)}, u32[]{:S(2)}, u32[]{:S(2)}) collective-permute-start(bf16[2,256,768]{2,1,0:T(8,128)(2,1)S(1)} %get-tuple-element.62), channel_id=1, source_target_pairs={{0,8},{8,0},{16,24},{24,16},{32,40},{40,32},{48,56},{56,48},{64,72... | collective-permute-start | bytes 2359304 | tf_op jit(solution)/shard_map/ppermute | solution.py:356
  22.1 26.4 %collective-permute-start.5 = (bf16[2,768,256]{2,1,0:T(8,128)(2,1)S(1)}, bf16[2,768,256]{2,1,0:T(8,128)(2,1)S(1)}, u32[]{:S(2)}, u32[]{:S(2)}) collective-permute-start(bf16[2,768,256]{2,1,0:T(8,128)(2,1)S(1)} %get-tuple-element.68), channel_id=1, source_target_pairs={{0,6},{1,7},{2,0},{3,1},{4,2},{5,3},{6,4},{7,5},{8,14},{9,15},{10,... | collective-permute-start | bytes 2359304 | tf_op jit(solution)/shard_map/ppermute | solution.py:402
  25.2 23.2 %collective-permute-start.4 = (bf16[2,768,256]{2,1,0:T(8,128)(2,1)S(1)}, bf16[2,768,256]{2,1,0:T(8,128)(2,1)S(1)}, u32[]{:S(2)}, u32[]{:S(2)}) collective-permute-start(bf16[2,768,256]{2,1,0:T(8,128)(2,1)S(1)} %get-tuple-element.63.refs_5_), channel_id=1, source_target_pairs={{0,2},{1,3},{2,4},{3,5},{4,6},{5,7},{6,0},{7,1},{8,10},{9,11},{10,... | collective-permute-start | bytes 2359304 | tf_op jit(solution)/shard_map/ppermute | solution.py:402
  29.3 26.6 %collective-permute-start.9 = (bf16[2,128,2048]{2,1,0:T(8,128)(2,1)S(1)}, bf16[2,128,2048]{2,1,0:T(8,128)(2,1)S(1)}, u32[]{:S(2)}, u32[]{:S(2)}) collective-permute-start(bf16[2,128,2048]{2,1,0:T(8,128)(2,1)S(1)} %get-tuple-element.72), channel_id=1, source_target_pairs={{0,96},{8,104},{16,112},{24,120},{32,0},{40,8},{48,16},{56,24},{64... | collective-permute-start | bytes 3145736 | tf_op jit(solution)/shard_map/ppermute | solution.py:405
  33.4 25.9 %collective-permute-start.8 = (bf16[2,128,2048]{2,1,0:T(8,128)(2,1)S(1)}, bf16[2,128,2048]{2,1,0:T(8,128)(2,1)S(1)}, u32[]{:S(2)}, u32[]{:S(2)}) collective-permute-start(bf16[2,128,2048]{2,1,0:T(8,128)(2,1)S(1)} %get-tuple-element.64.refs_4_), channel_id=1, source_target_pairs={{0,32},{8,40},{16,48},{24,56},{32,64},{40,72},{48,80},{56,88},{64,... | collective-permute-start | bytes 3145736 | tf_op jit(solution)/shard_map/ppermute | solution.py:405
  35.2 28.6 %collective-permute-start.11 = (bf16[256,2048]{1,0:T(8,128)(2,1)S(1)}, bf16[256,2048]{1,0:T(8,128)(2,1)S(1)}, u32[]{:S(2)}, u32[]{:S(2)}) collective-permute-start(bf16[256,2048]{1,0:T(8,128)(2,1)S(1)} %down.2.refs_5_), channel_id=1, source_target_pairs={{0,16},{8,24},{16,0},{24,8},{32,48},{40,56},{48,32},{56,40},{64,80... | collective-permute-start | bytes 3145736 | tf_op jit(solution)/shard_map/ppermute | solution.py:412
  48.6 13.0 %collective-permute-start.6 = (bf16[768,256]{1,0:T(8,128)(2,1)S(1)}, bf16[768,256]{1,0:T(8,128)(2,1)S(1)}, u32[]{:S(2)}, u32[]{:S(2)}) collective-permute-start(bf16[768,256]{1,0:T(8,128)(2,1)S(1)} %get-tuple-element.69), channel_id=1, source_target_pairs={{0,6},{1,7},{2,0},{3,1},{4,2},{5,3},{6,4},{7,5},{8,14},{9,15},{10,... | collective-permute-start | bytes 1179656 | tf_op jit(solution)/shard_map/ppermute | solution.py:404
  51.9 11.1 %collective-permute-start.7 = (bf16[768,256]{1,0:T(8,128)(2,1)S(1)}, bf16[768,256]{1,0:T(8,128)(2,1)S(1)}, u32[]{:S(2)}, u32[]{:S(2)}) collective-permute-start(bf16[768,256]{1,0:T(8,128)(2,1)S(1)} %get-tuple-element.70.refs_4_), channel_id=1, source_target_pairs={{0,2},{1,3},{2,4},{3,5},{4,6},{5,7},{6,0},{7,1},{8,10},{9,11},{10,... | collective-permute-start | bytes 1179656 | tf_op jit(solution)/shard_map/ppermute | solution.py:404
  59.6 14.9 %collective-permute-start.14 = (bf16[128,2048]{1,0:T(8,128)(2,1)S(1)}, bf16[128,2048]{1,0:T(8,128)(2,1)S(1)}, u32[]{:S(2)}, u32[]{:S(2)}) collective-permute-start(bf16[128,2048]{1,0:T(8,128)(2,1)S(1)} %get-tuple-element.76), channel_id=1, source_target_pairs={{0,96},{8,104},{16,112},{24,120},{32,0},{40,8},{48,16},{56,24},{64... | collective-permute-start | bytes 1572872 | tf_op jit(solution)/shard_map/ppermute | solution.py:407
  59.9 14.6 %collective-permute-start.13 = (bf16[128,2048]{1,0:T(8,128)(2,1)S(1)}, bf16[128,2048]{1,0:T(8,128)(2,1)S(1)}, u32[]{:S(2)}, u32[]{:S(2)}) collective-permute-start(bf16[128,2048]{1,0:T(8,128)(2,1)S(1)} %get-tuple-element.73.refs_3_), channel_id=1, source_target_pairs={{0,32},{8,40},{16,48},{24,56},{32,64},{40,72},{48,80},{56,88},{64,... | collective-permute-start | bytes 1572872 | tf_op jit(solution)/shard_map/ppermute | solution.py:407
  63.2 9.0 %collective-permute-start.10 = (bf16[768,256]{1,0:T(8,128)(2,1)S(1)}, bf16[768,256]{1,0:T(8,128)(2,1)S(1)}, u32[]{:S(2)}, u32[]{:S(2)}) collective-permute-start(bf16[768,256]{1,0:T(8,128)(2,1)S(1)} %crossing.2.refs_2_), channel_id=1, source_target_pairs={{0,1},{1,0},{2,3},{3,2},{4,5},{5,4},{6,7},{7,6},{8,9},{9,8},{10,11... | collective-permute-start | bytes 1179656 | tf_op jit(solution)/shard_map/ppermute | solution.py:409
  64.1 19.4 %collective-permute-start.12 = (bf16[128,2048]{1,0:T(8,128)(2,1)S(1)}, bf16[128,2048]{1,0:T(8,128)(2,1)S(1)}, u32[]{:S(2)}, u32[]{:S(2)}) collective-permute-start(bf16[128,2048]{1,0:T(8,128)(2,1)S(1)} %get-tuple-element.75.refs_3_), channel_id=1, source_target_pairs={{0,32},{8,40},{16,48},{24,56},{32,0},{40,8},{48,16},{56,24},{64,96... | collective-permute-start | bytes 1572872 | tf_op jit(solution)/shard_map/ppermute | solution.py:415
  74.7 12.6 %collective-permute-start.15 = (bf16[128,2048]{1,0:T(8,128)(2,1)S(1)}, bf16[128,2048]{1,0:T(8,128)(2,1)S(1)}, u32[]{:S(2)}, u32[]{:S(2)}) collective-permute-start(bf16[128,2048]{1,0:T(8,128)(2,1)S(1)} %crossing.3.refs_2_), channel_id=1, source_target_pairs={{0,16},{8,24},{16,0},{24,8},{32,48},{40,56},{48,32},{56,40},{64,80... | collective-permute-start | bytes 1572872 | tf_op jit(solution)/shard_map/ppermute | solution.py:417
  83.5 15.5 %copy-start.5 = (f32[128]{0:T(128)S(1)}, f32[128]{0:T(128)}, u32[]{:S(2)}) copy-start(f32[128]{0:T(128)} %param.16) | copy-start | bytes 1540
  83.5 15.5 %copy-start.6 = (f32[128]{0:T(128)S(1)}, f32[128]{0:T(128)}, u32[]{:S(2)}) copy-start(f32[128]{0:T(128)} %param.18) | copy-start | bytes 1540
  83.6 15.5 %copy-start.7 = (f32[64]{0:T(128)S(1)}, f32[64]{0:T(128)}, u32[]{:S(2)}) copy-start(f32[64]{0:T(128)} %param.20) | copy-start | bytes 772
  83.6 9.2 %collective-permute-start.16 = (bf16[64,2048]{1,0:T(8,128)(2,1)S(1)}, bf16[64,2048]{1,0:T(8,128)(2,1)S(1)}, u32[]{:S(2)}, u32[]{:S(2)}) collective-permute-start(bf16[64,2048]{1,0:T(8,128)(2,1)S(1)} %down_middle.1.refs_4_), channel_id=1, source_target_pairs={{0,96},{8,104},{16,112},{24,120},{32,64},{40,72},{48,80},{56,88},{... | collective-permute-start | bytes 786440 | tf_op jit(solution)/shard_map/ppermute | solution.py:422
  85.3 30.0 %copy-start.3 = (f32[1024]{0:T(1024)S(1)}, f32[1024]{0:T(1024)}, u32[]{:S(2)}) copy-start(f32[1024]{0:T(1024)} %param.17) | copy-start | bytes 12292
  85.3 30.0 %copy-start.4 = (f32[1024]{0:T(1024)S(1)}, f32[1024]{0:T(1024)}, u32[]{:S(2)}) copy-start(f32[1024]{0:T(1024)} %param.19) | copy-start | bytes 12292
  87.3 37.8 %copy-start.2 = (f32[2048]{0:T(1024)S(1)}, f32[2048]{0:T(1024)}, u32[]{:S(2)}) copy-start(f32[2048]{0:T(1024)} %param.21) | copy-start | bytes 24580
  88.3 10.8 %all-to-all-start = ((f32[8,8,128]{2,1,0:T(8,128)}), f32[8,8,128]{2,1,0:T(8,128)S(1)}, u32[]{:S(2)}, u32[]{:S(2)}) async-start(f32[8,8,128]{2,1,0:T(8,128)} %get-tuple-element.81), calls=%async_computation | async-start | bytes 65536 | tf_op jit(solution)/shard_map/all_to_all | solution.py:435

commit v4 on v3

--- a/solution.py
+++ b/solution.py
@@ -76,15 +76,19 @@
     tok_copy = [pltpu.make_async_copy(tok_in.at[r, :], tok.at[r, :], tok_sem.at[m])
                 for m, r in enumerate(rows)]
     wu_copy = pltpu.make_async_copy(wu_in, wu, wu_sem)
-    for copy in (tok_copy[0], *wg_copy, *tok_copy[1:], wu_copy):
+    for copy in (tok_copy[0], *wg_copy[:4], *tok_copy[1:], *wg_copy[4:], wu_copy):
         copy.start()
-    for copy in wg_copy:
-        copy.wait()
-    for m, r in enumerate(rows):
-        tok_copy[m].wait()
-        for n in range(2):
-            c = pl.ds(n * 512, 512)
-            gate[r, c] = contract(tok[r, :], wg[:, c], 1, 0)
+    for half in range(2):
+        depth = pl.ds(half * 1024, 1024)
+        for copy in wg_copy[half * 4 : half * 4 + 4]:
+            copy.wait()
+        for m, r in enumerate(rows):
+            if half == 0:
+                tok_copy[m].wait()
+            for n in range(2):
+                c = pl.ds(n * 512, 512)
+                term = contract(tok[r, depth], wg[depth, c], 1, 0)
+                gate[r, c] = term if half == 0 else gate[r, c] + term
     wu_copy.wait()
 
 

time: 127 us -> 126 us (level)
  transfers between devices with their start and end apart: 18 -> 18, of which waited for: 8 -> 8; matrix products, arithmetic and copies ran while one was open for 0% -> 0% of each run, Pallas kernels for 28% -> 27%
where the time goes in v4:
time: 126 us
  Pallas kernels  40.8 us (32%)
  waiting for transfers between devices  33 us (26%)
  starting transfers between devices  26.4 us (21%)
  blocking collectives  24.3 us (19%)
    pallas_call x19, Pallas kernels, local_kernel(): pl.pallas_call(run, in_specs=specs + [vmem] * count + [pl.BlockSpec(memor...  34.4 us
    all_to_all x1, blocking collectives, body(): col_got = lax.all_to_all(pay, 'dp', 0, 0, tiled=True)  15.1 us
    all_to_all x1, blocking collectives, body(): last = lax.all_to_all(pay, 'mp', 0, 0, tiled=True)  9.21 us
    ppermute x1, waiting for transfers between devices, body(): tok_last = lax.ppermute(tok_away, 'mp', x_across)  7.99 us
    pallas_call x1, Pallas kernels, gate_pre(): pl.pallas_call(gate_kernel, in_specs=[pl.BlockSpec(memory_space=pltpu.SME...  6.39 us
    all_to_all x1, waiting for transfers between devices, body(): row_got = lax.all_to_all(pay, 'mp', 0, 0, tiled=True)  6.25 us
    ppermute x1, waiting for transfers between devices, body(): down_got = lax.ppermute(down_away, 'dp', dp_pairs(1))  5.68 us
    all_to_all x1, starting transfers between devices, body(): row_got = lax.all_to_all(pay, 'mp', 0, 0, tiled=True)  4.47 us
  transfers between devices with their start and end apart: 18, of which 8 were waited for; matrix products, arithmetic and copies ran while one was open for 0% of the time, Pallas kernels for 27%

profile of v4, /device:TPU:0, one launch (start us, length us, event | category | flops | bytes accessed | tf_op | source)
XLA Modules:
  0.0 125.6 jit_solution(3701037268715572482)
XLA Ops:
  0.6 0.1 collective-permute-start.1
  0.8 0.1 stack.23.idx.refs_0_
  0.9 6.4 %gate_pre.1 = (f32[768,1024]{1,0:T(8,128)S(1)}, bf16[768,2048]{1,0:T(8,128)(2,1)S(1)}, bf16[2048,1024]{1,0:T(8,128)(2,1)S(1)}, bf16[2048,1024]{1,0:T(8,128)(2,1)S(1)}) custom-call(s32[5]{0:T(128)S(1)} %stack.23.idx.refs_0_, bf16[768,2048]{1,0:T(8,128)(2,1)} %tok_in.1, bf16[2048,1024]{1,0:T(8,128)(2,1)} %wg_in.1, bf16[2048,1024]{1,0:T(8,128)(2,1)} %wu_in.1), custom_call_target="tpu_custom_call" | custom-call | flops 1000000 | bytes 1024 | tf_op jit(solution)/shard_map/gate_pre/pallas_call | solution.py:99
  7.3 0.5 collective-permute-start
  7.8 5.3 %up_pre.1 = (f32[768,1024]{1,0:T(8,128)S(1)}, f32[768,1024]{1,0:T(8,128)S(1)}, bf16[2,256,768]{2,1,0:T(8,128)(2,1)S(1)}, bf16[2,256,768]{2,1,0:T(8,128)(2,1)S(1)}) custom-call(s32[5]{0:T(128)S(1)} %stack.23.idx.refs_0_, bf16[768,2048]{1,0:T(8,128)(2,1)S(1)} %get-tuple-element.55.refs_1_, bf16[2048,1024]{1,0:T(8,128)(2,1)S(1)} %get-tuple-element.56.refs_2_.refs_3_, ...), custom_call_target="tpu_custom_call" | custom-call | flops 201326592 | bytes 1024 | tf_op jit(solution)/shard_map/up_pre/pallas_call | solution.py:52
  13.1 3.5 %hidden_grad.1.refs_1_.refs_3_ = bf16[2,768,1024]{2,1,0:T(8,128)(2,1)S(1)} custom-call(bf16[768,2048]{1,0:T(8,128)(2,1)S(1)} %copy-done, bf16[1024,2048]{1,0:T(8,128)(2,1)S(1)} %copy-done.1, f32[768,1024]{1,0:T(8,128)S(1)} %get-tuple-element.58.refs_2_, f32[768,1024]{1,0:T(8,128)S(1)} %get-tuple-element.59.refs_3_, ...), custom_call_target="tpu_custom_call" | custom-call | flops 201326592 | bytes 1024 | tf_op jit(solution)/shard_map/hidden_grad/pallas_call | solution.py:52
  16.6 0.4 collective-permute-start.2
  17.0 0.3 collective-permute-start.3
  17.3 4.0 %token_grad.2 = (bf16[2,768,256]{2,1,0:T(8,128)(2,1)S(1)}, bf16[2,768,256]{2,1,0:T(8,128)(2,1)S(1)}) custom-call(s32[5]{0:T(128)S(1)} %stack.23.idx.refs_0_, bf16[2,768,1024]{2,1,0:T(8,128)(2,1)S(1)} %hidden_grad.1.refs_1_.refs_3_, bf16[2048,1024]{1,0:T(8,128)(2,1)S(1)} %get-tuple-element.60.refs_2_, bf16[2048,1024]{1,0:T(8,128)(2,1)S(1)} %get-tuple-element.56.refs_2_.refs_3_), custom_call_target="tpu_custom_call" | custom-call | flops 201326592 | bytes 1024 | tf_op jit(solution)/shard_map/token_grad/pallas_call | solution.py:52
  21.3 3.2 %collective-permute-start.5 = (bf16[2,768,256]{2,1,0:T(8,128)(2,1)S(1)}, bf16[2,768,256]{2,1,0:T(8,128)(2,1)S(1)}, u32[]{:S(2)}, u32[]{:S(2)}) collective-permute-start(bf16[2,768,256]{2,1,0:T(8,128)(2,1)S(1)} %get-tuple-element.68), channel_id=1, source_target_pairs={{0,6},{1,7},{2,0},{3,1},{4,2},{5,3},{6,4},{7,5},{8,14},{9,15},{10,... | collective-permute-start | bytes 2359304 | tf_op jit(solution)/shard_map/ppermute | solution.py:406
  24.4 4.1 %weight.2 = (bf16[2,128,2048]{2,1,0:T(8,128)(2,1)S(1)}, bf16[2,128,2048]{2,1,0:T(8,128)(2,1)S(1)}) custom-call(s32[5]{0:T(128)S(1)} %stack.23.idx.refs_0_, bf16[768,2048]{1,0:T(8,128)(2,1)S(1)} %get-tuple-element.55.refs_1_, bf16[768,2048]{1,0:T(8,128)(2,1)S(1)} %collective-permute-done.refs_4_.refs_2_, ...), custom_call_target="tpu_custom_call" | custom-call | flops 201326592 | bytes 1024 | tf_op jit(solution)/shard_map/weight/pallas_call | solution.py:52
  28.5 4.1 %collective-permute-start.9 = (bf16[2,128,2048]{2,1,0:T(8,128)(2,1)S(1)}, bf16[2,128,2048]{2,1,0:T(8,128)(2,1)S(1)}, u32[]{:S(2)}, u32[]{:S(2)}) collective-permute-start(bf16[2,128,2048]{2,1,0:T(8,128)(2,1)S(1)} %get-tuple-element.72), channel_id=1, source_target_pairs={{0,96},{8,104},{16,112},{24,120},{32,0},{40,8},{48,16},{56,24},{64... | collective-permute-start | bytes 3145736 | tf_op jit(solution)/shard_map/ppermute | solution.py:409
  32.6 1.8 %down.2.refs_5_ = bf16[256,2048]{1,0:T(8,128)(2,1)S(1)} custom-call(bf16[2,256,768]{2,1,0:T(8,128)(2,1)S(1)} %get-tuple-element.61.refs_0_, bf16[2,256,768]{2,1,0:T(8,128)(2,1)S(1)} %collective-permute-done.3.refs_1_, bf16[768,2048]{1,0:T(8,128)(2,1)S(1)} %copy-done, bf16[768,2048]{1,0:T(8,128)(2,1)S(1)} %collective-permute-done.1.refs_5_.refs_3_, ...), custom_call_target="tpu_custom_call" | custom-call | flops 100663296 | bytes 1024 | tf_op jit(solution)/shard_map/down/pallas_call | solution.py:52
  34.4 3.4 %collective-permute-start.11 = (bf16[256,2048]{1,0:T(8,128)(2,1)S(1)}, bf16[256,2048]{1,0:T(8,128)(2,1)S(1)}, u32[]{:S(2)}, u32[]{:S(2)}) collective-permute-start(bf16[256,2048]{1,0:T(8,128)(2,1)S(1)} %down.2.refs_5_), channel_id=1, source_target_pairs={{0,16},{8,24},{16,0},{24,8},{32,48},{40,56},{48,32},{56,40},{64,80... | collective-permute-start | bytes 3145736 | tf_op jit(solution)/shard_map/ppermute | solution.py:416
  37.8 4.0 %weight.3 = (bf16[2,128,2048]{2,1,0:T(8,128)(2,1)S(1)}, bf16[2,128,2048]{2,1,0:T(8,128)(2,1)S(1)}) custom-call(s32[5]{0:T(128)S(1)} %stack.23.idx.refs_0_, bf16[768,2048]{1,0:T(8,128)(2,1)S(1)} %get-tuple-element.55.refs_1_, bf16[768,2048]{1,0:T(8,128)(2,1)S(1)} %collective-permute-done.refs_4_.refs_2_, ...), custom_call_target="tpu_custom_call" | custom-call | flops 201326592 | bytes 1024 | tf_op jit(solution)/shard_map/weight/pallas_call | solution.py:52
  41.8 4.0 %token_grad.3 = (bf16[2,768,256]{2,1,0:T(8,128)(2,1)S(1)}, bf16[2,768,256]{2,1,0:T(8,128)(2,1)S(1)}) custom-call(s32[5]{0:T(128)S(1)} %stack.23.idx.refs_0_, bf16[2,768,1024]{2,1,0:T(8,128)(2,1)S(1)} %hidden_grad.1.refs_1_.refs_3_, bf16[2048,1024]{1,0:T(8,128)(2,1)S(1)} %get-tuple-element.60.refs_2_, ...), custom_call_target="tpu_custom_call" | custom-call | flops 201326592 | bytes 1024 | tf_op jit(solution)/shard_map/token_grad/pallas_call | solution.py:52
  45.8 1.8 %down.3.refs_4_.refs_0_ = bf16[256,2048]{1,0:T(8,128)(2,1)S(1)} custom-call(bf16[2,256,768]{2,1,0:T(8,128)(2,1)S(1)} %get-tuple-element.61.refs_0_, bf16[2,256,768]{2,1,0:T(8,128)(2,1)S(1)} %collective-permute-done.3.refs_1_, bf16[768,2048]{1,0:T(8,128)(2,1)S(1)} %copy-done, bf16[768,2048]{1,0:T(8,128)(2,1)S(1)} %collective-permute-done.1.refs_5_.refs_3_, ...), custom_call_target="tpu_custom_call" | custom-call | flops 100663296 | bytes 1024 | tf_op jit(solution)/shard_map/down/pallas_call | solution.py:52
  47.7 0.2 middle.2
  47.9 3.3 %collective-permute-start.6 = (bf16[768,256]{1,0:T(8,128)(2,1)S(1)}, bf16[768,256]{1,0:T(8,128)(2,1)S(1)}, u32[]{:S(2)}, u32[]{:S(2)}) collective-permute-start(bf16[768,256]{1,0:T(8,128)(2,1)S(1)} %get-tuple-element.69), channel_id=1, source_target_pairs={{0,6},{1,7},{2,0},{3,1},{4,2},{5,3},{6,4},{7,5},{8,14},{9,15},{10,... | collective-permute-start | bytes 1179656 | tf_op jit(solution)/shard_map/ppermute | solution.py:408
  51.2 4.0 %collective-permute-done.9.refs_3_.refs_1_ = bf16[2,128,2048]{2,1,0:T(8,128)(2,1)S(1)} collective-permute-done((bf16[2,128,2048]{2,1,0:T(8,128)(2,1)S(1)}, bf16[2,128,2048]{2,1,0:T(8,128)(2,1)S(1)}, u32[]{:S(2)}, u32[]{:S(2)}) %collective-permute-start.9) | collective-permute-done | bytes 1048608 | tf_op jit(solution)/shard_map/ppermute | solution.py:409
  55.1 3.4 %collective-permute-done.8.refs_2_.refs_1_ = bf16[2,128,2048]{2,1,0:T(8,128)(2,1)S(1)} collective-permute-done((bf16[2,128,2048]{2,1,0:T(8,128)(2,1)S(1)}, bf16[2,128,2048]{2,1,0:T(8,128)(2,1)S(1)}, u32[]{:S(2)}, u32[]{:S(2)}) %collective-permute-start.8) | collective-permute-done | bytes 1048608 | tf_op jit(solution)/shard_map/ppermute | solution.py:409
  58.6 0.2 middle.3
  58.8 0.4 collective-permute-start.14
  59.1 1.7 %collective-permute-start.13 = (bf16[128,2048]{1,0:T(8,128)(2,1)S(1)}, bf16[128,2048]{1,0:T(8,128)(2,1)S(1)}, u32[]{:S(2)}, u32[]{:S(2)}) collective-permute-start(bf16[128,2048]{1,0:T(8,128)(2,1)S(1)} %get-tuple-element.73.refs_3_), channel_id=1, source_target_pairs={{0,32},{8,40},{16,48},{24,56},{32,64},{40,72},{48,80},{56,88},{64,... | collective-permute-start | bytes 1572872 | tf_op jit(solution)/shard_map/ppermute | solution.py:411
  60.9 1.3 %collective-permute-done.7.refs_2_ = bf16[768,256]{1,0:T(8,128)(2,1)S(1)} collective-permute-done((bf16[768,256]{1,0:T(8,128)(2,1)S(1)}, bf16[768,256]{1,0:T(8,128)(2,1)S(1)}, u32[]{:S(2)}, u32[]{:S(2)}) %collective-permute-start.7) | collective-permute-done | bytes 393248 | tf_op jit(solution)/shard_map/ppermute | solution.py:408
  62.2 0.1 crossing.2.refs_2_
  62.4 0.7 collective-permute-start.10
  63.1 0.2 down_mix.1
  63.3 0.1 collective-permute-start.12
  63.4 8.0 %collective-permute-done.10.refs_5_.refs_3_ = bf16[768,256]{1,0:T(8,128)(2,1)S(1)} collective-permute-done((bf16[768,256]{1,0:T(8,128)(2,1)S(1)}, bf16[768,256]{1,0:T(8,128)(2,1)S(1)}, u32[]{:S(2)}, u32[]{:S(2)}) %collective-permute-start.10) | collective-permute-done | bytes 393248 | tf_op jit(solution)/shard_map/ppermute | solution.py:413
  71.4 2.3 %collective-permute-done.14.refs_4_.refs_2_ = bf16[128,2048]{1,0:T(8,128)(2,1)S(1)} collective-permute-done((bf16[128,2048]{1,0:T(8,128)(2,1)S(1)}, bf16[128,2048]{1,0:T(8,128)(2,1)S(1)}, u32[]{:S(2)}, u32[]{:S(2)}) %collective-permute-start.14) | collective-permute-done | bytes 524320 | tf_op jit(solution)/shard_map/ppermute | solution.py:411
  73.7 0.2 crossing.3.refs_2_
  73.9 3.1 %collective-permute-start.15 = (bf16[128,2048]{1,0:T(8,128)(2,1)S(1)}, bf16[128,2048]{1,0:T(8,128)(2,1)S(1)}, u32[]{:S(2)}, u32[]{:S(2)}) collective-permute-start(bf16[128,2048]{1,0:T(8,128)(2,1)S(1)} %crossing.3.refs_2_), channel_id=1, source_target_pairs={{0,16},{8,24},{16,0},{24,8},{32,48},{40,56},{48,32},{56,40},{64,80... | collective-permute-start | bytes 1572872 | tf_op jit(solution)/shard_map/ppermute | solution.py:421
  77.0 5.7 %collective-permute-done.12.refs_1_.refs_3_ = bf16[128,2048]{1,0:T(8,128)(2,1)S(1)} collective-permute-done((bf16[128,2048]{1,0:T(8,128)(2,1)S(1)}, bf16[128,2048]{1,0:T(8,128)(2,1)S(1)}, u32[]{:S(2)}, u32[]{:S(2)}) %collective-permute-start.12) | collective-permute-done | bytes 524320 | tf_op jit(solution)/shard_map/ppermute | solution.py:419
  82.7 0.1 down_middle.1.refs_4_
  82.8 0.0 copy-start.6
  82.8 0.0 copy-start.7
  82.8 0.8 collective-permute-start.16
  83.6 0.9 token_end.1
  84.5 2.0 %collective-permute-done.15.refs_3_ = bf16[128,2048]{1,0:T(8,128)(2,1)S(1)} collective-permute-done((bf16[128,2048]{1,0:T(8,128)(2,1)S(1)}, bf16[128,2048]{1,0:T(8,128)(2,1)S(1)}, u32[]{:S(2)}, u32[]{:S(2)}) %collective-permute-start.15) | collective-permute-done | bytes 524320 | tf_op jit(solution)/shard_map/ppermute | solution.py:421
  86.5 1.0 row_sums.1
  87.5 4.5 %all-to-all-start = ((f32[8,8,128]{2,1,0:T(8,128)}), f32[8,8,128]{2,1,0:T(8,128)S(1)}, u32[]{:S(2)}, u32[]{:S(2)}) async-start(f32[8,8,128]{2,1,0:T(8,128)} %get-tuple-element.81), calls=%async_computation | async-start | bytes 65536 | tf_op jit(solution)/shard_map/all_to_all | solution.py:439
  92.0 6.3 %all-to-all-done.refs_5_ = f32[8,8,128]{2,1,0:T(8,128)S(1)} async-done(((f32[8,8,128]{2,1,0:T(8,128)}), f32[8,8,128]{2,1,0:T(8,128)S(1)}, u32[]{:S(2)}, u32[]{:S(2)}) %all-to-all-start) | async-done | bytes 32800 | tf_op jit(solution)/shard_map/all_to_all | solution.py:439
  98.3 1.1 column_sums.1
  99.4 15.1 %all_to_all.15.refs_0_ = bf16[16,80,128]{2,1,0:T(8,128)(2,1)S(1)} all-to-all(bf16[16,80,128]{2,1,0:T(8,128)(2,1)S(1)} %get-tuple-element.82), channel_id=1, replica_groups=mesh['dp'=16,'mp'=8] {'dp'}, dimensions={0} | all-to-all | bytes 655360 | tf_op jit(solution)/shard_map/all_to_all | solution.py:456
  114.5 0.6 partial_sums.1
  115.1 9.2 %all_to_all.16.refs_0_ = f32[8,40,128]{2,1,0:T(8,128)S(1)} all-to-all(f32[8,40,128]{2,1,0:T(8,128)S(1)} %get-tuple-element.83), channel_id=1, replica_groups=mesh['dp'=16,'mp'=8] {'mp'}, dimensions={0} | all-to-all | bytes 327680 | tf_op jit(solution)/shard_map/all_to_all | solution.py:465
  124.3 1.3 %updates.1 = (f32[128,1024]{1,0:T(8,128)}, f32[128,1024]{1,0:T(8,128)}, f32[64,2048]{1,0:T(8,128)}, f32[16,128]{1,0:T(8,128)}) custom-call(f32[8,40,128]{2,1,0:T(8,128)S(1)} %all_to_all.16.refs_0_, f32[8,128]{1,0:T(8,128)S(1)} %get-tuple-element.84.refs_1_, f32[16,128]{1,0:T(8,128)S(1)} %bitcast.17, f32[128,1024]{1,0:T(8,128)S(1)} %get-tuple-element.79.refs_0_.refs_3_, ...), custom_call_target="tpu_custom_call" | custom-call | flops 62 | bytes 1024 | tf_op jit(solution)/shard_map/updates/pallas_call | solution.py:52
  (27 shorter events, 0.1 us)
Async XLA Ops:
  0.6 12.4 %collective-permute-start.1 = (bf16[768,2048]{1,0:T(8,128)(2,1)}, bf16[768,2048]{1,0:T(8,128)(2,1)S(1)}, u32[]{:S(2)}, u32[]{:S(2)}) collective-permute-start(bf16[768,2048]{1,0:T(8,128)(2,1)} %refs_2_.3), channel_id=1, source_target_pairs={{0,8},{8,0},{16,24},{24,16},{32,40},{40,32},{48,56},{56,48},{64,72... | collective-permute-start | bytes 9437192 | tf_op jit(solution)/shard_map/ppermute | solution.py:352
  7.3 5.8 %collective-permute-start = (bf16[768,2048]{1,0:T(8,128)(2,1)S(1)}, bf16[768,2048]{1,0:T(8,128)(2,1)S(1)}, u32[]{:S(2)}, u32[]{:S(2)}) collective-permute-start(bf16[768,2048]{1,0:T(8,128)(2,1)S(1)} %get-tuple-element.55.refs_1_), channel_id=1, source_target_pairs={{0,8},{8,0},{16,24},{24,16},{32,40},{40,32},{48,56},{56,48},{64,72... | collective-permute-start | bytes 9437192 | tf_op jit(solution)/shard_map/ppermute | solution.py:355
  7.8 5.3 %copy-start = (bf16[768,2048]{1,0:T(8,128)(2,1)S(1)}, bf16[768,2048]{1,0:T(8,128)(2,1)}, u32[]{:S(2)}) copy-start(bf16[768,2048]{1,0:T(8,128)(2,1)} %refs_2_.3) | copy-start | bytes 9437188
  7.8 5.3 %copy-start.1 = (bf16[1024,2048]{1,0:T(8,128)(2,1)S(1)}, bf16[1024,2048]{1,0:T(8,128)(2,1)}, u32[]{:S(2)}) copy-start(bf16[1024,2048]{1,0:T(8,128)(2,1)} %refs_1_.1) | copy-start | bytes 12582916
  16.6 7.9 %collective-permute-start.2 = (bf16[2,768,1024]{2,1,0:T(8,128)(2,1)S(1)}, bf16[2,768,1024]{2,1,0:T(8,128)(2,1)S(1)}, u32[]{:S(2)}, u32[]{:S(2)}) collective-permute-start(bf16[2,768,1024]{2,1,0:T(8,128)(2,1)S(1)} %hidden_grad.1.refs_1_.refs_3_), channel_id=1, source_target_pairs={{0,8},{8,0},{16,24},{24,16},{32,40},{40,32},{48,56},{56,48},{64,72... | collective-permute-start | bytes 9437192 | tf_op jit(solution)/shard_map/ppermute | solution.py:366
  17.0 15.6 %collective-permute-start.3 = (bf16[2,256,768]{2,1,0:T(8,128)(2,1)S(1)}, bf16[2,256,768]{2,1,0:T(8,128)(2,1)S(1)}, u32[]{:S(2)}, u32[]{:S(2)}) collective-permute-start(bf16[2,256,768]{2,1,0:T(8,128)(2,1)S(1)} %get-tuple-element.62), channel_id=1, source_target_pairs={{0,8},{8,0},{16,24},{24,16},{32,40},{40,32},{48,56},{56,48},{64,72... | collective-permute-start | bytes 2359304 | tf_op jit(solution)/shard_map/ppermute | solution.py:360
  21.3 26.4 %collective-permute-start.5 = (bf16[2,768,256]{2,1,0:T(8,128)(2,1)S(1)}, bf16[2,768,256]{2,1,0:T(8,128)(2,1)S(1)}, u32[]{:S(2)}, u32[]{:S(2)}) collective-permute-start(bf16[2,768,256]{2,1,0:T(8,128)(2,1)S(1)} %get-tuple-element.68), channel_id=1, source_target_pairs={{0,6},{1,7},{2,0},{3,1},{4,2},{5,3},{6,4},{7,5},{8,14},{9,15},{10,... | collective-permute-start | bytes 2359304 | tf_op jit(solution)/shard_map/ppermute | solution.py:406
  24.4 23.2 %collective-permute-start.4 = (bf16[2,768,256]{2,1,0:T(8,128)(2,1)S(1)}, bf16[2,768,256]{2,1,0:T(8,128)(2,1)S(1)}, u32[]{:S(2)}, u32[]{:S(2)}) collective-permute-start(bf16[2,768,256]{2,1,0:T(8,128)(2,1)S(1)} %get-tuple-element.63.refs_5_), channel_id=1, source_target_pairs={{0,2},{1,3},{2,4},{3,5},{4,6},{5,7},{6,0},{7,1},{8,10},{9,11},{10,... | collective-permute-start | bytes 2359304 | tf_op jit(solution)/shard_map/ppermute | solution.py:406
  28.5 26.6 %collective-permute-start.9 = (bf16[2,128,2048]{2,1,0:T(8,128)(2,1)S(1)}, bf16[2,128,2048]{2,1,0:T(8,128)(2,1)S(1)}, u32[]{:S(2)}, u32[]{:S(2)}) collective-permute-start(bf16[2,128,2048]{2,1,0:T(8,128)(2,1)S(1)} %get-tuple-element.72), channel_id=1, source_target_pairs={{0,96},{8,104},{16,112},{24,120},{32,0},{40,8},{48,16},{56,24},{64... | collective-permute-start | bytes 3145736 | tf_op jit(solution)/shard_map/ppermute | solution.py:409
  32.6 26.0 %collective-permute-start.8 = (bf16[2,128,2048]{2,1,0:T(8,128)(2,1)S(1)}, bf16[2,128,2048]{2,1,0:T(8,128)(2,1)S(1)}, u32[]{:S(2)}, u32[]{:S(2)}) collective-permute-start(bf16[2,128,2048]{2,1,0:T(8,128)(2,1)S(1)} %get-tuple-element.64.refs_4_), channel_id=1, source_target_pairs={{0,32},{8,40},{16,48},{24,56},{32,64},{40,72},{48,80},{56,88},{64,... | collective-permute-start | bytes 3145736 | tf_op jit(solution)/shard_map/ppermute | solution.py:409
  34.4 28.6 %collective-permute-start.11 = (bf16[256,2048]{1,0:T(8,128)(2,1)S(1)}, bf16[256,2048]{1,0:T(8,128)(2,1)S(1)}, u32[]{:S(2)}, u32[]{:S(2)}) collective-permute-start(bf16[256,2048]{1,0:T(8,128)(2,1)S(1)} %down.2.refs_5_), channel_id=1, source_target_pairs={{0,16},{8,24},{16,0},{24,8},{32,48},{40,56},{48,32},{56,40},{64,80... | collective-permute-start | bytes 3145736 | tf_op jit(solution)/shard_map/ppermute | solution.py:416
  47.9 13.0 %collective-permute-start.6 = (bf16[768,256]{1,0:T(8,128)(2,1)S(1)}, bf16[768,256]{1,0:T(8,128)(2,1)S(1)}, u32[]{:S(2)}, u32[]{:S(2)}) collective-permute-start(bf16[768,256]{1,0:T(8,128)(2,1)S(1)} %get-tuple-element.69), channel_id=1, source_target_pairs={{0,6},{1,7},{2,0},{3,1},{4,2},{5,3},{6,4},{7,5},{8,14},{9,15},{10,... | collective-permute-start | bytes 1179656 | tf_op jit(solution)/shard_map/ppermute | solution.py:408
  51.2 11.1 %collective-permute-start.7 = (bf16[768,256]{1,0:T(8,128)(2,1)S(1)}, bf16[768,256]{1,0:T(8,128)(2,1)S(1)}, u32[]{:S(2)}, u32[]{:S(2)}) collective-permute-start(bf16[768,256]{1,0:T(8,128)(2,1)S(1)} %get-tuple-element.70.refs_4_), channel_id=1, source_target_pairs={{0,2},{1,3},{2,4},{3,5},{4,6},{5,7},{6,0},{7,1},{8,10},{9,11},{10,... | collective-permute-start | bytes 1179656 | tf_op jit(solution)/shard_map/ppermute | solution.py:408
  58.8 14.9 %collective-permute-start.14 = (bf16[128,2048]{1,0:T(8,128)(2,1)S(1)}, bf16[128,2048]{1,0:T(8,128)(2,1)S(1)}, u32[]{:S(2)}, u32[]{:S(2)}) collective-permute-start(bf16[128,2048]{1,0:T(8,128)(2,1)S(1)} %get-tuple-element.76), channel_id=1, source_target_pairs={{0,96},{8,104},{16,112},{24,120},{32,0},{40,8},{48,16},{56,24},{64... | collective-permute-start | bytes 1572872 | tf_op jit(solution)/shard_map/ppermute | solution.py:411
  59.1 14.6 %collective-permute-start.13 = (bf16[128,2048]{1,0:T(8,128)(2,1)S(1)}, bf16[128,2048]{1,0:T(8,128)(2,1)S(1)}, u32[]{:S(2)}, u32[]{:S(2)}) collective-permute-start(bf16[128,2048]{1,0:T(8,128)(2,1)S(1)} %get-tuple-element.73.refs_3_), channel_id=1, source_target_pairs={{0,32},{8,40},{16,48},{24,56},{32,64},{40,72},{48,80},{56,88},{64,... | collective-permute-start | bytes 1572872 | tf_op jit(solution)/shard_map/ppermute | solution.py:411
  62.4 9.0 %collective-permute-start.10 = (bf16[768,256]{1,0:T(8,128)(2,1)S(1)}, bf16[768,256]{1,0:T(8,128)(2,1)S(1)}, u32[]{:S(2)}, u32[]{:S(2)}) collective-permute-start(bf16[768,256]{1,0:T(8,128)(2,1)S(1)} %crossing.2.refs_2_), channel_id=1, source_target_pairs={{0,1},{1,0},{2,3},{3,2},{4,5},{5,4},{6,7},{7,6},{8,9},{9,8},{10,11... | collective-permute-start | bytes 1179656 | tf_op jit(solution)/shard_map/ppermute | solution.py:413
  63.3 19.4 %collective-permute-start.12 = (bf16[128,2048]{1,0:T(8,128)(2,1)S(1)}, bf16[128,2048]{1,0:T(8,128)(2,1)S(1)}, u32[]{:S(2)}, u32[]{:S(2)}) collective-permute-start(bf16[128,2048]{1,0:T(8,128)(2,1)S(1)} %get-tuple-element.75.refs_3_), channel_id=1, source_target_pairs={{0,32},{8,40},{16,48},{24,56},{32,0},{40,8},{48,16},{56,24},{64,96... | collective-permute-start | bytes 1572872 | tf_op jit(solution)/shard_map/ppermute | solution.py:419
  73.9 12.6 %collective-permute-start.15 = (bf16[128,2048]{1,0:T(8,128)(2,1)S(1)}, bf16[128,2048]{1,0:T(8,128)(2,1)S(1)}, u32[]{:S(2)}, u32[]{:S(2)}) collective-permute-start(bf16[128,2048]{1,0:T(8,128)(2,1)S(1)} %crossing.3.refs_2_), channel_id=1, source_target_pairs={{0,16},{8,24},{16,0},{24,8},{32,48},{40,56},{48,32},{56,40},{64,80... | collective-permute-start | bytes 1572872 | tf_op jit(solution)/shard_map/ppermute | solution.py:421
  82.8 15.5 %copy-start.5 = (f32[128]{0:T(128)S(1)}, f32[128]{0:T(128)}, u32[]{:S(2)}) copy-start(f32[128]{0:T(128)} %param.16) | copy-start | bytes 1540
  82.8 15.5 %copy-start.6 = (f32[128]{0:T(128)S(1)}, f32[128]{0:T(128)}, u32[]{:S(2)}) copy-start(f32[128]{0:T(128)} %param.18) | copy-start | bytes 1540
  82.8 15.5 %copy-start.7 = (f32[64]{0:T(128)S(1)}, f32[64]{0:T(128)}, u32[]{:S(2)}) copy-start(f32[64]{0:T(128)} %param.20) | copy-start | bytes 772
  82.8 9.2 %collective-permute-start.16 = (bf16[64,2048]{1,0:T(8,128)(2,1)S(1)}, bf16[64,2048]{1,0:T(8,128)(2,1)S(1)}, u32[]{:S(2)}, u32[]{:S(2)}) collective-permute-start(bf16[64,2048]{1,0:T(8,128)(2,1)S(1)} %down_middle.1.refs_4_), channel_id=1, source_target_pairs={{0,96},{8,104},{16,112},{24,120},{32,64},{40,72},{48,80},{56,88},{... | collective-permute-start | bytes 786440 | tf_op jit(solution)/shard_map/ppermute | solution.py:426
  84.5 30.0 %copy-start.3 = (f32[1024]{0:T(1024)S(1)}, f32[1024]{0:T(1024)}, u32[]{:S(2)}) copy-start(f32[1024]{0:T(1024)} %param.17) | copy-start | bytes 12292
  84.5 30.0 %copy-start.4 = (f32[1024]{0:T(1024)S(1)}, f32[1024]{0:T(1024)}, u32[]{:S(2)}) copy-start(f32[1024]{0:T(1024)} %param.19) | copy-start | bytes 12292
  86.5 37.8 %copy-start.2 = (f32[2048]{0:T(1024)S(1)}, f32[2048]{0:T(1024)}, u32[]{:S(2)}) copy-start(f32[2048]{0:T(1024)} %param.21) | copy-start | bytes 24580
  87.5 10.7 %all-to-all-start = ((f32[8,8,128]{2,1,0:T(8,128)}), f32[8,8,128]{2,1,0:T(8,128)S(1)}, u32[]{:S(2)}, u32[]{:S(2)}) async-start(f32[8,8,128]{2,1,0:T(8,128)} %get-tuple-element.81), calls=%async_computation | async-start | bytes 65536 | tf_op jit(solution)/shard_map/all_to_all | solution.py:439

commit v5 on v4

--- a/solution.py
+++ b/solution.py
@@ -411,23 +411,18 @@
     pair_end = lax.ppermute(pair_mid[0], "dp", forth), lax.ppermute(pair_mid[1], "dp", back)
     tok_away = crossing(tok_a, tok_got[1], tok_end[0], (pair_mid[0], tok_end[1]))
     tok_last = lax.ppermute(tok_away, "mp", x_across)
+    pair_away = crossing(pair_a, pair_got[1], pair_end[0], (pair_end[1], tok_last))
+    pair_last = lax.ppermute(pair_away, "dp", across)
     part = near((units // 8, width), BF)
     down_away, down_keep = local_kernel(
         "down_mix", mix_kernel, None, [own, lax.ppermute(away, "dp", across)], [part] * 2, 1000,
-        after=(tok_away,),
+        after=(pair_away,),
     )
     down_got = lax.ppermute(down_away, "dp", dp_pairs(1))
-    pair_away = crossing(pair_a, pair_got[1], pair_end[0], (down_away, pair_end[1], tok_last))
-    pair_last = lax.ppermute(pair_away, "dp", across)
-    (down_mid,) = local_kernel(
-        "down_middle", down_middle_kernel, None, [down_keep, down_got],
-        [near((units // 16, width), BF)], 1000, after=(pair_away,),
-    )
-    down_end = lax.ppermute(down_mid, "dp", dp_pairs(3))
     token_grad, tok_ended = local_kernel(
         "token_end", token_end_kernel, None, [tok_b, tok_got[0], tok_end[1], tok_last],
         [jax.ShapeDtypeStruct((rows, width // 8), BF), near((8, 128), F32)], 1000,
-        after=(down_mid,),
+        after=(down_away,),
     )
 
     shard = near((width // 16, units), F32)
@@ -436,6 +431,11 @@
         [pair_b, pair_got[0], pair_end[1], pair_last],
         [shard, shard, near((8, 8, 128), F32)], 1000, after=(tok_ended,), limit=4,
     )
+    (down_mid,) = local_kernel(
+        "down_middle", down_middle_kernel, None, [down_keep, down_got],
+        [near((units // 16, width), BF)], 1000, after=(g_gate,),
+    )
+    down_end = lax.ppermute(down_mid, "dp", dp_pairs(3))
     row_got = lax.all_to_all(pay, "mp", 0, 0, tiled=True)
 
     counts = (all_units, width)

time: 126 us -> 127 us (level)
  blocking collectives: 24.3 us -> 34.9 us
  starting transfers between devices: 26.4 us -> 22 us
  waiting for transfers between devices: 33 us -> 28.6 us
    all_to_all x0 -> x1, blocking collectives: none -> 9.66 us  [body(): row_got = lax.all_to_all(pay, 'mp', 0, 0, tiled=True)]
    ppermute x1, waiting for transfers between devices: 2 us -> 8.74 us  [body(): pair_last = lax.ppermute(pair_away, 'dp', across)]
    all_to_all x1 -> x0, waiting for transfers between devices: 6.25 us -> none  [body(): row_got = lax.all_to_all(pay, 'mp', 0, 0, tiled=True)]
    ppermute x1, waiting for transfers between devices: 5.68 us -> 1.11 us  [body(): down_got = lax.ppermute(down_away, 'dp', dp_pairs(1))]
    all_to_all x1 -> x0, starting transfers between devices: 4.47 us -> none  [body(): row_got = lax.all_to_all(pay, 'mp', 0, 0, tiled=True)]
    ppermute x1, waiting for transfers between devices: 2.34 us -> 0.1 us  [body(): lax.ppermute(pair_mid[1], 'dp', back)]
    ppermute x1, waiting for transfers between devices: 0.01 us -> 1.53 us  [body(): lax.ppermute(pair_mid[0], 'dp', forth)]
  transfers between devices with their start and end apart: 18 -> 17, of which waited for: 8 -> 8; matrix products, arithmetic and copies ran while one was open for 0% -> 0% of each run, Pallas kernels for 27% -> 27%
where the time goes in v5:
time: 127 us
  Pallas kernels  40.2 us (32%)
  blocking collectives  34.9 us (27%)
  waiting for transfers between devices  28.6 us (23%)
  starting transfers between devices  22 us (17%)
    pallas_call x19, Pallas kernels, local_kernel(): pl.pallas_call(run, in_specs=specs + [vmem] * count + [pl.BlockSpec(memor...  33.8 us
    all_to_all x1, blocking collectives, body(): col_got = lax.all_to_all(pay, 'dp', 0, 0, tiled=True)  16 us
    all_to_all x1, blocking collectives, body(): row_got = lax.all_to_all(pay, 'mp', 0, 0, tiled=True)  9.66 us
    all_to_all x1, blocking collectives, body(): last = lax.all_to_all(pay, 'mp', 0, 0, tiled=True)  9.21 us
    ppermute x1, waiting for transfers between devices, body(): pair_last = lax.ppermute(pair_away, 'dp', across)  8.74 us
    ppermute x1, waiting for transfers between devices, body(): tok_last = lax.ppermute(tok_away, 'mp', x_across)  8.33 us
    pallas_call x1, Pallas kernels, gate_pre(): pl.pallas_call(gate_kernel, in_specs=[pl.BlockSpec(memory_space=pltpu.SME...  6.39 us
    ppermute x1, starting transfers between devices, body(): lax.ppermute(pair_l, 'dp', back)  4.08 us
  transfers between devices with their start and end apart: 17, of which 8 were waited for; matrix products, arithmetic and copies ran while one was open for 0% of the time, Pallas kernels for 27%

profile of v5, /device:TPU:0, one launch (start us, length us, event | category | flops | bytes accessed | tf_op | source)
XLA Modules:
  0.0 126.7 jit_solution(14084247179037604427)
XLA Ops:
  0.6 0.1 collective-permute-start.1
  0.8 0.1 stack.23.idx.refs_0_
  0.9 6.4 %gate_pre.1 = (f32[768,1024]{1,0:T(8,128)S(1)}, bf16[768,2048]{1,0:T(8,128)(2,1)S(1)}, bf16[2048,1024]{1,0:T(8,128)(2,1)S(1)}, bf16[2048,1024]{1,0:T(8,128)(2,1)S(1)}) custom-call(s32[5]{0:T(128)S(1)} %stack.23.idx.refs_0_, bf16[768,2048]{1,0:T(8,128)(2,1)} %tok_in.1, bf16[2048,1024]{1,0:T(8,128)(2,1)} %wg_in.1, bf16[2048,1024]{1,0:T(8,128)(2,1)} %wu_in.1), custom_call_target="tpu_custom_call" | custom-call | flops 1000000 | bytes 1024 | tf_op jit(solution)/shard_map/gate_pre/pallas_call | solution.py:99
  7.3 0.5 collective-permute-start
  7.8 5.3 %up_pre.1 = (f32[768,1024]{1,0:T(8,128)S(1)}, f32[768,1024]{1,0:T(8,128)S(1)}, bf16[2,256,768]{2,1,0:T(8,128)(2,1)S(1)}, bf16[2,256,768]{2,1,0:T(8,128)(2,1)S(1)}) custom-call(s32[5]{0:T(128)S(1)} %stack.23.idx.refs_0_, bf16[768,2048]{1,0:T(8,128)(2,1)S(1)} %get-tuple-element.55.refs_1_, bf16[2048,1024]{1,0:T(8,128)(2,1)S(1)} %get-tuple-element.56.refs_2_.refs_3_, ...), custom_call_target="tpu_custom_call" | custom-call | flops 201326592 | bytes 1024 | tf_op jit(solution)/shard_map/up_pre/pallas_call | solution.py:52
  13.1 3.5 %hidden_grad.1.refs_1_.refs_3_ = bf16[2,768,1024]{2,1,0:T(8,128)(2,1)S(1)} custom-call(bf16[768,2048]{1,0:T(8,128)(2,1)S(1)} %copy-done, bf16[1024,2048]{1,0:T(8,128)(2,1)S(1)} %copy-done.1, f32[768,1024]{1,0:T(8,128)S(1)} %get-tuple-element.58.refs_2_, f32[768,1024]{1,0:T(8,128)S(1)} %get-tuple-element.59.refs_3_, ...), custom_call_target="tpu_custom_call" | custom-call | flops 201326592 | bytes 1024 | tf_op jit(solution)/shard_map/hidden_grad/pallas_call | solution.py:52
  16.6 0.4 collective-permute-start.2
  17.0 0.3 collective-permute-start.3
  17.3 4.0 %token_grad.2 = (bf16[2,768,256]{2,1,0:T(8,128)(2,1)S(1)}, bf16[2,768,256]{2,1,0:T(8,128)(2,1)S(1)}) custom-call(s32[5]{0:T(128)S(1)} %stack.23.idx.refs_0_, bf16[2,768,1024]{2,1,0:T(8,128)(2,1)S(1)} %hidden_grad.1.refs_1_.refs_3_, bf16[2048,1024]{1,0:T(8,128)(2,1)S(1)} %get-tuple-element.60.refs_2_, bf16[2048,1024]{1,0:T(8,128)(2,1)S(1)} %get-tuple-element.56.refs_2_.refs_3_), custom_call_target="tpu_custom_call" | custom-call | flops 201326592 | bytes 1024 | tf_op jit(solution)/shard_map/token_grad/pallas_call | solution.py:52
  21.3 3.2 %collective-permute-start.5 = (bf16[2,768,256]{2,1,0:T(8,128)(2,1)S(1)}, bf16[2,768,256]{2,1,0:T(8,128)(2,1)S(1)}, u32[]{:S(2)}, u32[]{:S(2)}) collective-permute-start(bf16[2,768,256]{2,1,0:T(8,128)(2,1)S(1)} %get-tuple-element.68), channel_id=1, source_target_pairs={{0,6},{1,7},{2,0},{3,1},{4,2},{5,3},{6,4},{7,5},{8,14},{9,15},{10,... | collective-permute-start | bytes 2359304 | tf_op jit(solution)/shard_map/ppermute | solution.py:406
  24.4 4.1 %weight.2 = (bf16[2,128,2048]{2,1,0:T(8,128)(2,1)S(1)}, bf16[2,128,2048]{2,1,0:T(8,128)(2,1)S(1)}) custom-call(s32[5]{0:T(128)S(1)} %stack.23.idx.refs_0_, bf16[768,2048]{1,0:T(8,128)(2,1)S(1)} %get-tuple-element.55.refs_1_, bf16[768,2048]{1,0:T(8,128)(2,1)S(1)} %collective-permute-done.refs_4_.refs_2_, ...), custom_call_target="tpu_custom_call" | custom-call | flops 201326592 | bytes 1024 | tf_op jit(solution)/shard_map/weight/pallas_call | solution.py:52
  28.5 4.1 %collective-permute-start.9 = (bf16[2,128,2048]{2,1,0:T(8,128)(2,1)S(1)}, bf16[2,128,2048]{2,1,0:T(8,128)(2,1)S(1)}, u32[]{:S(2)}, u32[]{:S(2)}) collective-permute-start(bf16[2,128,2048]{2,1,0:T(8,128)(2,1)S(1)} %get-tuple-element.72), channel_id=1, source_target_pairs={{0,96},{8,104},{16,112},{24,120},{32,0},{40,8},{48,16},{56,24},{64... | collective-permute-start | bytes 3145736 | tf_op jit(solution)/shard_map/ppermute | solution.py:409
  32.6 1.8 %down.2.refs_5_ = bf16[256,2048]{1,0:T(8,128)(2,1)S(1)} custom-call(bf16[2,256,768]{2,1,0:T(8,128)(2,1)S(1)} %get-tuple-element.61.refs_0_, bf16[2,256,768]{2,1,0:T(8,128)(2,1)S(1)} %collective-permute-done.3.refs_1_, bf16[768,2048]{1,0:T(8,128)(2,1)S(1)} %copy-done, bf16[768,2048]{1,0:T(8,128)(2,1)S(1)} %collective-permute-done.1.refs_5_.refs_3_, ...), custom_call_target="tpu_custom_call" | custom-call | flops 100663296 | bytes 1024 | tf_op jit(solution)/shard_map/down/pallas_call | solution.py:52
  34.4 3.4 %collective-permute-start.11 = (bf16[256,2048]{1,0:T(8,128)(2,1)S(1)}, bf16[256,2048]{1,0:T(8,128)(2,1)S(1)}, u32[]{:S(2)}, u32[]{:S(2)}) collective-permute-start(bf16[256,2048]{1,0:T(8,128)(2,1)S(1)} %down.2.refs_5_), channel_id=1, source_target_pairs={{0,16},{8,24},{16,0},{24,8},{32,48},{40,56},{48,32},{56,40},{64,80... | collective-permute-start | bytes 3145736 | tf_op jit(solution)/shard_map/ppermute | solution.py:418
  37.8 4.0 %weight.3 = (bf16[2,128,2048]{2,1,0:T(8,128)(2,1)S(1)}, bf16[2,128,2048]{2,1,0:T(8,128)(2,1)S(1)}) custom-call(s32[5]{0:T(128)S(1)} %stack.23.idx.refs_0_, bf16[768,2048]{1,0:T(8,128)(2,1)S(1)} %get-tuple-element.55.refs_1_, bf16[768,2048]{1,0:T(8,128)(2,1)S(1)} %collective-permute-done.refs_4_.refs_2_, ...), custom_call_target="tpu_custom_call" | custom-call | flops 201326592 | bytes 1024 | tf_op jit(solution)/shard_map/weight/pallas_call | solution.py:52
  41.8 4.0 %token_grad.3 = (bf16[2,768,256]{2,1,0:T(8,128)(2,1)S(1)}, bf16[2,768,256]{2,1,0:T(8,128)(2,1)S(1)}) custom-call(s32[5]{0:T(128)S(1)} %stack.23.idx.refs_0_, bf16[2,768,1024]{2,1,0:T(8,128)(2,1)S(1)} %hidden_grad.1.refs_1_.refs_3_, bf16[2048,1024]{1,0:T(8,128)(2,1)S(1)} %get-tuple-element.60.refs_2_, ...), custom_call_target="tpu_custom_call" | custom-call | flops 201326592 | bytes 1024 | tf_op jit(solution)/shard_map/token_grad/pallas_call | solution.py:52
  45.8 1.8 %down.3.refs_4_.refs_0_ = bf16[256,2048]{1,0:T(8,128)(2,1)S(1)} custom-call(bf16[2,256,768]{2,1,0:T(8,128)(2,1)S(1)} %get-tuple-element.61.refs_0_, bf16[2,256,768]{2,1,0:T(8,128)(2,1)S(1)} %collective-permute-done.3.refs_1_, bf16[768,2048]{1,0:T(8,128)(2,1)S(1)} %copy-done, bf16[768,2048]{1,0:T(8,128)(2,1)S(1)} %collective-permute-done.1.refs_5_.refs_3_, ...), custom_call_target="tpu_custom_call" | custom-call | flops 100663296 | bytes 1024 | tf_op jit(solution)/shard_map/down/pallas_call | solution.py:52
  47.7 0.2 middle.2
  47.9 3.3 %collective-permute-start.6 = (bf16[768,256]{1,0:T(8,128)(2,1)S(1)}, bf16[768,256]{1,0:T(8,128)(2,1)S(1)}, u32[]{:S(2)}, u32[]{:S(2)}) collective-permute-start(bf16[768,256]{1,0:T(8,128)(2,1)S(1)} %get-tuple-element.69), channel_id=1, source_target_pairs={{0,6},{1,7},{2,0},{3,1},{4,2},{5,3},{6,4},{7,5},{8,14},{9,15},{10,... | collective-permute-start | bytes 1179656 | tf_op jit(solution)/shard_map/ppermute | solution.py:408
  51.2 4.0 %collective-permute-done.9.refs_3_.refs_1_ = bf16[2,128,2048]{2,1,0:T(8,128)(2,1)S(1)} collective-permute-done((bf16[2,128,2048]{2,1,0:T(8,128)(2,1)S(1)}, bf16[2,128,2048]{2,1,0:T(8,128)(2,1)S(1)}, u32[]{:S(2)}, u32[]{:S(2)}) %collective-permute-start.9) | collective-permute-done | bytes 1048608 | tf_op jit(solution)/shard_map/ppermute | solution.py:409
  55.1 3.4 %collective-permute-done.8.refs_2_.refs_1_ = bf16[2,128,2048]{2,1,0:T(8,128)(2,1)S(1)} collective-permute-done((bf16[2,128,2048]{2,1,0:T(8,128)(2,1)S(1)}, bf16[2,128,2048]{2,1,0:T(8,128)(2,1)S(1)}, u32[]{:S(2)}, u32[]{:S(2)}) %collective-permute-start.8) | collective-permute-done | bytes 1048608 | tf_op jit(solution)/shard_map/ppermute | solution.py:409
  58.6 0.2 middle.3
  58.8 0.4 collective-permute-start.13
  59.1 1.7 %collective-permute-start.12 = (bf16[128,2048]{1,0:T(8,128)(2,1)S(1)}, bf16[128,2048]{1,0:T(8,128)(2,1)S(1)}, u32[]{:S(2)}, u32[]{:S(2)}) collective-permute-start(bf16[128,2048]{1,0:T(8,128)(2,1)S(1)} %get-tuple-element.73.refs_3_), channel_id=1, source_target_pairs={{0,32},{8,40},{16,48},{24,56},{32,64},{40,72},{48,80},{56,88},{64,... | collective-permute-start | bytes 1572872 | tf_op jit(solution)/shard_map/ppermute | solution.py:411
  60.9 1.3 %collective-permute-done.7.refs_2_ = bf16[768,256]{1,0:T(8,128)(2,1)S(1)} collective-permute-done((bf16[768,256]{1,0:T(8,128)(2,1)S(1)}, bf16[768,256]{1,0:T(8,128)(2,1)S(1)}, u32[]{:S(2)}, u32[]{:S(2)}) %collective-permute-start.7) | collective-permute-done | bytes 393248 | tf_op jit(solution)/shard_map/ppermute | solution.py:408
  62.2 0.1 crossing.2
  62.4 0.7 collective-permute-start.10
  63.0 8.3 %collective-permute-done.10.refs_4_.refs_3_ = bf16[768,256]{1,0:T(8,128)(2,1)S(1)} collective-permute-done((bf16[768,256]{1,0:T(8,128)(2,1)S(1)}, bf16[768,256]{1,0:T(8,128)(2,1)S(1)}, u32[]{:S(2)}, u32[]{:S(2)}) %collective-permute-start.10) | collective-permute-done | bytes 393248 | tf_op jit(solution)/shard_map/ppermute | solution.py:413
  71.4 0.1 collective-permute-done.13.refs_3_.refs_2_
  71.5 1.5 %collective-permute-done.12.refs_2_ = bf16[128,2048]{1,0:T(8,128)(2,1)S(1)} collective-permute-done((bf16[128,2048]{1,0:T(8,128)(2,1)S(1)}, bf16[128,2048]{1,0:T(8,128)(2,1)S(1)}, u32[]{:S(2)}, u32[]{:S(2)}) %collective-permute-start.12) | collective-permute-done | bytes 524320 | tf_op jit(solution)/shard_map/ppermute | solution.py:411
  73.0 0.2 crossing.3.refs_2_
  73.2 3.1 %collective-permute-start.14 = (bf16[128,2048]{1,0:T(8,128)(2,1)S(1)}, bf16[128,2048]{1,0:T(8,128)(2,1)S(1)}, u32[]{:S(2)}, u32[]{:S(2)}) collective-permute-start(bf16[128,2048]{1,0:T(8,128)(2,1)S(1)} %crossing.3.refs_2_), channel_id=1, source_target_pairs={{0,16},{8,24},{16,0},{24,8},{32,48},{40,56},{48,32},{56,40},{64,80... | collective-permute-start | bytes 1572872 | tf_op jit(solution)/shard_map/ppermute | solution.py:415
  76.3 0.2 down_mix.1
  76.6 0.3 collective-permute-start.15
  76.8 0.9 token_end.1
  77.8 8.7 %collective-permute-done.14.refs_3_ = bf16[128,2048]{1,0:T(8,128)(2,1)S(1)} collective-permute-done((bf16[128,2048]{1,0:T(8,128)(2,1)S(1)}, bf16[128,2048]{1,0:T(8,128)(2,1)S(1)}, u32[]{:S(2)}, u32[]{:S(2)}) %collective-permute-start.14) | collective-permute-done | bytes 524320 | tf_op jit(solution)/shard_map/ppermute | solution.py:415
  86.5 0.4 row_sums.1
  86.9 0.0 copy-start.3
  86.9 0.0 copy-start.4
  87.0 1.1 collective-permute-done.15.refs_1_.refs_3_
  88.1 0.1 down_middle.1
  88.1 0.6 collective-permute-start.16
  88.8 9.7 %all_to_all.15.refs_5_ = f32[8,8,128]{2,1,0:T(8,128)S(1)} all-to-all(f32[8,8,128]{2,1,0:T(8,128)S(1)} %get-tuple-element.81), channel_id=1, replica_groups=mesh['dp'=16,'mp'=8] {'mp'}, dimensions={0} | all-to-all | bytes 65536 | tf_op jit(solution)/shard_map/all_to_all | solution.py:439
  98.5 1.1 column_sums.1
  99.6 16.0 %all_to_all.16.refs_0_ = bf16[16,80,128]{2,1,0:T(8,128)(2,1)S(1)} all-to-all(bf16[16,80,128]{2,1,0:T(8,128)(2,1)S(1)} %get-tuple-element.82), channel_id=1, replica_groups=mesh['dp'=16,'mp'=8] {'dp'}, dimensions={0} | all-to-all | bytes 655360 | tf_op jit(solution)/shard_map/all_to_all | solution.py:456
  115.6 0.6 partial_sums.1
  116.2 9.2 %all_to_all.17.refs_0_ = f32[8,40,128]{2,1,0:T(8,128)S(1)} all-to-all(f32[8,40,128]{2,1,0:T(8,128)S(1)} %get-tuple-element.83), channel_id=1, replica_groups=mesh['dp'=16,'mp'=8] {'mp'}, dimensions={0} | all-to-all | bytes 327680 | tf_op jit(solution)/shard_map/all_to_all | solution.py:465
  125.5 1.3 updates.1
  (26 shorter events, 0.1 us)
Async XLA Ops:
  0.6 12.4 %collective-permute-start.1 = (bf16[768,2048]{1,0:T(8,128)(2,1)}, bf16[768,2048]{1,0:T(8,128)(2,1)S(1)}, u32[]{:S(2)}, u32[]{:S(2)}) collective-permute-start(bf16[768,2048]{1,0:T(8,128)(2,1)} %refs_2_.3), channel_id=1, source_target_pairs={{0,8},{8,0},{16,24},{24,16},{32,40},{40,32},{48,56},{56,48},{64,72... | collective-permute-start | bytes 9437192 | tf_op jit(solution)/shard_map/ppermute | solution.py:352
  7.3 5.8 %collective-permute-start = (bf16[768,2048]{1,0:T(8,128)(2,1)S(1)}, bf16[768,2048]{1,0:T(8,128)(2,1)S(1)}, u32[]{:S(2)}, u32[]{:S(2)}) collective-permute-start(bf16[768,2048]{1,0:T(8,128)(2,1)S(1)} %get-tuple-element.55.refs_1_), channel_id=1, source_target_pairs={{0,8},{8,0},{16,24},{24,16},{32,40},{40,32},{48,56},{56,48},{64,72... | collective-permute-start | bytes 9437192 | tf_op jit(solution)/shard_map/ppermute | solution.py:355
  7.8 5.3 %copy-start = (bf16[768,2048]{1,0:T(8,128)(2,1)S(1)}, bf16[768,2048]{1,0:T(8,128)(2,1)}, u32[]{:S(2)}) copy-start(bf16[768,2048]{1,0:T(8,128)(2,1)} %refs_2_.3) | copy-start | bytes 9437188
  7.8 5.3 %copy-start.1 = (bf16[1024,2048]{1,0:T(8,128)(2,1)S(1)}, bf16[1024,2048]{1,0:T(8,128)(2,1)}, u32[]{:S(2)}) copy-start(bf16[1024,2048]{1,0:T(8,128)(2,1)} %refs_1_.1) | copy-start | bytes 12582916
  16.6 7.9 %collective-permute-start.2 = (bf16[2,768,1024]{2,1,0:T(8,128)(2,1)S(1)}, bf16[2,768,1024]{2,1,0:T(8,128)(2,1)S(1)}, u32[]{:S(2)}, u32[]{:S(2)}) collective-permute-start(bf16[2,768,1024]{2,1,0:T(8,128)(2,1)S(1)} %hidden_grad.1.refs_1_.refs_3_), channel_id=1, source_target_pairs={{0,8},{8,0},{16,24},{24,16},{32,40},{40,32},{48,56},{56,48},{64,72... | collective-permute-start | bytes 9437192 | tf_op jit(solution)/shard_map/ppermute | solution.py:366
  17.0 15.6 %collective-permute-start.3 = (bf16[2,256,768]{2,1,0:T(8,128)(2,1)S(1)}, bf16[2,256,768]{2,1,0:T(8,128)(2,1)S(1)}, u32[]{:S(2)}, u32[]{:S(2)}) collective-permute-start(bf16[2,256,768]{2,1,0:T(8,128)(2,1)S(1)} %get-tuple-element.62), channel_id=1, source_target_pairs={{0,8},{8,0},{16,24},{24,16},{32,40},{40,32},{48,56},{56,48},{64,72... | collective-permute-start | bytes 2359304 | tf_op jit(solution)/shard_map/ppermute | solution.py:360
  21.3 26.4 %collective-permute-start.5 = (bf16[2,768,256]{2,1,0:T(8,128)(2,1)S(1)}, bf16[2,768,256]{2,1,0:T(8,128)(2,1)S(1)}, u32[]{:S(2)}, u32[]{:S(2)}) collective-permute-start(bf16[2,768,256]{2,1,0:T(8,128)(2,1)S(1)} %get-tuple-element.68), channel_id=1, source_target_pairs={{0,6},{1,7},{2,0},{3,1},{4,2},{5,3},{6,4},{7,5},{8,14},{9,15},{10,... | collective-permute-start | bytes 2359304 | tf_op jit(solution)/shard_map/ppermute | solution.py:406
  24.4 23.2 %collective-permute-start.4 = (bf16[2,768,256]{2,1,0:T(8,128)(2,1)S(1)}, bf16[2,768,256]{2,1,0:T(8,128)(2,1)S(1)}, u32[]{:S(2)}, u32[]{:S(2)}) collective-permute-start(bf16[2,768,256]{2,1,0:T(8,128)(2,1)S(1)} %get-tuple-element.63.refs_5_), channel_id=1, source_target_pairs={{0,2},{1,3},{2,4},{3,5},{4,6},{5,7},{6,0},{7,1},{8,10},{9,11},{10,... | collective-permute-start | bytes 2359304 | tf_op jit(solution)/shard_map/ppermute | solution.py:406
  28.5 26.6 %collective-permute-start.9 = (bf16[2,128,2048]{2,1,0:T(8,128)(2,1)S(1)}, bf16[2,128,2048]{2,1,0:T(8,128)(2,1)S(1)}, u32[]{:S(2)}, u32[]{:S(2)}) collective-permute-start(bf16[2,128,2048]{2,1,0:T(8,128)(2,1)S(1)} %get-tuple-element.72), channel_id=1, source_target_pairs={{0,96},{8,104},{16,112},{24,120},{32,0},{40,8},{48,16},{56,24},{64... | collective-permute-start | bytes 3145736 | tf_op jit(solution)/shard_map/ppermute | solution.py:409
  32.6 26.0 %collective-permute-start.8 = (bf16[2,128,2048]{2,1,0:T(8,128)(2,1)S(1)}, bf16[2,128,2048]{2,1,0:T(8,128)(2,1)S(1)}, u32[]{:S(2)}, u32[]{:S(2)}) collective-permute-start(bf16[2,128,2048]{2,1,0:T(8,128)(2,1)S(1)} %get-tuple-element.64.refs_4_), channel_id=1, source_target_pairs={{0,32},{8,40},{16,48},{24,56},{32,64},{40,72},{48,80},{56,88},{64,... | collective-permute-start | bytes 3145736 | tf_op jit(solution)/shard_map/ppermute | solution.py:409
  34.4 41.9 %collective-permute-start.11 = (bf16[256,2048]{1,0:T(8,128)(2,1)S(1)}, bf16[256,2048]{1,0:T(8,128)(2,1)S(1)}, u32[]{:S(2)}, u32[]{:S(2)}) collective-permute-start(bf16[256,2048]{1,0:T(8,128)(2,1)S(1)} %down.2.refs_5_), channel_id=1, source_target_pairs={{0,16},{8,24},{16,0},{24,8},{32,48},{40,56},{48,32},{56,40},{64,80... | collective-permute-start | bytes 3145736 | tf_op jit(solution)/shard_map/ppermute | solution.py:418
  47.9 13.0 %collective-permute-start.6 = (bf16[768,256]{1,0:T(8,128)(2,1)S(1)}, bf16[768,256]{1,0:T(8,128)(2,1)S(1)}, u32[]{:S(2)}, u32[]{:S(2)}) collective-permute-start(bf16[768,256]{1,0:T(8,128)(2,1)S(1)} %get-tuple-element.69), channel_id=1, source_target_pairs={{0,6},{1,7},{2,0},{3,1},{4,2},{5,3},{6,4},{7,5},{8,14},{9,15},{10,... | collective-permute-start | bytes 1179656 | tf_op jit(solution)/shard_map/ppermute | solution.py:408
  51.2 11.1 %collective-permute-start.7 = (bf16[768,256]{1,0:T(8,128)(2,1)S(1)}, bf16[768,256]{1,0:T(8,128)(2,1)S(1)}, u32[]{:S(2)}, u32[]{:S(2)}) collective-permute-start(bf16[768,256]{1,0:T(8,128)(2,1)S(1)} %get-tuple-element.70.refs_4_), channel_id=1, source_target_pairs={{0,2},{1,3},{2,4},{3,5},{4,6},{5,7},{6,0},{7,1},{8,10},{9,11},{10,... | collective-permute-start | bytes 1179656 | tf_op jit(solution)/shard_map/ppermute | solution.py:408
  58.8 12.7 %collective-permute-start.13 = (bf16[128,2048]{1,0:T(8,128)(2,1)S(1)}, bf16[128,2048]{1,0:T(8,128)(2,1)S(1)}, u32[]{:S(2)}, u32[]{:S(2)}) collective-permute-start(bf16[128,2048]{1,0:T(8,128)(2,1)S(1)} %get-tuple-element.74), channel_id=1, source_target_pairs={{0,96},{8,104},{16,112},{24,120},{32,0},{40,8},{48,16},{56,24},{64... | collective-permute-start | bytes 1572872 | tf_op jit(solution)/shard_map/ppermute | solution.py:411
  59.1 13.9 %collective-permute-start.12 = (bf16[128,2048]{1,0:T(8,128)(2,1)S(1)}, bf16[128,2048]{1,0:T(8,128)(2,1)S(1)}, u32[]{:S(2)}, u32[]{:S(2)}) collective-permute-start(bf16[128,2048]{1,0:T(8,128)(2,1)S(1)} %get-tuple-element.73.refs_3_), channel_id=1, source_target_pairs={{0,32},{8,40},{16,48},{24,56},{32,64},{40,72},{48,80},{56,88},{64,... | collective-permute-start | bytes 1572872 | tf_op jit(solution)/shard_map/ppermute | solution.py:411
  62.4 9.0 %collective-permute-start.10 = (bf16[768,256]{1,0:T(8,128)(2,1)S(1)}, bf16[768,256]{1,0:T(8,128)(2,1)S(1)}, u32[]{:S(2)}, u32[]{:S(2)}) collective-permute-start(bf16[768,256]{1,0:T(8,128)(2,1)S(1)} %crossing.2), channel_id=1, source_target_pairs={{0,1},{1,0},{2,3},{3,2},{4,5},{5,4},{6,7},{7,6},{8,9},{9,8},{10,11... | collective-permute-start | bytes 1179656 | tf_op jit(solution)/shard_map/ppermute | solution.py:413
  73.2 13.3 %collective-permute-start.14 = (bf16[128,2048]{1,0:T(8,128)(2,1)S(1)}, bf16[128,2048]{1,0:T(8,128)(2,1)S(1)}, u32[]{:S(2)}, u32[]{:S(2)}) collective-permute-start(bf16[128,2048]{1,0:T(8,128)(2,1)S(1)} %crossing.3.refs_2_), channel_id=1, source_target_pairs={{0,16},{8,24},{16,0},{24,8},{32,48},{40,56},{48,32},{56,40},{64,80... | collective-permute-start | bytes 1572872 | tf_op jit(solution)/shard_map/ppermute | solution.py:415
  76.6 11.5 %collective-permute-start.15 = (bf16[128,2048]{1,0:T(8,128)(2,1)S(1)}, bf16[128,2048]{1,0:T(8,128)(2,1)S(1)}, u32[]{:S(2)}, u32[]{:S(2)}) collective-permute-start(bf16[128,2048]{1,0:T(8,128)(2,1)S(1)} %get-tuple-element.75.refs_4_), channel_id=1, source_target_pairs={{0,32},{8,40},{16,48},{24,56},{32,0},{40,8},{48,16},{56,24},{64,96... | collective-permute-start | bytes 1572872 | tf_op jit(solution)/shard_map/ppermute | solution.py:421
  77.8 20.7 %copy-start.5 = (f32[128]{0:T(128)S(1)}, f32[128]{0:T(128)}, u32[]{:S(2)}) copy-start(f32[128]{0:T(128)} %param.16) | copy-start | bytes 1540
  77.8 20.7 %copy-start.6 = (f32[128]{0:T(128)S(1)}, f32[128]{0:T(128)}, u32[]{:S(2)}) copy-start(f32[128]{0:T(128)} %param.18) | copy-start | bytes 1540
  77.8 20.7 %copy-start.7 = (f32[64]{0:T(128)S(1)}, f32[64]{0:T(128)}, u32[]{:S(2)}) copy-start(f32[64]{0:T(128)} %param.20) | copy-start | bytes 772
  86.9 28.7 %copy-start.3 = (f32[1024]{0:T(1024)S(1)}, f32[1024]{0:T(1024)}, u32[]{:S(2)}) copy-start(f32[1024]{0:T(1024)} %param.17) | copy-start | bytes 12292
  86.9 28.7 %copy-start.4 = (f32[1024]{0:T(1024)S(1)}, f32[1024]{0:T(1024)}, u32[]{:S(2)}) copy-start(f32[1024]{0:T(1024)} %param.19) | copy-start | bytes 12292
  87.0 38.5 %copy-start.2 = (f32[2048]{0:T(1024)S(1)}, f32[2048]{0:T(1024)}, u32[]{:S(2)}) copy-start(f32[2048]{0:T(1024)} %param.21) | copy-start | bytes 24580
  88.1 10.3 %collective-permute-start.16 = (bf16[64,2048]{1,0:T(8,128)(2,1)S(1)}, bf16[64,2048]{1,0:T(8,128)(2,1)S(1)}, u32[]{:S(2)}, u32[]{:S(2)}) collective-permute-start(bf16[64,2048]{1,0:T(8,128)(2,1)S(1)} %down_middle.1), channel_id=1, source_target_pairs={{0,96},{8,104},{16,112},{24,120},{32,64},{40,72},{48,80},{56,88},{... | collective-permute-start | bytes 786440 | tf_op jit(solution)/shard_map/ppermute | solution.py:438
